TPU v7x, 256 devices: a whole 4x4x8 slice. The times are simulated.
256 devices in a mesh: section: 4 (over z_lo, core), shard: 64 (over y, z_hi, x).
Axes of the slice: x: 4, y: 4, z: 8 (z_hi: 4, z_lo: 2; z = z_hi * 2 + z_lo), core: 2. Of those that a mesh axis runs over, the one named last changes fastest.
Arguments:
- hidden: bfloat16 [4, 512, 5120], P('section', 'shard'), may hold values from -6 to 6
- w_qkv: bfloat16 [3, 5120, 5120], P(None, 'shard'), may hold values from -0.078125 to 0.078125
- q_gain: float32 [5120], replicated, may hold values from 0.5 to 2
- k_gain: float32 [5120], replicated, may hold values from 0.5 to 2
- modulation: float32 [4, 3, 5120], replicated, may hold values from -3 to 3
- step_index: int32 [4], P('section'), may hold values from 0 to 3
- cache_k: bfloat16 [7, 512, 5120], P(None, 'shard'), may hold values from -900 to 900
- cache_v: bfloat16 [7, 512, 5120], P(None, 'shard'), may hold values from -6 to 6
- slot_rank: int32 [7], replicated, may hold values from 0 to 6, each once
- visible: int32 [4], P('section'), may hold values from 1 to 7, as said below
Outputs:
- handed: bfloat16 [4, 512, 5120], P('section', 'shard')
Inputs may be any that keep to these rules, and one draw needn't show every extreme that they name: slot_rank[c] counts the cached groups newer than the one in slot c. `visible`: some section has 7.
All inputs are finite; a program needn't handle non-finite values.
Results may differ from a plain program's by a relative error of at most 0.0055.
The roundings to bfloat16 on the way count: a program that leaves them out, or rounds other values in their place, can miss the bound.
Values may be sent and summed in bfloat16 or wider, within the bound.
No kernel may reach another device: no remote copies, remote signals or barrier semaphores. Data moves between devices by JAX's collectives and lax.ppermute only.
A program may use at most 128 MiB of HBM per device.

v0:
```python
import math

import jax
import jax.numpy as jnp
from jax import lax
from jax.sharding import PartitionSpec as P

HEADS = 40


epsilon = 1e-06


def spread(shard, axis, root):
    mine = lax.axis_index(axis) == root
    return lax.psum(jnp.where(mine, shard, jnp.zeros_like(shard)), axis)


def shifted(shard, axis, by):
    length = lax.axis_size(axis)
    return lax.ppermute(shard, axis, [(i, (i + by) % length) for i in range(length)])


def shards(
    hidden, w_qkv, q_gain, k_gain, modulation, step_index, cache_k, cache_v, slot_rank, visible
):
    shard_count = lax.axis_size("shard")
    section_count = lax.axis_size("section")
    shard_here = lax.axis_index("shard")
    tok_rows = hidden.shape[1]
    width = hidden.shape[2]
    columns = w_qkv.shape[1]
    group_rows = tok_rows * shard_count
    head_count = HEADS
    head_size = width // head_count
    slot_count = cache_k.shape[0]
    picked = (jnp.arange(modulation.shape[0]) == step_index[0]).astype(jnp.float32)
    mod_rows = jnp.sum(picked[:, None, None] * modulation, axis=0)
    residual = hidden[0].astype(jnp.float32)
    centered = residual - jnp.mean(residual, axis=-1, keepdims=True)
    variance = jnp.mean(centered * centered, axis=-1, keepdims=True)
    modulated = (
        centered * lax.rsqrt(variance + epsilon) * (1.0 + mod_rows[1]) + mod_rows[0]
    ).astype(jnp.bfloat16)
    projected = jnp.einsum(
        "td,kcd->ktc",
        lax.all_gather(modulated, "shard", axis=0, tiled=True),
        w_qkv,
        preferred_element_type=jnp.float32,
    )
    q_part = projected[0]
    k_part = projected[1]
    v_part = projected[2]
    square_sums = lax.psum(
        (jnp.sum(q_part * q_part, axis=1), jnp.sum(k_part * k_part, axis=1)), "shard"
    )
    q_cols = lax.dynamic_slice_in_dim(q_gain, shard_here * columns, columns)
    k_cols = lax.dynamic_slice_in_dim(k_gain, shard_here * columns, columns)
    q_half = (q_part * lax.rsqrt(square_sums[0] / width + epsilon)[:, None] * q_cols).astype(
        jnp.bfloat16
    )
    k_half = (k_part * lax.rsqrt(square_sums[1] / width + epsilon)[:, None] * k_cols).astype(
        jnp.bfloat16
    )
    v_half = v_part.astype(jnp.bfloat16)
    queries = lax.all_gather(q_half, "shard", axis=1, tiled=True)
    own_k, own_v = (
        lax.all_to_all(k_half, "shard", split_axis=0, concat_axis=1, tiled=True),
        lax.all_to_all(v_half, "shard", split_axis=0, concat_axis=1, tiled=True),
    )
    fresh_k, fresh_v = (
        spread(own_k, "section", section_count - 1),
        spread(own_v, "section", section_count - 1),
    )
    written = (slot_rank == slot_count - 1)[:, None, None]
    new_rank = (slot_rank + 1) % slot_count
    keys_all = jnp.concatenate([own_k[None], jnp.where(written, fresh_k[None], cache_k)], axis=0)
    keys_all = keys_all.reshape(-1, head_count, head_size)
    values_all = jnp.concatenate([own_v[None], jnp.where(written, fresh_v[None], cache_v)], axis=0)
    values_all = values_all.reshape(-1, head_count, head_size)
    slot_seen = jnp.concatenate([jnp.ones((1,), jnp.bool_), new_rank < visible[0]])
    key_mask = jnp.broadcast_to(slot_seen[:, None], (slot_count + 1, tok_rows)).reshape(-1)
    query_heads = queries.reshape(group_rows, head_count, head_size)
    scores = jnp.einsum(
        "qhd,khd->hqk", query_heads, keys_all, preferred_element_type=jnp.float32
    ) * (1.0 / math.sqrt(head_size))
    scores = jnp.where(key_mask[None, None, :], scores, -jnp.inf)
    block_max = jnp.max(scores, axis=2)
    weights = jnp.exp(scores - block_max[:, :, None])
    block_den = jnp.sum(weights, axis=2)
    numerator = jnp.einsum(
        "hqk,khd->qhd", weights.astype(jnp.bfloat16), values_all, preferred_element_type=jnp.float32
    )
    max_rows = block_max.T
    den_rows = block_den.T
    row_top = lax.pmax(max_rows.astype(jnp.bfloat16), "shard").astype(max_rows.dtype)
    factor = jnp.exp(max_rows - row_top)
    scaled_num = (numerator * factor[:, :, None]).reshape(group_rows, width)
    num_sum, den_sum = (
        lax.psum_scatter(scaled_num, "shard", scatter_dimension=0, tiled=True),
        lax.psum_scatter(den_rows * factor, "shard", scatter_dimension=0, tiled=True),
    )
    attended = (num_sum.reshape(tok_rows, head_count, head_size) / den_sum[:, :, None]).reshape(
        tok_rows, width
    )
    layer_out = (residual + mod_rows[2] * attended).astype(jnp.bfloat16)
    return shifted(layer_out[None], "section", 1)


def solution(mesh):
    return jax.shard_map(
        shards,
        mesh=mesh,
        in_specs=(
            P("section", "shard", None),
            P(None, "shard", None),
            P(),
            P(),
            P(),
            P("section"),
            P(None, "shard", None),
            P(None, "shard", None),
            P(),
            P("section"),
        ),
        out_specs=P("section", "shard", None),
        check_vma=False,
    )
```

profile of v0, /device:TPU:32, one launch (start us, length us, event | category | flops | bytes accessed | tf_op | source)
XLA Modules:
  0.0 1916.6 jit_solution(13366469636906248520)
XLA Ops:
  7.4 1.0 convert_reduce_fusion
  8.4 1.1 fusion.22
  9.5 1.2 multiply_reduce_fusion
  11.4 1.6 fusion.25
  13.0 0.8 dynamic_slice.6
  13.8 0.8 dynamic_slice.7
  14.6 93.8 %all-gather.3.cloned.1.call-done = bf16[512,5120]{1,0:T(8,128)(2,1)} async-done(((bf16[8,5120]{1,0:T(8,128)(2,1)}), bf16[512,5120]{1,0:T(8,128)(2,1)}) %all-gather.3.cloned.1.call-update) | async-done | bytes 5242896 | tf_op jit(solution)/shard_map/all_gather | solution.py:47
  108.3 4.0 fusion.10
  112.5 0.8 copy.33
  113.2 11.3 all-to-all-start
  124.6 194.4 %all-reduce.1 = (f32[512]{0:T(512)S(1)}, f32[512]{0:T(512)S(1)}) all-reduce(f32[512]{0:T(512)S(1)} %multiply_reduce_fusion.2, f32[512]{0:T(512)S(1)} %get-tuple-element.12), channel_id=1, replica_groups=mesh['section'=4,'shard'=64] {'shard'}, use_global_device_ids=true, to_apply=%region_5.0 | all-reduce | flops 1024 | bytes 8192 | tf_op jit(solution)/shard_map/psum | solution.py:54
  319.2 0.8 fusion.17
  320.0 4.6 all-to-all-start.1
  324.6 12.9 all-to-all-done.1
  337.6 0.8 select_n.47
  338.4 0.8 select_n.42
  339.4 0.7 multiply_convert_fusion
  341.5 31.1 %all-reduce.8.cloned.1.call-done = (bf16[8,5120]{1,0:T(8,128)(2,1)}, bf16[8,5120]{1,0:T(8,128)(2,1)}) async-done(((bf16[8,5120]{1,0:T(8,128)(2,1)}, bf16[8,5120]{1,0:T(8,128)(2,1)}), (bf16[8,5120]{1,0:T(8,128)(2,1)}, bf16[8,5120]{1,0:T(8,128)(2,1)})) %all-reduce.8.cloned.1.call-update) | async-done | bytes 163856 | tf_op jit(solution)/shard_map/psum | solution.py:16
  372.6 1.4 broadcast_select_fusion.1
  374.3 1.0 copy.48
  375.3 95.2 %all-gather.5.cloned.1.call-done = bf16[512,5120]{0,1:T(8,128)(2,1)} async-done(((bf16[512,80]{0,1:T(8,128)(2,1)}), bf16[512,5120]{0,1:T(8,128)(2,1)}) %all-gather.5.cloned.1.call-update) | async-done | bytes 5242896 | tf_op jit(solution)/shard_map/all_gather | solution.py:66
  470.4 6.1 fusion.2
  476.5 378.2 %pmax.7 = bf16[512,40]{0,1:T(8,128)(2,1)S(1)} all-reduce(bf16[512,40]{0,1:T(8,128)(2,1)S(1)} %bitcast_convert_fusion), channel_id=1, replica_groups=mesh['section'=4,'shard'=64] {'shard'}, use_global_device_ids=true, to_apply=%region_10.11 | all-reduce | flops 20480 | bytes 81920 | tf_op jit(solution)/shard_map/pmax | solution.py:96
  854.8 3.8 fusion.3
  858.5 0.7 bitcast_multiply_fusion.2
  859.3 7.9 bitcast_multiply_fusion
  867.2 11.5 copy.44
  880.5 609.0 %all-reduce.6.cloned.1.call-done = f32[512,40]{0,1:T(8,128)} async-done(((f32[512,40]{0,1:T(8,128)}), f32[512,40]{0,1:T(8,128)}) %all-reduce.6.cloned.1.call-update) | async-done | bytes 81936
  1489.5 0.8 constant_dynamic-slice_fusion
  1490.3 414.2 %reduce-scatter.3.cloned.1.call-done = f32[8,5120]{1,0:T(8,128)} async-done(((f32[512,5120]{1,0:T(8,128)}), f32[8,5120]{1,0:T(8,128)}) %reduce-scatter.3.cloned.1.call-update) | async-done | bytes 163856 | tf_op jit(solution)/shard_map/reduce_scatter | solution.py:100
  1904.5 1.0 fusion.29
  1905.6 3.9 collective-permute-done
  (50 shorter events, 4.1 us)
Async XLA Ops:
  6.5 101.8 %copy-start = (bf16[3,80,5120]{2,1,0:T(8,128)(2,1)S(1)}, bf16[3,80,5120]{2,1,0:T(8,128)(2,1)}, u32[]{:S(2)}) copy-start(bf16[3,80,5120]{2,1,0:T(8,128)(2,1)} %param.11) | copy-start | bytes 7372804
  6.5 101.8 %all-gather.3.cloned.1.call-start = ((), (), s32[]{:S(2)}) async-start(), calls=%async_computation.3 | async-start | bytes 5324800 | tf_op jit(solution)/shard_map/all_gather | solution.py:47
  14.6 326.2 %copy-start.3 = (s32[7]{0:T(128)S(1)}, s32[7]{0:T(128)}, u32[]{:S(2)}) copy-start(s32[7]{0:T(128)} %param.18) | copy-start | bytes 88
  113.2 206.7 %all-to-all-start = ((bf16[64,8,80]{2,1,0:T(8,128)(2,1)}), bf16[64,8,80]{2,1,0:T(8,128)(2,1)S(1)}, u32[]{:S(2)}, u32[]{:S(2)}) async-start(bf16[64,8,80]{2,1,0:T(8,128)(2,1)} %bitcast.7), calls=%async_computation | async-start | bytes 262144 | tf_op jit(solution)/shard_map/all_to_all | solution.py:69
  320.0 17.6 all-to-all-start.1
  324.6 48.0 %all-reduce.8.cloned.1.call-start = ((), (), s32[]{:S(2)}) async-start(), calls=%async_computation.7 | async-start | bytes 327680 | tf_op jit(solution)/shard_map/psum | solution.py:16
  339.3 131.1 %all-gather.5.cloned.1.call-start = ((), (), s32[]{:S(2)}) async-start(), calls=%async_computation.4 | async-start | bytes 5324800 | tf_op jit(solution)/shard_map/all_gather | solution.py:66
  340.1 1149.4 %all-reduce.6.cloned.1.call-start = ((), (), s32[]{:S(2)}) async-start(), calls=%async_computation.6 | async-start | bytes 163840
  859.2 1045.2 %reduce-scatter.3.cloned.1.call-start = ((), (), s32[]{:S(2)}) async-start(), calls=%async_computation.5 | async-start | bytes 10649600 | tf_op jit(solution)/shard_map/reduce_scatter | solution.py:100
  878.7 0.7 copy-start.4
  878.7 1025.8 %copy-start.1 = (bf16[1,8,5120]{2,1,0:T(8,128)(2,1)S(1)}, bf16[1,8,5120]{2,1,0:T(8,128)(2,1)}, u32[]{:S(2)}) copy-start(bf16[1,8,5120]{2,1,0:T(8,128)(2,1)} %param.10) | copy-start | bytes 245764
  878.7 1025.8 %copy-start.2 = (f32[1,5120]{1,0:T(1,128)S(1)}, f32[1,5120]{1,0:T(1,128)}, u32[]{:S(2)}) copy-start(f32[1,5120]{1,0:T(1,128)} %get-tuple-element.13) | copy-start | bytes 61444
  1905.5 3.9 collective-permute-start
Sparse Core Ops, SparseCore 0:
  13.1 95.1 all-gather.2
  339.4 33.1 all-reduce.7
  376.5 93.9 all-gather.4
  859.4 630.0 all-reduce.5
  1491.9 412.5 reduce-scatter.2
where the time goes:
time: 1920 us
  waiting for transfers between devices  1260 us (66%)
  blocking collectives  573 us (30%)
  local copies, waits for them, and re-layouts  20 us (1%)
    unnamed x6, waiting for transfers between devices  609 us
    reduce_scatter x1, waiting for transfers between devices, shards(): lax.psum_scatter(scaled_num, 'shard', scatter_dimension=0, tiled=True)  414 us
    pmax x1, blocking collectives, shards(): lax.pmax(max_rows.astype(jnp.bfloat16), 'shard').astype(max_rows.dtype)  378 us
    psum x1, blocking collectives, shards(): lax.psum((jnp.sum(q_part * q_part, axis=1), jnp.sum(k_part * k_part, axis...  194 us
    all_gather x1, waiting for transfers between devices, shards(): queries = lax.all_gather(q_half, 'shard', axis=1, tiled=True)  95.2 us
    all_gather x1, waiting for transfers between devices, shards(): lax.all_gather(modulated, 'shard', axis=0, tiled=True)  93.8 us
  transfers between devices with their start and end apart: 8, of which 7 were waited for; matrix products, arithmetic and copies ran while one was open for 1% of the time, Pallas kernels for 0%

commit v1 on v0

v1 whole, which is shorter than its diff:
```python
import math

import jax
import jax.numpy as jnp
from jax import lax
from jax.experimental import pallas as pl
from jax.experimental.pallas import tpu as pltpu
from jax.sharding import Mesh
from jax.sharding import PartitionSpec as P

AXES = ("zl", "core", "y", "zh1", "zh0", "x")
SIZES = (2, 2, 4, 2, 2, 4)
SECTION = ("zl", "core")
SHARD = ("y", "zh1", "zh0", "x")
GROUPS = ("y", "zh1")
MEMBERS = ("zh0", "x")

F32 = jnp.float32
BF16 = jnp.bfloat16
EPS = 1e-6
WIDTH = 5120
HEAD = 128
TOK = 8
SLOTS = 7
COLS = 80
PART = 640
PART_HEADS = 5
HALF_TOK = 256
CACHED = 896
TILE = 1280
VMEM_BYTES = 48 * 1024 * 1024


def params(**more):
    return pltpu.CompilerParams(vmem_limit_bytes=VMEM_BYTES, **more)


def swapped(value, axis):
    return lax.ppermute(value, axis, [(0, 1), (1, 0)])


def around(value, axis, by):
    length = lax.axis_size(axis)
    return lax.ppermute(value, axis, [(i, (i + by) % length) for i in range(length)])


def in_order(index, mine, other, axis=0):
    first = index == 0
    return jnp.concatenate(
        [jnp.where(first, mine, other), jnp.where(first, other, mine)], axis=axis
    )


def modulate_kernel(step_ref, hidden_ref, mod_ref, out_ref):
    tokens = hidden_ref[...].astype(F32)
    centered = tokens - jnp.mean(tokens, axis=-1, keepdims=True)
    variance = jnp.mean(centered * centered, axis=-1, keepdims=True)
    shift = mod_ref[0, 0:1, :]
    scale = mod_ref[0, 1:2, :]
    out_ref[...] = (centered * lax.rsqrt(variance + EPS) * (1.0 + scale) + shift).astype(BF16)


def modulate(hidden, modulation, step_index):
    return pl.pallas_call(
        modulate_kernel,
        grid_spec=pltpu.PrefetchScalarGridSpec(
            num_scalar_prefetch=1,
            grid=(1,),
            in_specs=[
                pl.BlockSpec((TOK, WIDTH), lambda i, step: (0, 0)),
                pl.BlockSpec((1, 3, WIDTH), lambda i, step: (step[0], 0, 0)),
            ],
            out_specs=pl.BlockSpec((TOK, WIDTH), lambda i, step: (0, 0)),
        ),
        out_shape=jax.ShapeDtypeStruct((TOK, WIDTH), BF16),
        compiler_params=params(),
        name="modulate",
    )(step_index, hidden, modulation)


def project_kernel(place_ref, x_ref, own_ref, near_ref, far_ref, q_ref, kv_ref, sums_ref, acc):
    step = pl.program_id(0)
    half = place_ref[1]
    mine = pl.multiple_of(half * COLS, 16)
    theirs = pl.multiple_of((1 - half) * COLS, 16)
    x = x_ref[...]

    @pl.when(step == 0)
    def _():
        acc[...] = jnp.zeros_like(acc)

    def add(rows, at):
        for i in range(3):
            acc[i, pl.ds(at, COLS), :] += lax.dot_general(
                rows[i], x, (((1,), (1,)), ((), ())), preferred_element_type=F32
            )

    add(own_ref, mine)

    @pl.when(step < 2)
    def _():
        add(near_ref, theirs)

    @pl.when(step >= 2)
    def _():
        add(far_ref, theirs)

    @pl.when(step == 3)
    def _():
        q, k, v = acc[0], acc[1], acc[2]
        q_ref[...] = q
        lane = lax.broadcasted_iota(jnp.int32, (2 * COLS, 128), 1)
        row = lax.broadcasted_iota(jnp.int32, (64, 128), 0) % 4
        q_sum = jnp.sum(q * q, axis=0, keepdims=True)
        k_sum = jnp.sum(k * k, axis=0, keepdims=True)
        sums_ref[:, 0:HALF_TOK] = jnp.broadcast_to(q_sum, (64, HALF_TOK))
        packed = jnp.zeros((64, 128), F32)
        for t in range(2):
            kt = k[:, 128 * t : 128 * t + 128]
            vt = v[:, 128 * t : 128 * t + 128]
            kv_ref[2 * t] = jnp.where(lane < 64, kt, pltpu.roll(vt, 64, 1))
            kv_ref[2 * t + 1] = jnp.where(lane < 64, pltpu.roll(kt, 64, 1), vt)
            st = jnp.broadcast_to(k_sum[:, 128 * t : 128 * t + 128], (64, 128))
            packed = jnp.where(row == 2 * t, st, packed)
            packed = jnp.where(row == 2 * t + 1, pltpu.roll(st, 64, 1), packed)
        sums_ref[:, HALF_TOK : HALF_TOK + 128] = packed


def project(place, x, own, near, far):
    def tile(j, place):
        return 2 * ((j // 2 + place[0]) % 2) + j % 2

    return pl.pallas_call(
        project_kernel,
        grid_spec=pltpu.PrefetchScalarGridSpec(
            num_scalar_prefetch=1,
            grid=(4,),
            in_specs=[
                pl.BlockSpec((HALF_TOK, TILE), lambda j, p: (0, tile(j, p))),
                pl.BlockSpec((3, COLS, TILE), lambda j, p: (0, 0, tile(j, p))),
                pl.BlockSpec((3, COLS, TILE), lambda j, p: (0, 0, jnp.minimum(j, 1))),
                pl.BlockSpec((3, COLS, TILE), lambda j, p: (0, 0, jnp.maximum(j - 2, 0))),
            ],
            out_specs=[
                pl.BlockSpec((2 * COLS, HALF_TOK), lambda j, p: (0, 0)),
                pl.BlockSpec((4, 2 * COLS, 128), lambda j, p: (0, 0, 0)),
                pl.BlockSpec((64, HALF_TOK + 128), lambda j, p: (0, 0)),
            ],
            scratch_shapes=[pltpu.VMEM((3, 2 * COLS, HALF_TOK), F32)],
        ),
        out_shape=[
            jax.ShapeDtypeStruct((2 * COLS, HALF_TOK), F32),
            jax.ShapeDtypeStruct((4, 2 * COLS, 128), F32),
            jax.ShapeDtypeStruct((64, HALF_TOK + 128), F32),
        ],
        compiler_params=params(),
        name="project",
    )(place, x, own, near, far)


def half_sums(sums_ref):
    total = sums_ref[0:8, :]
    for i in range(1, 8):
        total = total + sums_ref[8 * i : 8 * i + 8, :]
    return [jnp.sum(total[4 * h : 4 * h + 4, :], axis=0, keepdims=True) for h in range(2)]


def own_kernel(kv_ref, sums_ref, gain_ref, out_ref):
    lane = lax.broadcasted_iota(jnp.int32, (PART, 128), 1)
    gain = gain_ref[...]
    for h, total in enumerate(half_sums(sums_ref)):
        rate = lax.rsqrt(total[:, HALF_TOK : HALF_TOK + 128] / WIDTH + EPS)
        pieces = [kv_ref[4 * h + c, COLS * e : COLS * e + COLS, :] for e in range(2) for c in range(4)]
        joined = jnp.concatenate(pieces, axis=0)
        joined = jnp.where(lane < 64, joined * rate * gain, joined)
        for n in range(PART_HEADS):
            turned = joined[HEAD * n : HEAD * n + HEAD, :].T.astype(BF16)
            out_ref[0, 64 * h : 64 * h + 64, HEAD * n : HEAD * n + HEAD] = turned[0:64]
            out_ref[1, 64 * h : 64 * h + 64, HEAD * n : HEAD * n + HEAD] = turned[64:128]


def own_rows(kv, sums, gain):
    return pl.pallas_call(
        own_kernel,
        out_shape=jax.ShapeDtypeStruct((2, 128, PART), BF16),
        compiler_params=params(),
        name="own_rows",
    )(kv, sums, gain)


def attend_kernel(
    place_ref, q0, q1, q2, q3, sums_ref, gain_ref, cached_k, cached_v, own, fresh, bias_ref,
    out_ref, query, stats,
):
    head = pl.program_id(0)

    @pl.when(head == 0)
    def _():
        low, high = half_sums(sums_ref)
        total = jnp.where(place_ref[1] == 0, low, high)[:, 0:HALF_TOK]
        rate = lax.rsqrt(total / WIDTH + EPS)
        for by, piece in enumerate((q0, q1, q2, q3)):
            source = lax.rem(place_ref[2] + 4 - by, 4)
            for e in range(2):
                at = pl.multiple_of(source * COLS + e * (PART // 2), 16)
                rows = piece[COLS * e : COLS * e + COLS, :] * rate * gain_ref[pl.ds(at, COLS), :]
                query[pl.ds(at, COLS), :] = rows.astype(BF16)
        stats[...] = jnp.zeros_like(stats)

    q = query[pl.ds(pl.multiple_of(head * HEAD, HEAD), HEAD), :]
    factor = 1.0 / math.sqrt(HEAD)
    keys = (cached_k[0], own[0], fresh[0])
    values = (cached_v[0], own[1], fresh[1])
    scores = [jnp.dot(k, q, preferred_element_type=F32) * factor for k in keys]
    scores[0] = scores[0] + bias_ref[...]
    top = jnp.max(scores[0], axis=0, keepdims=True)
    for s in scores[1:]:
        top = jnp.maximum(top, jnp.max(s, axis=0, keepdims=True))
    den = jnp.zeros((1, HALF_TOK), F32)
    num = jnp.zeros((HEAD, HALF_TOK), F32)
    for s, v in zip(scores, values):
        w = jnp.exp(s - top)
        den = den + jnp.sum(w, axis=0, keepdims=True)
        num = num + lax.dot_general(
            v, w.astype(BF16), (((0,), (0,)), ((), ())), preferred_element_type=F32
        )
    rows = (num / den).T.astype(BF16)
    at = pl.multiple_of(head * HEAD, HEAD)
    for y in range(4):
        for x in range(4):
            out_ref[x, 16 * y : 16 * y + 16, pl.ds(at, HEAD)] = rows[16 * (4 * y + x) : 16 * (4 * y + x) + 16]
    stats[pl.ds(head, 1), :] = top
    stats[pl.ds(head + 8, 1), :] = den

    @pl.when(head == PART_HEADS - 1)
    def _():
        full = stats[0:16, :]
        hi = full.astype(BF16).astype(F32)
        mid = (full - hi).astype(BF16).astype(F32)
        low = full - hi - mid
        stats[0:16, :] = hi
        stats[16:32, :] = mid
        stats[32:48, :] = low
        turned = stats[...].T.astype(BF16)
        for y in range(4):
            for x in range(4):
                out_ref[x, 16 * y : 16 * y + 16, PART : PART + 128] = turned[
                    16 * (4 * y + x) : 16 * (4 * y + x) + 16
                ]


def attend(place, queries, sums, gain, cached, own, fresh, bias):
    whole = lambda *shape: pl.BlockSpec(shape, lambda h, p: (0,) * len(shape))
    return pl.pallas_call(
        attend_kernel,
        grid_spec=pltpu.PrefetchScalarGridSpec(
            num_scalar_prefetch=1,
            grid=(PART_HEADS,),
            in_specs=[whole(2 * COLS, HALF_TOK)] * 4
            + [
                whole(64, HALF_TOK + 128),
                whole(PART, 1),
                pl.BlockSpec((1, CACHED, HEAD), lambda h, p: (0, 0, h)),
                pl.BlockSpec((1, CACHED, HEAD), lambda h, p: (1, 0, h)),
                pl.BlockSpec((2, 128, HEAD), lambda h, p: (0, 0, h)),
                pl.BlockSpec((2, 128, HEAD), lambda h, p: (0, 0, h)),
                whole(CACHED, 1),
            ],
            out_specs=whole(4, 64, PART + 128),
            scratch_shapes=[
                pltpu.VMEM((PART, HALF_TOK), BF16),
                pltpu.VMEM((128, HALF_TOK), F32),
            ],
        ),
        out_shape=jax.ShapeDtypeStruct((4, 64, PART + 128), BF16),
        compiler_params=params(),
        name="attend",
    )(place, *queries, sums, gain, cached, cached, own, fresh, bias)


def join_kernel(in_ref, out_ref):
    tops, dens = [], []
    for j in range(4):
        parts = in_ref[j, :, PART : PART + 128].astype(F32)
        full = parts[:, 0:16] + parts[:, 16:32] + parts[:, 32:48]
        tops.append(full[:, 0:8])
        dens.append(full[:, 8:16])
    top = jnp.maximum(jnp.maximum(tops[0], tops[1]), jnp.maximum(tops[2], tops[3]))
    shares = [jnp.exp(t - top) * d for t, d in zip(tops, dens)]
    total = shares[0] + shares[1] + shares[2] + shares[3]
    for n in range(PART_HEADS):
        cols = slice(HEAD * n, HEAD * n + HEAD)
        joined = jnp.zeros((64, HEAD), F32)
        for j in range(4):
            joined = joined + in_ref[j, :, cols].astype(F32) * shares[j][:, n : n + 1]
        joined = joined / total[:, n : n + 1]
        for g in range(8):
            out_ref[g, :, cols] = joined[TOK * g : TOK * g + TOK]


def join(shares):
    return pl.pallas_call(
        join_kernel,
        out_shape=jax.ShapeDtypeStruct((8, TOK, PART), F32),
        compiler_params=params(),
        name="join",
    )(shares)


def finish_kernel(step_ref, att_ref, hidden_ref, mod_ref, out_ref):
    for g in range(8):
        cols = slice(PART * g, PART * g + PART)
        out_ref[:, cols] = (
            hidden_ref[:, cols].astype(F32) + mod_ref[0, 2:3, cols] * att_ref[g]
        ).astype(BF16)


def finish(attended, hidden, modulation, step_index):
    return pl.pallas_call(
        finish_kernel,
        grid_spec=pltpu.PrefetchScalarGridSpec(
            num_scalar_prefetch=1,
            grid=(1,),
            in_specs=[
                pl.BlockSpec((8, TOK, PART), lambda i, step: (0, 0, 0)),
                pl.BlockSpec((TOK, WIDTH), lambda i, step: (0, 0)),
                pl.BlockSpec((1, 3, WIDTH), lambda i, step: (step[0], 0, 0)),
            ],
            out_specs=pl.BlockSpec((TOK, WIDTH), lambda i, step: (0, 0)),
        ),
        out_shape=jax.ShapeDtypeStruct((TOK, WIDTH), BF16),
        compiler_params=params(),
        name="finish",
    )(step_index, attended, hidden, modulation)


def shards(
    hidden, w_qkv, q_gain, k_gain, modulation, step_index, cache_k, cache_v, slot_rank, visible
):
    zl, core = lax.axis_index("zl"), lax.axis_index("core")
    half, x_here = lax.axis_index("zh0"), lax.axis_index("x")
    section = lax.axis_index(SECTION)
    group = lax.axis_index(GROUPS)
    place = jnp.stack([core, half, x_here]).astype(jnp.int32)

    near = swapped(lax.dynamic_slice_in_dim(w_qkv, core * (WIDTH // 2), WIDTH // 2, 2), "zh0")
    far = swapped(near, "core")

    modulated = modulate(hidden[0], modulation, step_index)
    pair = in_order(lax.axis_index("zh1"), modulated, swapped(modulated, "zh1"))
    tokens = lax.all_to_all(
        jnp.broadcast_to(pair[None], (16,) + pair.shape), ("y", "x"), 0, 0, tiled=True
    ).reshape(HALF_TOK, WIDTH)

    caches = jnp.stack([cache_k, cache_v])
    quarter = lax.dynamic_slice_in_dim(caches, section * 2, 2, 2)
    quarter = quarter.reshape(2, SLOTS * 2, 8, PART).transpose(2, 0, 1, 3)
    quarter = lax.all_to_all(quarter, GROUPS, 0, 0, tiled=True)
    cached = quarter.transpose(1, 0, 2, 3).reshape(2, 8 * SLOTS * 2, PART)
    for axis in ("zh0", "zl", "core"):
        cached = jnp.concatenate([cached, swapped(cached, axis)], axis=1)
    new_rank = (slot_rank + 1) % SLOTS
    seen = (slot_rank != SLOTS - 1) & (new_rank < visible[0])
    bias = jnp.where(seen, 0.0, -jnp.inf).astype(F32)
    bias = jnp.tile(jnp.repeat(bias, 2), CACHED // (2 * SLOTS))[:, None]

    q_cols = lax.dynamic_slice_in_dim(q_gain, group * PART, PART)[:, None]
    k_cols = lax.dynamic_slice_in_dim(k_gain, group * PART, PART)[:, None]

    q_part, kv_part, sums = project(place, tokens, w_qkv, near, far)
    sums = lax.all_to_all(sums, SHARD, 0, 0, tiled=True)
    kv_sent = jnp.broadcast_to(kv_part[None], (2,) + kv_part.shape).reshape(8, 2 * COLS, 128)
    kv_all = lax.all_to_all(kv_sent, MEMBERS, 0, 0, tiled=True)
    queries = [q_part] + [around(q_part, "x", by) for by in (1, 2, 3)]
    own = own_rows(kv_all, sums, k_cols)
    across = lax.ppermute(own, SECTION, [(3, 1)])
    fresh = jnp.where((zl == 0) & (core == 1), across, own)
    beside = lax.ppermute(fresh, SECTION, [(3, 2), (1, 0)])
    fresh = jnp.where(core == 0, beside, fresh)
    shares = attend(place, queries, sums, q_cols, cached, own, fresh, bias)
    shares = lax.all_to_all(shares, "x", 0, 0, tiled=True)
    attended = lax.all_to_all(join(shares), GROUPS, 0, 0, tiled=True)
    layer_out = finish(attended, hidden[0], modulation, step_index)
    return around(layer_out[None], SECTION, 1)


def solution(mesh):
    fine = Mesh(mesh.devices.reshape(SIZES), AXES)
    return jax.shard_map(
        shards,
        mesh=fine,
        in_specs=(
            P(SECTION, SHARD, None),
            P(None, SHARD, None),
            P(),
            P(),
            P(),
            P(SECTION),
            P(None, SHARD, None),
            P(None, SHARD, None),
            P(),
            P(SECTION),
        ),
        out_specs=P(SECTION, SHARD, None),
        check_vma=False,
    )
```

time: 1920 us -> 204 us (0.11)
  waiting for transfers between devices: 1260 us -> 69.8 us
  blocking collectives: 573 us -> 62.8 us
  starting transfers between devices: 16.2 us -> 36.8 us
    unnamed x6 -> x0, waiting for transfers between devices: 609 us -> none
    reduce_scatter x1 -> x0, waiting for transfers between devices: 414 us -> none  [shards(): lax.psum_scatter(scaled_num, 'shard', scatter_dimension=0, tiled=True)]
    pmax x1 -> x0, blocking collectives: 378 us -> none  [shards(): lax.pmax(max_rows.astype(jnp.bfloat16), 'shard').astype(max_rows.dtype)]
    psum x1 -> x0, blocking collectives: 194 us -> none  [shards(): lax.psum((jnp.sum(q_part * q_part, axis=1), jnp.sum(k_part * k_part, axis...]
    all_gather x2 -> x0, waiting for transfers between devices: 189 us -> none  [the longest x1 95.2 us: shards(): queries = lax.all_gather(q_half, 'shard', axis=1, tiled=True)]
    all_to_all x0 -> x3, blocking collectives: none -> 62.8 us  [the longest x1 36.7 us: shards(): sums = lax.all_to_all(sums, SHARD, 0, 0, tiled=True)]
    ppermute x1 -> x12, waiting for transfers between devices: 3.85 us -> 58.5 us  [the longest x6 52.6 us: swapped(): return lax.ppermute(value, axis, [(0, 1), (1, 0)])]
    psum x1 -> x0, waiting for transfers between devices: 31.1 us -> none  [spread(): return lax.psum(jnp.where(mine, shard, jnp.zeros_like(shard)), axis)]
  transfers between devices with their start and end apart: 8 -> 15, of which waited for: 7 -> 6; matrix products, arithmetic and copies ran while one was open for 1% -> 6% of each run, Pallas kernels for 0% -> 4%
where the time goes in v1:
time: 204 us; the launch traced here: 202 us
  waiting for transfers between devices  69.8 us (34%)
  blocking collectives  62.8 us (31%)
  starting transfers between devices  36.8 us (18%)
  Pallas kernels  16 us (8%)
  local copies, waits for them, and re-layouts  11.2 us (5%)
  other arithmetic  4.13 us (2%)
    ppermute x6, waiting for transfers between devices, swapped(): return lax.ppermute(value, axis, [(0, 1), (1, 0)])  52.6 us
    all_to_all x1, blocking collectives, shards(): sums = lax.all_to_all(sums, SHARD, 0, 0, tiled=True)  36.7 us
    all_to_all x1, blocking collectives, shards(): attended = lax.all_to_all(join(shares), GROUPS, 0, 0, tiled=True)  14.9 us
    ppermute x6, starting transfers between devices, swapped(): return lax.ppermute(value, axis, [(0, 1), (1, 0)])  13 us
    all_to_all x1, waiting for transfers between devices, shards(): quarter = lax.all_to_all(quarter, GROUPS, 0, 0, tiled=True)  11.3 us
    all_to_all x1, blocking collectives, shards(): shares = lax.all_to_all(shares, 'x', 0, 0, tiled=True)  11.1 us
    pallas_call x1, Pallas kernels, project(): pl.pallas_call(project_kernel, grid_spec=pltpu.PrefetchScalarGridSpec(num...  8.73 us
    ppermute x4, starting transfers between devices, around(): lax.ppermute(value, axis, [(i, (i + by) % length) for i in range(length)])  7.85 us
  transfers between devices with their start and end apart: 15, of which 6 were waited for; matrix products, arithmetic and copies ran while one was open for 6% of the time, Pallas kernels for 4%

profile of v1, /device:TPU:32, one launch (start us, length us, event | category | flops | bytes accessed | tf_op | source)
XLA Modules:
  0.0 202.3 jit_solution(14144608063012145333)
XLA Ops:
  0.7 1.1 copy.35.mod_ref
  1.8 0.9 copy-done.1
  3.0 6.4 %collective-permute-start = (bf16[8,5120]{1,0:T(8,128)(2,1)S(1)}, bf16[8,5120]{1,0:T(8,128)(2,1)S(1)}, u32[]{:S(2)}, u32[]{:S(2)}) collective-permute-start(bf16[8,5120]{1,0:T(8,128)(2,1)S(1)} %modulate.1), channel_id=1, source_target_pairs={{0,8},{8,0},{1,9},{9,1},{2,10},{10,2},{3,11},{11,3},{4,12},{12,4},... | collective-permute-start | bytes 245768 | tf_op jit(solution)/shard_map/ppermute | solution.py:39
  9.4 2.4 %constant_dynamic-slice_fusion = bf16[3,80,2560]{2,1,0:T(8,128)(2,1)} fusion(bf16[3,80,5120]{2,1,0:T(8,128)(2,1)} %own_ref.1, s32[]{:T(128)S(6)} %select_n.50), kind=kLoop, calls=%fused_computation.14 | loop fusion | bytes 2457604 | tf_op jit(solution)/shard_map/dynamic_slice | solution.py:346
  11.8 1.5 collective-permute-start.1
  13.7 0.9 copy.37
  14.7 5.3 %all-to-all-start.2 = ((bf16[8,2,14,640]{3,1,2,0:T(2,128)(2,1)}), bf16[8,2,14,640]{3,1,2,0:T(2,128)(2,1)S(1)}, u32[]{:S(2)}, u32[]{:S(2)}) async-start(bf16[8,2,14,640]{3,1,2,0:T(2,128)(2,1)} %copy.37), calls=%async_computation.2 | async-start | bytes 573440 | tf_op jit(solution)/shard_map/all_to_all | solution.py:358
  20.1 11.3 %all-to-all-done.2 = bf16[8,2,14,640]{3,1,2,0:T(2,128)(2,1)S(1)} async-done(((bf16[8,2,14,640]{3,1,2,0:T(2,128)(2,1)}), bf16[8,2,14,640]{3,1,2,0:T(2,128)(2,1)S(1)}, u32[]{:S(2)}, u32[]{:S(2)}) %all-to-all-start.2) | async-done | bytes 286752 | tf_op jit(solution)/shard_map/all_to_all | solution.py:358
  31.4 1.9 broadcast_in_dim.32
  33.3 5.1 %all-to-all-start = ((bf16[16,16,5120]{2,1,0:T(8,128)(2,1)}), bf16[16,16,5120]{2,1,0:T(8,128)(2,1)}, u32[]{:S(2)}, u32[]{:S(2)}) async-start(bf16[16,16,5120]{2,1,0:T(8,128)(2,1)} %broadcast_in_dim.32), calls=%async_computation | async-start | bytes 5242880 | tf_op jit(solution)/shard_map/all_to_all | solution.py:351
  38.4 33.7 %collective-permute-done.1.near_ref = bf16[3,80,2560]{2,1,0:T(8,128)(2,1)} collective-permute-done((bf16[3,80,2560]{2,1,0:T(8,128)(2,1)}, bf16[3,80,2560]{2,1,0:T(8,128)(2,1)}, u32[]{:S(2)}, u32[]{:S(2)}) %collective-permute-start.1) | collective-permute-done | bytes 1228832 | tf_op jit(solution)/shard_map/ppermute | solution.py:39
  72.1 3.5 %collective-permute-start.6 = (bf16[2,112,640]{2,1,0:T(8,128)(2,1)S(1)}, bf16[2,112,640]{2,1,0:T(8,128)(2,1)S(1)}, u32[]{:S(2)}, u32[]{:S(2)}) collective-permute-start(bf16[2,112,640]{2,1,0:T(8,128)(2,1)S(1)} %copy.41), channel_id=1, source_target_pairs={{0,4},{4,0},{1,5},{5,1},{2,6},{6,2},{3,7},{7,3},{8,12},{12,8},{9,1... | collective-permute-start | bytes 860168 | tf_op jit(solution)/shard_map/ppermute | solution.py:39
  75.6 8.7 %project.1 = (f32[160,256]{1,0:T(8,128)S(1)}, f32[4,160,128]{2,1,0:T(8,128)S(1)}, f32[64,384]{1,0:T(8,128)S(1)}) custom-call(s32[3]{0:T(128)S(1)} %pad_add_fusion.place_ref, bf16[256,5120]{1,0:T(8,128)(2,1)} %bitcast.4.x_ref, bf16[3,80,5120]{2,1,0:T(8,128)(2,1)S(1)} %copy-done, bf16[3,80,2560]{2,1,0:T(8,128)(2,1)} %collective-permute-done.1.near_ref, ...), custom_call_target="tpu_custom_call" | custom-call | tf_op jit(solution)/shard_map/project/pallas_call | solution.py:133
  84.5 36.7 %all_to_all.36 = f32[64,1,384]{2,1,0:T(1,128)S(1)} all-to-all(f32[64,1,384]{2,1,0:T(1,128)S(1)} %copy.36), channel_id=1, replica_groups=mesh['zl'=2,'core'=2,'y'=4,'zh1'=2,'zh0'=2,'x'=4] {'y','zh1','zh0','x'}, dimensions={0} | all-to-all | bytes 196608 | tf_op jit(solution)/shard_map/all_to_all | solution.py:371
  121.2 0.9 broadcast_in_dim.34
  122.1 3.5 %all-to-all-start.3 = ((f32[8,160,128]{2,1,0:T(8,128)}), f32[8,160,128]{2,1,0:T(8,128)S(1)}, u32[]{:S(2)}, u32[]{:S(2)}) async-start(f32[8,160,128]{2,1,0:T(8,128)} %bitcast.11), calls=%async_computation.3 | async-start | bytes 1310720 | tf_op jit(solution)/shard_map/all_to_all | solution.py:373
  125.7 1.6 collective-permute-start.7
  127.3 18.9 %collective-permute-done.7 = bf16[2,224,640]{2,1,0:T(8,128)(2,1)S(1)} collective-permute-done((bf16[2,224,640]{2,1,0:T(8,128)(2,1)S(1)}, bf16[2,224,640]{2,1,0:T(8,128)(2,1)S(1)}, u32[]{:S(2)}, u32[]{:S(2)}) %collective-permute-start.7) | collective-permute-done | bytes 573472 | tf_op jit(solution)/shard_map/ppermute | solution.py:39
  146.2 1.1 pad_maximum_fusion.1
  149.3 0.8 dynamic_slice.13
  151.0 1.3 collective-permute-start.10
  152.7 1.5 pad_maximum_fusion.cached_k.cached_v
  154.1 1.8 collective-permute-start.3
  155.9 2.7 %collective-permute-start.4 = (f32[160,256]{1,0:T(8,128)S(1)}, f32[160,256]{1,0:T(8,128)S(1)}, u32[]{:S(2)}, u32[]{:S(2)}) collective-permute-start(f32[160,256]{1,0:T(8,128)S(1)} %get-tuple-element.8.q0), channel_id=1, source_target_pairs={{0,2},{1,3},{2,0},{3,1},{4,6},{5,7},{6,4},{7,5},{8,10},{9,11},{10,... | collective-permute-start | bytes 491528 | tf_op jit(solution)/shard_map/ppermute | solution.py:44
  158.6 1.5 collective-permute-start.5
  160.0 1.0 broadcast_select_fusion.1.fresh
  161.1 2.5 %collective-permute-done.4.q2 = f32[160,256]{1,0:T(8,128)S(1)} collective-permute-done((f32[160,256]{1,0:T(8,128)S(1)}, f32[160,256]{1,0:T(8,128)S(1)}, u32[]{:S(2)}, u32[]{:S(2)}) %collective-permute-start.4) | collective-permute-done | bytes 163872 | tf_op jit(solution)/shard_map/ppermute | solution.py:44
  163.9 6.2 %attend.1 = bf16[4,64,768]{2,1,0:T(8,128)(2,1)S(1)} custom-call(s32[3]{0:T(128)S(1)} %pad_add_fusion.place_ref, f32[160,256]{1,0:T(8,128)S(1)} %get-tuple-element.8.q0, f32[160,256]{1,0:T(8,128)S(1)} %collective-permute-done.3.q1, f32[160,256]{1,0:T(8,128)S(1)} %collective-permute-done.4.q2, f32[160,256]{1,0:T(8,128)S(1)} %collective-permute-done.5.q3, ...), custom_call_target="tpu_custom_call" | custom-call | tf_op jit(solution)/shard_map/attend/pallas_call | solution.py:254
  170.1 11.1 %all_to_all.37.in_ref = bf16[4,64,768]{2,1,0:T(8,128)(2,1)S(1)} all-to-all(bf16[4,64,768]{2,1,0:T(8,128)(2,1)S(1)} %attend.1), channel_id=1, replica_groups=mesh['zl'=2,'core'=2,'y'=4,'zh1'=2,'zh0'=2,'x'=4] {'x'}, dimensions={0} | all-to-all | bytes 786432 | tf_op jit(solution)/shard_map/all_to_all | solution.py:381
  181.7 14.9 %all_to_all.38.att_ref = f32[8,8,640]{2,1,0:T(8,128)S(1)} all-to-all(f32[8,8,640]{2,1,0:T(8,128)S(1)} %join.1), channel_id=1, replica_groups=mesh['zl'=2,'core'=2,'y'=4,'zh1'=2,'zh0'=2,'x'=4] {'y','zh1'}, dimensions={0} | all-to-all | bytes 327680 | tf_op jit(solution)/shard_map/all_to_all | solution.py:382
  196.7 1.9 collective-permute-start.11
  198.6 3.1 %collective-permute-done.11 = bf16[1,8,5120]{2,1,0:T(8,128)(2,1)S(1)} collective-permute-done((bf16[1,8,5120]{2,1,0:T(8,128)(2,1)S(1)}, bf16[1,8,5120]{2,1,0:T(8,128)(2,1)S(1)}, u32[]{:S(2)}, u32[]{:S(2)}) %collective-permute-start.11) | collective-permute-done | bytes 81952 | tf_op jit(solution)/shard_map/ppermute | solution.py:44
  (47 shorter events, 4.9 us)
Async XLA Ops:
  0.0 13.2 %copy-start.3 = (bf16[7,8,5120]{2,1,0:T(8,128)(2,1)S(1)}, bf16[7,8,5120]{2,1,0:T(8,128)(2,1)}, u32[]{:S(2)}) copy-start(bf16[7,8,5120]{2,1,0:T(8,128)(2,1)} %param.16) | copy-start | bytes 1720324
  1.8 0.9 copy-start.1
  2.7 10.5 %copy-start.4 = (bf16[7,8,5120]{2,1,0:T(8,128)(2,1)S(1)}, bf16[7,8,5120]{2,1,0:T(8,128)(2,1)}, u32[]{:S(2)}) copy-start(bf16[7,8,5120]{2,1,0:T(8,128)(2,1)} %param.17) | copy-start | bytes 1720324
  3.0 17.0 %collective-permute-start = (bf16[8,5120]{1,0:T(8,128)(2,1)S(1)}, bf16[8,5120]{1,0:T(8,128)(2,1)S(1)}, u32[]{:S(2)}, u32[]{:S(2)}) collective-permute-start(bf16[8,5120]{1,0:T(8,128)(2,1)S(1)} %modulate.1), channel_id=1, source_target_pairs={{0,8},{8,0},{1,9},{9,1},{2,10},{10,2},{3,11},{11,3},{4,12},{12,4},... | collective-permute-start | bytes 245768 | tf_op jit(solution)/shard_map/ppermute | solution.py:39
  11.8 60.3 %collective-permute-start.1 = (bf16[3,80,2560]{2,1,0:T(8,128)(2,1)}, bf16[3,80,2560]{2,1,0:T(8,128)(2,1)}, u32[]{:S(2)}, u32[]{:S(2)}) collective-permute-start(bf16[3,80,2560]{2,1,0:T(8,128)(2,1)} %constant_dynamic-slice_fusion), channel_id=1, source_target_pairs={{0,4},{4,0},{1,5},{5,1},{2,6},{6,2},{3,7},{7,3},{8,12},{12,8},{9,1... | collective-permute-start | bytes 3686408 | tf_op jit(solution)/shard_map/ppermute | solution.py:39
  14.7 16.7 %all-to-all-start.2 = ((bf16[8,2,14,640]{3,1,2,0:T(2,128)(2,1)}), bf16[8,2,14,640]{3,1,2,0:T(2,128)(2,1)S(1)}, u32[]{:S(2)}, u32[]{:S(2)}) async-start(bf16[8,2,14,640]{3,1,2,0:T(2,128)(2,1)} %copy.37), calls=%async_computation.2 | async-start | bytes 573440 | tf_op jit(solution)/shard_map/all_to_all | solution.py:358
  33.3 42.4 %copy-start = (bf16[3,80,5120]{2,1,0:T(8,128)(2,1)S(1)}, bf16[3,80,5120]{2,1,0:T(8,128)(2,1)}, u32[]{:S(2)}) copy-start(bf16[3,80,5120]{2,1,0:T(8,128)(2,1)} %own_ref.1) | copy-start | bytes 7372804
  33.3 42.4 %all-to-all-start = ((bf16[16,16,5120]{2,1,0:T(8,128)(2,1)}), bf16[16,16,5120]{2,1,0:T(8,128)(2,1)}, u32[]{:S(2)}, u32[]{:S(2)}) async-start(bf16[16,16,5120]{2,1,0:T(8,128)(2,1)} %broadcast_in_dim.32), calls=%async_computation | async-start | bytes 5242880 | tf_op jit(solution)/shard_map/all_to_all | solution.py:351
  72.0 3.6 %collective-permute-start.2 = (bf16[3,80,2560]{2,1,0:T(8,128)(2,1)}, bf16[3,80,2560]{2,1,0:T(8,128)(2,1)}, u32[]{:S(2)}, u32[]{:S(2)}) collective-permute-start(bf16[3,80,2560]{2,1,0:T(8,128)(2,1)} %collective-permute-done.1.near_ref), channel_id=1, source_target_pairs={{0,64},{64,0},{1,65},{65,1},{2,66},{66,2},{3,67},{67,3},{4,68},{68... | collective-permute-start | bytes 3686408 | tf_op jit(solution)/shard_map/ppermute | solution.py:39
  72.1 53.5 %collective-permute-start.6 = (bf16[2,112,640]{2,1,0:T(8,128)(2,1)S(1)}, bf16[2,112,640]{2,1,0:T(8,128)(2,1)S(1)}, u32[]{:S(2)}, u32[]{:S(2)}) collective-permute-start(bf16[2,112,640]{2,1,0:T(8,128)(2,1)S(1)} %copy.41), channel_id=1, source_target_pairs={{0,4},{4,0},{1,5},{5,1},{2,6},{6,2},{3,7},{7,3},{8,12},{12,8},{9,1... | collective-permute-start | bytes 860168 | tf_op jit(solution)/shard_map/ppermute | solution.py:39
  122.1 26.2 %all-to-all-start.3 = ((f32[8,160,128]{2,1,0:T(8,128)}), f32[8,160,128]{2,1,0:T(8,128)S(1)}, u32[]{:S(2)}, u32[]{:S(2)}) async-start(f32[8,160,128]{2,1,0:T(8,128)} %bitcast.11), calls=%async_computation.3 | async-start | bytes 1310720 | tf_op jit(solution)/shard_map/all_to_all | solution.py:373
  125.7 26.6 %copy-start.5 = (s32[7]{0:T(128)S(1)}, s32[7]{0:T(128)}, u32[]{:S(2)}) copy-start(s32[7]{0:T(128)} %param.18) | copy-start | bytes 88
  125.7 20.5 %collective-permute-start.7 = (bf16[2,224,640]{2,1,0:T(8,128)(2,1)S(1)}, bf16[2,224,640]{2,1,0:T(8,128)(2,1)S(1)}, u32[]{:S(2)}, u32[]{:S(2)}) collective-permute-start(bf16[2,224,640]{2,1,0:T(8,128)(2,1)S(1)} %pad_maximum_fusion.2), channel_id=1, source_target_pairs={{0,128},{128,0},{1,129},{129,1},{2,130},{130,2},{3,131},{131,3},{4... | collective-permute-start | bytes 1720328 | tf_op jit(solution)/shard_map/ppermute | solution.py:39
  147.4 5.3 %collective-permute-start.8 = (bf16[2,448,640]{2,1,0:T(8,128)(2,1)}, bf16[2,448,640]{2,1,0:T(8,128)(2,1)}, u32[]{:S(2)}, u32[]{:S(2)}) collective-permute-start(bf16[2,448,640]{2,1,0:T(8,128)(2,1)} %pad_maximum_fusion.1), channel_id=1, source_target_pairs={{0,64},{64,0},{1,65},{65,1},{2,66},{66,2},{3,67},{67,3},{4,68},{68... | collective-permute-start | bytes 3440648 | tf_op jit(solution)/shard_map/ppermute | solution.py:39
  148.6 2.3 %collective-permute-start.9 = (bf16[2,128,640]{2,1,0:T(8,128)(2,1)S(1)}, bf16[2,128,640]{2,1,0:T(8,128)(2,1)S(1)}, u32[]{:S(2)}, u32[]{:S(2)}) collective-permute-start(bf16[2,128,640]{2,1,0:T(8,128)(2,1)S(1)} %own_rows.1.own), channel_id=1, source_target_pairs={{192,64},{193,65},{194,66},{195,67},{196,68},{197,69},{198,70},{19... | collective-permute-start | bytes 983048 | tf_op jit(solution)/shard_map/ppermute | solution.py:376
  151.0 9.1 %collective-permute-start.10 = (bf16[2,128,640]{2,1,0:T(8,128)(2,1)S(1)}, bf16[2,128,640]{2,1,0:T(8,128)(2,1)}, u32[]{:S(2)}, u32[]{:S(2)}) collective-permute-start(bf16[2,128,640]{2,1,0:T(8,128)(2,1)S(1)} %broadcast_select_fusion), channel_id=1, source_target_pairs={{192,128},{64,0},{193,129},{65,1},{194,130},{66,2},{195,131},{67,3... | collective-permute-start | bytes 983048 | tf_op jit(solution)/shard_map/ppermute | solution.py:378
  154.1 7.0 %collective-permute-start.3 = (f32[160,256]{1,0:T(8,128)S(1)}, f32[160,256]{1,0:T(8,128)S(1)}, u32[]{:S(2)}, u32[]{:S(2)}) collective-permute-start(f32[160,256]{1,0:T(8,128)S(1)} %get-tuple-element.8.q0), channel_id=1, source_target_pairs={{0,1},{1,2},{2,3},{3,0},{4,5},{5,6},{6,7},{7,4},{8,9},{9,10},{10,1... | collective-permute-start | bytes 491528 | tf_op jit(solution)/shard_map/ppermute | solution.py:44
  155.9 7.7 %collective-permute-start.4 = (f32[160,256]{1,0:T(8,128)S(1)}, f32[160,256]{1,0:T(8,128)S(1)}, u32[]{:S(2)}, u32[]{:S(2)}) collective-permute-start(f32[160,256]{1,0:T(8,128)S(1)} %get-tuple-element.8.q0), channel_id=1, source_target_pairs={{0,2},{1,3},{2,0},{3,1},{4,6},{5,7},{6,4},{7,5},{8,10},{9,11},{10,... | collective-permute-start | bytes 491528 | tf_op jit(solution)/shard_map/ppermute | solution.py:44
  158.6 5.3 %collective-permute-start.5 = (f32[160,256]{1,0:T(8,128)S(1)}, f32[160,256]{1,0:T(8,128)S(1)}, u32[]{:S(2)}, u32[]{:S(2)}) collective-permute-start(f32[160,256]{1,0:T(8,128)S(1)} %get-tuple-element.8.q0), channel_id=1, source_target_pairs={{0,3},{1,0},{2,1},{3,2},{4,7},{5,4},{6,5},{7,6},{8,11},{9,8},{10,9... | collective-permute-start | bytes 491528 | tf_op jit(solution)/shard_map/ppermute | solution.py:44
  161.1 35.6 %copy-start.2 = (bf16[1,8,5120]{2,1,0:T(8,128)(2,1)S(1)}, bf16[1,8,5120]{2,1,0:T(8,128)(2,1)}, u32[]{:S(2)}) copy-start(bf16[1,8,5120]{2,1,0:T(8,128)(2,1)} %param.10) | copy-start | bytes 245764
  196.7 5.0 %collective-permute-start.11 = (bf16[1,8,5120]{2,1,0:T(8,128)(2,1)S(1)}, bf16[1,8,5120]{2,1,0:T(8,128)(2,1)S(1)}, u32[]{:S(2)}, u32[]{:S(2)}) collective-permute-start(bf16[1,8,5120]{2,1,0:T(8,128)(2,1)S(1)} %bitcast.24), channel_id=1, source_target_pairs={{0,64},{64,128},{128,192},{192,0},{1,65},{65,129},{129,193},{193,1... | collective-permute-start | bytes 245768 | tf_op jit(solution)/shard_map/ppermute | solution.py:44

commit v2 on v0

v2 whole, which is shorter than its diff:
```python
import functools
import math

import jax
import jax.numpy as jnp
from jax import lax
from jax.experimental import pallas as pl
from jax.experimental.pallas import tpu as pltpu
from jax.sharding import Mesh
from jax.sharding import PartitionSpec as P

AXES = ("zl", "core", "y", "zh1", "zh0", "x")
SIZES = (2, 2, 4, 2, 2, 4)
SECTION = ("zl", "core")
SHARD = ("y", "zh1", "zh0", "x")
GROUPS = ("y", "zh1")
MEMBERS = ("zh0", "x")

F32 = jnp.float32
BF16 = jnp.bfloat16
EPS = 1e-6
WIDTH = 5120
HEAD = 128
TOK = 8
SLOTS = 7
COLS = 80
PART = 640
PART_HEADS = 5
HALF_TOK = 256
CACHED = 896
TILE = 1280


def params(mebibytes):
    return pltpu.CompilerParams(vmem_limit_bytes=mebibytes * 1024 * 1024)


def swapped(value, axis):
    return lax.ppermute(value, axis, [(0, 1), (1, 0)])


def around(value, axis, by):
    length = lax.axis_size(axis)
    return lax.ppermute(value, axis, [(i, (i + by) % length) for i in range(length)])


def in_order(index, mine, other, axis=0):
    first = index == 0
    return jnp.concatenate(
        [jnp.where(first, mine, other), jnp.where(first, other, mine)], axis=axis
    )


def modulate_kernel(numbers_ref, place_ref, mine_ref, other_ref, mod_ref, out_ref):
    shift = mod_ref[0, 0:1, :]
    scale = mod_ref[0, 1:2, :]

    def of(ref):
        tokens = ref[...].astype(F32)
        centered = tokens - jnp.mean(tokens, axis=-1, keepdims=True)
        variance = jnp.mean(centered * centered, axis=-1, keepdims=True)
        return centered * lax.rsqrt(variance + EPS) * (1.0 + scale) + shift

    mine, other = of(mine_ref), of(other_ref)
    first = place_ref[5] == 0
    rows = jnp.concatenate(
        [jnp.where(first, mine, other), jnp.where(first, other, mine)], axis=0
    ).astype(BF16)
    for i in range(16):
        out_ref[i] = rows


def modulate(numbers, place, mine, other, modulation):
    return pl.pallas_call(
        modulate_kernel,
        grid_spec=pltpu.PrefetchScalarGridSpec(
            num_scalar_prefetch=2,
            grid=(1,),
            in_specs=[
                pl.BlockSpec((TOK, WIDTH), lambda i, n, p: (0, 0)),
                pl.BlockSpec((TOK, WIDTH), lambda i, n, p: (0, 0)),
                pl.BlockSpec((1, 3, WIDTH), lambda i, n, p: (n[0], 0, 0)),
            ],
            out_specs=pl.BlockSpec((16, 2 * TOK, WIDTH), lambda i, n, p: (0, 0, 0)),
        ),
        out_shape=jax.ShapeDtypeStruct((16, 2 * TOK, WIDTH), BF16),
        compiler_params=params(16),
        name="modulate",
    )(numbers, place, mine, other, modulation)


def project_kernel(
    place_ref, x_ref, own_ref, t0_ref, t1_ref, t2_ref, t3_ref,
    q_ref, kv_ref, sums_ref, m1_hbm, m2_hbm, m3_hbm, acc, m_ref, sem,
):
    step = pl.program_id(0)
    half = place_ref[1]
    mine = pl.multiple_of(half * 3 * COLS, 16)
    theirs = pl.multiple_of((1 - half) * 3 * COLS, 16)
    x = x_ref[...]

    @pl.when(step == 0)
    def _():
        acc[...] = jnp.zeros_like(acc)

    def add(weight, at):
        acc[pl.ds(at, 3 * COLS), :] += lax.dot_general(
            weight.reshape(3 * COLS, TILE), x, (((1,), (1,)), ((), ())), preferred_element_type=F32
        )

    add(own_ref[...], mine)
    for i, theirs_ref in enumerate((t0_ref, t1_ref, t2_ref, t3_ref)):

        @pl.when(step == i)
        def _(theirs_ref=theirs_ref):
            add(theirs_ref[...], theirs)

    @pl.when(step == 3)
    def _():
        q, k, v = [
            jnp.concatenate(
                [acc[(3 * e + i) * COLS : (3 * e + i + 1) * COLS, :] for e in range(2)], axis=0
            )
            for i in range(3)
        ]
        q_ref[...] = q
        for i in range(3):
            m_ref[i, :, 0:HALF_TOK] = q
        lane = lax.broadcasted_iota(jnp.int32, (2 * COLS, 128), 1)
        quarters = []
        for t in range(2):
            kt = k[:, 128 * t : 128 * t + 128]
            vt = v[:, 128 * t : 128 * t + 128]
            quarters.append(jnp.where(lane < 64, kt, pltpu.roll(vt, 64, 1)))
            quarters.append(jnp.where(lane < 64, pltpu.roll(kt, 64, 1), vt))
        for here in range(4):

            @pl.when(place_ref[2] == here)
            def _(here=here):
                kv_ref[...] = quarters[here]
                for i in range(3):
                    m_ref[i, :, HALF_TOK : HALF_TOK + 128] = quarters[here ^ (i + 1)]

        copies = [
            pltpu.make_async_copy(m_ref.at[i], to, sem.at[i])
            for i, to in enumerate((m1_hbm, m2_hbm, m3_hbm))
        ]
        for copy in copies:
            copy.start()
        sub = lax.broadcasted_iota(jnp.int32, (TOK, 128), 0)
        tile = jnp.zeros((TOK, 128), F32)
        for i, part in enumerate((q, k)):
            total = jnp.sum(part * part, axis=0, keepdims=True)
            for t in range(2):
                tile = jnp.where(sub == 2 * i + t, total[:, 128 * t : 128 * t + 128], tile)
        for i in range(32):
            sums_ref[i] = tile
        for copy in copies:
            copy.wait()


def project(place, x, own, theirs):
    def tile(j, place):
        return 2 * ((j % 2 + place[3]) % 2) + (j // 2 + place[0]) % 2

    piece = pl.BlockSpec((3, COLS, TILE), lambda j, p: (0, 0, 0))
    whole = lambda *shape: pl.BlockSpec(shape, lambda j, p: (0,) * len(shape))
    both = (2 * COLS, HALF_TOK + 128)
    outs = [(2 * COLS, HALF_TOK), (2 * COLS, 128), (32, TOK, 128)]
    return pl.pallas_call(
        project_kernel,
        grid_spec=pltpu.PrefetchScalarGridSpec(
            num_scalar_prefetch=1,
            grid=(4,),
            in_specs=[
                pl.BlockSpec((HALF_TOK, TILE), lambda j, p: (0, tile(j, p))),
                pl.BlockSpec((3, COLS, TILE), lambda j, p: (0, 0, tile(j, p))),
                piece, piece, piece, piece,
            ],
            out_specs=[whole(*shape) for shape in outs] + [pl.BlockSpec(memory_space=pltpu.HBM)] * 3,
            scratch_shapes=[
                pltpu.VMEM((6 * COLS, HALF_TOK), F32),
                pltpu.VMEM((3,) + both, F32),
                pltpu.SemaphoreType.DMA((3,)),
            ],
        ),
        out_shape=[jax.ShapeDtypeStruct(shape, F32) for shape in outs + [both] * 3],
        compiler_params=params(24),
        name="project",
    )(place, x, own, *theirs)


def gather_rows(place_ref, mine, messages, columns, held, sem, rate, gain_ref, out_ref, lanes=None):
    copies = [
        pltpu.make_async_copy(m.at[:, columns], held.at[i], sem.at[i]) for i, m in enumerate(messages)
    ]
    for copy in copies:
        copy.start()
    for i in range(4):
        if i:
            copies[i - 1].wait()
        for e in range(2):
            at = pl.multiple_of((place_ref[2] ^ i) * COLS + e * (PART // 2), 16)
            part = slice(COLS * e, COLS * e + COLS)
            raw = held[i - 1, part, :] if i else mine[part, :]
            rows = raw * rate * gain_ref[pl.ds(at, COLS), :]
            if lanes is not None:
                rows = jnp.where(lanes, rows, raw)
            out_ref[pl.ds(at, COLS), :] = rows.astype(BF16)


def all_rates(sums_ref):
    picked = [sums_ref[g] for g in range(32)]
    while len(picked) > 1:
        picked = [a + b for a, b in zip(picked[0::2], picked[1::2])]
    return lax.rsqrt(picked[0] / WIDTH + EPS)


def own_kernel(place_ref, kv0_ref, m1_hbm, m2_hbm, m3_hbm, sums_ref, gain_ref, out_ref, held, sem):
    rates = all_rates(sums_ref)
    rate = jnp.where(place_ref[2] < 2, rates[2:3, :], rates[3:4, :])
    rate = jnp.broadcast_to(rate, (TOK, 128))
    rate = jnp.where(place_ref[2] % 2 == 0, rate, pltpu.roll(rate, 64, 1))[0:1, :]
    lanes = lax.broadcasted_iota(jnp.int32, (COLS, 128), 1) < 64
    gather_rows(
        place_ref, kv0_ref, (m1_hbm, m2_hbm, m3_hbm), pl.ds(HALF_TOK, 128), held, sem,
        rate, gain_ref, out_ref, lanes,
    )


def own_rows(place, kv, messages, sums, gain):
    vmem = pl.BlockSpec(memory_space=pltpu.VMEM)
    return pl.pallas_call(
        own_kernel,
        in_specs=[pl.BlockSpec(memory_space=pltpu.SMEM), vmem]
        + [pl.BlockSpec(memory_space=pltpu.HBM)] * 3
        + [vmem, vmem],
        out_specs=vmem,
        scratch_shapes=[pltpu.VMEM((3, 2 * COLS, 128), F32), pltpu.SemaphoreType.DMA((3,))],
        out_shape=jax.ShapeDtypeStruct((PART, 128), BF16),
        compiler_params=params(8),
        name="own_rows",
    )(place, kv, *messages, sums, gain)


def absorb(q, parts, top, den, num):
    rate = math.log2(math.e) / math.sqrt(HEAD)
    turned = (((0,), (0,)), ((), ()))
    scores = []
    for part in parts:
        if isinstance(part, tuple):
            scores.append(jnp.dot(part[0], q, preferred_element_type=F32) + part[2])
        else:
            scores.append(lax.dot_general(part, q, turned, preferred_element_type=F32)[0:64])
    new_top = functools.reduce(
        jnp.maximum, [jnp.max(s, axis=0, keepdims=True) for s in scores] + ([] if top is None else [top])
    )
    if top is not None:
        factor = jnp.exp2((top - new_top) * rate)
        den, num = den * factor, num * factor
    else:
        den, num = jnp.zeros(new_top.shape, F32), jnp.zeros(q.shape, F32)
    for s, part in zip(scores, parts):
        w = jnp.exp2((s - new_top) * rate)
        den = den + jnp.sum(w, axis=0, keepdims=True)
        w = w.astype(BF16)
        if isinstance(part, tuple):
            num = num + lax.dot_general(part[1], w, turned, preferred_element_type=F32)
        else:
            w = jnp.concatenate([jnp.zeros_like(w), w], axis=0)
            num = num + jnp.dot(part, w, preferred_element_type=F32)
    return new_top, den, num


def attend_kernel(
    place_ref, q0, m1_hbm, m2_hbm, m3_hbm, sums_ref, gain_ref, c0, c1, c2, c3, own, bias_ref,
    query, stats, num_ref, held, sem,
):
    head = pl.program_id(0)

    @pl.when(head == 0)
    def _():
        rates = all_rates(sums_ref)
        rate = jnp.concatenate([rates[0:1, :], rates[1:2, :]], axis=1)
        gather_rows(
            place_ref, q0, (m1_hbm, m2_hbm, m3_hbm), pl.ds(0, HALF_TOK), held, sem,
            rate, gain_ref, query,
        )

    q = query[pl.ds(pl.multiple_of(head * HEAD, HEAD), HEAD), :]
    parts = [(c[0], c[1], bias_ref[...]) for c in (c0, c1, c2, c3)] + [own[...]]
    top, den, num = absorb(q, parts, None, None, None)
    num_ref[...] = num
    stats[0, 0:1, :] = top
    stats[0, 1:2, :] = den


def attend(place, query, messages, sums, gain, cached, own, bias):
    cached_spec = pl.BlockSpec((2, CACHED // 4, HEAD), lambda h, p: (0, 0, h))
    whole = lambda *shape: pl.BlockSpec(shape, lambda h, p: (0,) * len(shape))
    return pl.pallas_call(
        attend_kernel,
        grid_spec=pltpu.PrefetchScalarGridSpec(
            num_scalar_prefetch=1,
            grid=(PART_HEADS,),
            in_specs=[whole(2 * COLS, HALF_TOK)]
            + [pl.BlockSpec(memory_space=pltpu.HBM)] * 3
            + [whole(32, TOK, 128), whole(PART, 1)]
            + [cached_spec] * 4
            + [pl.BlockSpec((HEAD, 128), lambda h, p: (h, 0)), whole(CACHED // 4, 1)],
            out_specs=[
                whole(PART, HALF_TOK),
                pl.BlockSpec((1, 8, HALF_TOK), lambda h, p: (h, 0, 0)),
                pl.BlockSpec((HEAD, HALF_TOK), lambda h, p: (h, 0)),
            ],
            scratch_shapes=[pltpu.VMEM((3, 2 * COLS, HALF_TOK), F32), pltpu.SemaphoreType.DMA((3,))],
        ),
        out_shape=[
            jax.ShapeDtypeStruct((PART, HALF_TOK), BF16),
            jax.ShapeDtypeStruct((PART_HEADS, 8, HALF_TOK), F32),
            jax.ShapeDtypeStruct((PART, HALF_TOK), F32),
        ],
        compiler_params=params(14),
        cost_estimate=pl.CostEstimate(flops=700_000_000, bytes_accessed=5_000_000, transcendentals=1_300_000),
        name="attend",
    )(place, query, *messages, sums, gain, *cached, own, bias)


def close_kernel(place_ref, query, stats_ref, num_ref, near, spread, beside, out_ref, stats):
    stats[...] = jnp.zeros_like(stats)
    first = place_ref[0] == 0

    for h in range(PART_HEADS):
        cols = slice(HEAD * h, HEAD * h + HEAD)
        parts = [
            near[cols, :],
            jnp.where(first, spread[0, cols, :], beside[0, cols, :]),
            jnp.where(first, spread[1, cols, :], beside[1, cols, :]),
        ]
        top, den, num = absorb(
            query[cols, :], parts, stats_ref[h, 0:1, :], stats_ref[h, 1:2, :], num_ref[cols, :]
        )
        out_ref[:, cols] = (num / den).T.astype(BF16)
        stats[h : h + 1, :] = top
        stats[h + 8 : h + 9, :] = den
    full = stats[0:16, :]
    hi = full.astype(BF16).astype(F32)
    mid = (full - hi).astype(BF16).astype(F32)
    stats[0:16, :] = hi
    stats[16:32, :] = mid
    stats[32:48, :] = full - hi - mid
    out_ref[:, PART : PART + 128] = stats[...].T.astype(BF16)


def close(place, query, stats, num, fresh):
    vmem = pl.BlockSpec(memory_space=pltpu.VMEM)
    return pl.pallas_call(
        close_kernel,
        in_specs=[pl.BlockSpec(memory_space=pltpu.SMEM)] + [vmem] * 6,
        out_shape=jax.ShapeDtypeStruct((HALF_TOK, PART + 128), BF16),
        scratch_shapes=[pltpu.VMEM((128, HALF_TOK), F32)],
        compiler_params=params(8),
        name="close",
    )(place, query, stats, num, *fresh)


def finish_kernel(step_ref, in_ref, hidden_ref, mod_ref, out_ref):
    for g in range(8):
        tops, dens = [], []
        for j in range(4):
            parts = in_ref[8 * (g // 2) + 2 * j + g % 2, :, PART : PART + 128].astype(F32)
            full = parts[:, 0:16] + parts[:, 16:32] + parts[:, 32:48]
            tops.append(full[:, 0:8])
            dens.append(full[:, 8:16])
        top = jnp.maximum(jnp.maximum(tops[0], tops[1]), jnp.maximum(tops[2], tops[3]))
        shares = [jnp.exp((t - top) * (1.0 / math.sqrt(HEAD))) * d for t, d in zip(tops, dens)]
        total = shares[0] + shares[1] + shares[2] + shares[3]
        for n in range(PART_HEADS):
            cols = slice(HEAD * n, HEAD * n + HEAD)
            to = slice(PART * g + HEAD * n, PART * g + HEAD * n + HEAD)
            joined = jnp.zeros((TOK, HEAD), F32)
            for j in range(4):
                joined = joined + in_ref[8 * (g // 2) + 2 * j + g % 2, :, cols].astype(F32) * shares[j][:, n : n + 1]
            joined = joined / total[:, n : n + 1]
            out_ref[:, to] = (
                hidden_ref[:, to].astype(F32) + mod_ref[0, 2:3, to] * joined
            ).astype(BF16)


def finish(shares, hidden, modulation, step_index):
    return pl.pallas_call(
        finish_kernel,
        grid_spec=pltpu.PrefetchScalarGridSpec(
            num_scalar_prefetch=1,
            grid=(1,),
            in_specs=[
                pl.BlockSpec((32, TOK, PART + 128), lambda i, step: (0, 0, 0)),
                pl.BlockSpec((TOK, WIDTH), lambda i, step: (0, 0)),
                pl.BlockSpec((1, 3, WIDTH), lambda i, step: (step[0], 0, 0)),
            ],
            out_specs=pl.BlockSpec((TOK, WIDTH), lambda i, step: (0, 0)),
        ),
        out_shape=jax.ShapeDtypeStruct((TOK, WIDTH), BF16),
        compiler_params=params(8),
        name="finish",
    )(step_index, shares, hidden, modulation)


def flipped(value, axes, sizes, by):
    count = math.prod(sizes)
    return lax.ppermute(value, axes, [(i, i ^ by) for i in range(count)])


def shards(
    hidden, w_qkv, q_gain, k_gain, modulation, step_index, cache_k, cache_v, slot_rank, visible
):
    zl, core = lax.axis_index("zl"), lax.axis_index("core")
    zh1, half, x_here = lax.axis_index("zh1"), lax.axis_index("zh0"), lax.axis_index("x")
    y_here = lax.axis_index("y")
    fetch = lax.axis_index(SECTION)
    group = lax.axis_index(GROUPS)
    place = jnp.stack([core, half, x_here, zl, y_here, zh1]).astype(jnp.int32)

    moved = [(s, (s + 1) % 4) for s in range(4)]
    mine = lax.ppermute(hidden[0], SECTION, moved)
    other = lax.ppermute(
        hidden[0], SECTION + ("zh1",), [(2 * s + z, 2 * t + 1 - z) for s, t in moved for z in range(2)]
    )
    numbers = lax.ppermute(jnp.concatenate([step_index, visible]), SECTION, moved)

    w_sent = lax.dynamic_slice_in_dim(w_qkv, fetch * TILE, TILE, 2)
    w_sent, mine, other = lax.optimization_barrier((w_sent, mine, other))
    w0 = swapped(w_sent, "zh0")
    pair = modulate(numbers, place, mine, other, modulation)
    tokens = lax.all_to_all(pair, ("y", "x"), 0, 0, tiled=True).reshape(HALF_TOK, WIDTH)
    w0, cache_k, cache_v = lax.optimization_barrier((w0, cache_k, cache_v))
    w1 = swapped(w0, "zl")
    w2 = swapped(w0, "core")

    caches = jnp.stack([cache_k, cache_v]).reshape(2, SLOTS * TOK, WIDTH)
    towards = 2 * (y_here ^ fetch)
    c_same = lax.dynamic_slice_in_dim(caches, (towards + zh1) * PART, PART, 2)
    c_flip = lax.dynamic_slice_in_dim(caches, ((towards ^ 4) + 1 - zh1) * PART, PART, 2)
    places = [(f, y, z) for f in range(4) for y in range(4) for z in range(2)]
    spot = lambda f, y, z: 8 * f + 2 * y + z
    four = SECTION + GROUPS
    c_same = lax.ppermute(c_same, four, [(spot(f, y, z), spot(f, y ^ f, z)) for f, y, z in places])
    c_flip = lax.ppermute(
        c_flip, four, [(spot(f ^ 2, y, z), spot(f, y ^ f, 1 - z)) for f, y, z in places]
    )

    new_rank = (slot_rank + 1) % SLOTS
    seen = (slot_rank != SLOTS - 1) & (new_rank < numbers[1])
    bias = jnp.where(seen, 0.0, -jnp.inf).astype(F32)
    bias = jnp.tile(jnp.repeat(bias, TOK), CACHED // (4 * TOK * SLOTS))[:, None]
    q_cols = lax.dynamic_slice_in_dim(q_gain, group * PART, PART)[:, None]
    k_cols = lax.dynamic_slice_in_dim(k_gain, group * PART, PART)[:, None]

    w1, c_same, c_flip, bias, q_cols, k_cols = lax.optimization_barrier(
        (w1, c_same, c_flip, bias, q_cols, k_cols)
    )
    w3 = swapped(w1, "core")
    cached = jnp.concatenate([c_same, c_flip], axis=1)
    across = swapped(cached, "zh0")
    query, kv, sums, m1, m2, m3 = project(place, tokens, w_qkv, (w0, w1, w2, w3))
    messages = [flipped(m, "x", (4,), i) for i, m in ((1, m1), (2, m2), (3, m3))]
    sums = lax.all_to_all(sums, ("y", "zh1", "x"), 0, 0, tiled=True)
    messages, sums, across = lax.optimization_barrier((messages, sums, across))
    cached = jnp.concatenate([cached, across], axis=1)
    beyond = swapped(cached, "zl")
    beside = swapped(cached, "core")
    own = own_rows(place, kv, messages, sums, k_cols)
    near = swapped(own, "zh0")
    low = lax.ppermute(own, SECTION, [(0, 2)])
    high = lax.ppermute(own, SECTION + ("zh0",), [(h, 2 * 2 + 1 - h) for h in range(2)])
    near, low, high, beyond, beside = lax.optimization_barrier((near, low, high, beyond, beside))
    cached = [cached, beyond, beside, swapped(beyond, "core")]
    fresh = jnp.where(zl == 0, jnp.stack([own, near]), jnp.stack([low, high]))
    passed = lax.ppermute(fresh, SECTION, [(0, 1), (2, 3)])
    query, stats, num = attend(place, query, messages, sums, q_cols, cached, own, bias)
    shares = close(place, query, stats, num, [near, fresh, passed])
    shares = shares.reshape(32, TOK, PART + 128)
    shares = lax.all_to_all(shares, ("y", "x", "zh1"), 0, 0, tiled=True)
    return finish(shares, mine, modulation, numbers)[None]


def solution(mesh):
    fine = Mesh(mesh.devices.reshape(SIZES), AXES)
    return jax.shard_map(
        shards,
        mesh=fine,
        in_specs=(
            P(SECTION, SHARD, None),
            P(None, SHARD, None),
            P(),
            P(),
            P(),
            P(SECTION),
            P(None, SHARD, None),
            P(None, SHARD, None),
            P(),
            P(SECTION),
        ),
        out_specs=P(SECTION, SHARD, None),
        check_vma=False,
    )
```

time: 1920 us -> 178 us (0.09)
  waiting for transfers between devices: 1260 us -> 63 us
  blocking collectives: 573 us -> 23.5 us
  starting transfers between devices: 16.2 us -> 44.9 us
  Pallas kernels: 0 us -> 21.9 us
    unnamed x6 -> x0, waiting for transfers between devices: 609 us -> none
    reduce_scatter x1 -> x0, waiting for transfers between devices: 414 us -> none  [shards(): lax.psum_scatter(scaled_num, 'shard', scatter_dimension=0, tiled=True)]
    pmax x1 -> x0, blocking collectives: 378 us -> none  [shards(): lax.pmax(max_rows.astype(jnp.bfloat16), 'shard').astype(max_rows.dtype)]
    psum x1 -> x0, blocking collectives: 194 us -> none  [shards(): lax.psum((jnp.sum(q_part * q_part, axis=1), jnp.sum(k_part * k_part, axis...]
    all_gather x2 -> x0, waiting for transfers between devices: 189 us -> none  [the longest x1 95.2 us: shards(): queries = lax.all_gather(q_half, 'shard', axis=1, tiled=True)]
    ppermute x1 -> x20, waiting for transfers between devices: 3.85 us -> 63 us  [the longest x9 38.3 us: swapped(): return lax.ppermute(value, axis, [(0, 1), (1, 0)])]
    psum x1 -> x0, waiting for transfers between devices: 31.1 us -> none  [spread(): return lax.psum(jnp.where(mine, shard, jnp.zeros_like(shard)), axis)]
    ppermute x1 -> x20, starting transfers between devices: 0.08 us -> 30 us  [the longest x9 7.39 us: swapped(): return lax.ppermute(value, axis, [(0, 1), (1, 0)])]
  transfers between devices with their start and end apart: 8 -> 22, of which waited for: 7 -> 9; matrix products, arithmetic and copies ran while one was open for 1% -> 6% of each run, Pallas kernels for 0% -> 9%
where the time goes in v2:
time: 178 us; the launch traced here: 176 us
  waiting for transfers between devices  63 us (35%)
  starting transfers between devices  44.9 us (25%)
  blocking collectives  23.5 us (13%)
  Pallas kernels  21.9 us (12%)
  local copies, waits for them, and re-layouts  18.1 us (10%)
  other arithmetic  3.22 us (2%)
    ppermute x9, waiting for transfers between devices, swapped(): return lax.ppermute(value, axis, [(0, 1), (1, 0)])  38.3 us
    all_to_all x1, blocking collectives, shards(): shares = lax.all_to_all(shares, ('y', 'x', 'zh1'), 0, 0, tiled=True)  23.5 us
    unnamed x35, local copies, waits for them, and re-layouts  12.3 us
    ppermute x3, waiting for transfers between devices, flipped(): return lax.ppermute(value, axes, [(i, i ^ by) for i in range(count)])  12 us
    ppermute x1, waiting for transfers between devices, shards(): lax.ppermute(c_flip, four, [(spot(f ^ 2, y, z), spot(f, y ^ f, 1 - z)) fo...  7.98 us
    all_to_all x1, starting transfers between devices, shards(): sums = lax.all_to_all(sums, ('y', 'zh1', 'x'), 0, 0, tiled=True)  7.81 us
    pallas_call x1, Pallas kernels, project(): pl.pallas_call(project_kernel, grid_spec=pltpu.PrefetchScalarGridSpec(num...  7.64 us
    ppermute x9, starting transfers between devices, swapped(): return lax.ppermute(value, axis, [(0, 1), (1, 0)])  7.39 us
  transfers between devices with their start and end apart: 22, of which 9 were waited for; matrix products, arithmetic and copies ran while one was open for 6% of the time, Pallas kernels for 9%

profile of v2, /device:TPU:32, one launch (start us, length us, event | category | flops | bytes accessed | tf_op | source)
XLA Modules:
  0.0 176.4 jit_solution(15552317349796706210)
XLA Ops:
  0.0 7.0 %collective-permute-start.2 = (bf16[8,5120]{1,0:T(8,128)(2,1)}, bf16[8,5120]{1,0:T(8,128)(2,1)S(1)}, u32[]{:S(2)}, u32[]{:S(2)}) collective-permute-start(bf16[8,5120]{1,0:T(8,128)(2,1)} %bitcast.26), channel_id=1, source_target_pairs={{0,72},{8,64},{64,136},{72,128},{128,200},{136,192},{192,8},{200,0... | collective-permute-start | bytes 245768 | tf_op jit(solution)/shard_map/ppermute | solution.py:426
  8.4 1.9 %constant_dynamic-slice_fusion = bf16[3,80,1280]{2,1,0:T(8,128)(2,1)} fusion(bf16[3,80,5120]{2,1,0:T(8,128)(2,1)} %own_ref.1, s32[]{:T(128)S(6)} %select_n.32), kind=kLoop, calls=%fused_computation.13 | loop fusion | bytes 1228804 | tf_op jit(solution)/shard_map/dynamic_slice | solution.py:431
  10.4 1.1 copy.13.mod_ref
  11.6 2.5 %modulate.1 = bf16[16,16,5120]{2,1,0:T(8,128)(2,1)} custom-call(s32[2]{0:T(128)S(1)} %collective-permute-done.numbers_ref.step_ref, s32[6]{0:T(128)S(1)} %stack.54.place_ref, bf16[8,5120]{1,0:T(8,128)(2,1)S(1)} %collective-permute-done.1.mine_ref.hidden_ref, bf16[8,5120]{1,0:T(8,128)(2,1)S(1)} %collective-permute-done.2.other_ref, ...), custom_call_target="tpu_custom_call" | custom-call | tf_op jit(solution)/shard_map/modulate/pallas_call | solution.py:74
  14.1 7.2 %all-to-all-start = ((bf16[16,16,5120]{2,1,0:T(8,128)(2,1)}), bf16[16,16,5120]{2,1,0:T(8,128)(2,1)S(1)}, u32[]{:S(2)}, u32[]{:S(2)}) async-start(bf16[16,16,5120]{2,1,0:T(8,128)(2,1)} %modulate.1), calls=%async_computation | async-start | bytes 5242880 | tf_op jit(solution)/shard_map/all_to_all | solution.py:435
  21.3 1.6 collective-permute-start.3
  22.8 27.6 %collective-permute-done.3.t0_ref = bf16[3,80,1280]{2,1,0:T(8,128)(2,1)} collective-permute-done((bf16[3,80,1280]{2,1,0:T(8,128)(2,1)}, bf16[3,80,1280]{2,1,0:T(8,128)(2,1)}, u32[]{:S(2)}, u32[]{:S(2)}) %collective-permute-start.3) | collective-permute-done | bytes 614432 | tf_op jit(solution)/shard_map/ppermute | solution.py:39
  50.4 2.9 %collective-permute-start.4 = (bf16[3,80,1280]{2,1,0:T(8,128)(2,1)}, bf16[3,80,1280]{2,1,0:T(8,128)(2,1)}, u32[]{:S(2)}, u32[]{:S(2)}) collective-permute-start(bf16[3,80,1280]{2,1,0:T(8,128)(2,1)} %collective-permute-done.3.t0_ref), channel_id=1, source_target_pairs={{0,128},{128,0},{1,129},{129,1},{2,130},{130,2},{3,131},{131,3},{4... | collective-permute-start | bytes 1843208 | tf_op jit(solution)/shard_map/ppermute | solution.py:39
  55.5 1.7 fusion
  57.1 5.0 %collective-permute-start.5 = (bf16[2,56,640]{2,1,0:T(8,128)(2,1)}, bf16[2,56,640]{2,1,0:T(8,128)(2,1)S(1)}, u32[]{:S(2)}, u32[]{:S(2)}) collective-permute-start(bf16[2,56,640]{2,1,0:T(8,128)(2,1)} %get-tuple-element.68), channel_id=1, source_target_pairs={{0,0},{8,8},{16,16},{24,24},{32,32},{40,40},{48,48},{56,56},{64,80... | collective-permute-start | bytes 430088 | tf_op jit(solution)/shard_map/ppermute | solution.py:447
  63.2 3.7 %collective-permute-done.5 = bf16[2,56,640]{2,1,0:T(8,128)(2,1)S(1)} collective-permute-done((bf16[2,56,640]{2,1,0:T(8,128)(2,1)}, bf16[2,56,640]{2,1,0:T(8,128)(2,1)S(1)}, u32[]{:S(2)}, u32[]{:S(2)}) %collective-permute-start.5) | collective-permute-done | bytes 143392 | tf_op jit(solution)/shard_map/ppermute | solution.py:447
  66.8 8.0 %collective-permute-done.6 = bf16[2,56,640]{2,1,0:T(8,128)(2,1)S(1)} collective-permute-done((bf16[2,56,640]{2,1,0:T(8,128)(2,1)}, bf16[2,56,640]{2,1,0:T(8,128)(2,1)S(1)}, u32[]{:S(2)}, u32[]{:S(2)}) %collective-permute-start.6) | collective-permute-done | bytes 143392 | tf_op jit(solution)/shard_map/ppermute | solution.py:448
  77.9 1.7 copy-done
  79.6 1.1 copy-done.2
  80.7 1.1 copy-done.4
  81.8 7.6 %project.1 = (f32[160,256]{1,0:T(8,128)S(1)}, f32[160,128]{1,0:T(8,128)S(1)}, f32[32,8,128]{2,1,0:T(8,128)}, f32[160,384]{1,0:T(8,128)S(1)}, f32[160,384]{1,0:T(8,128)S(1)}, /*index=5*/f32[160,384]{1,0:T(8,128)S(1)}) custom-call(s32[6]{0:T(128)S(1)} %stack.54.place_ref, bf16[256,5120]{1,0:T(8,128)(2,1)S(1)} %bitcast.17, bf16[3,80,5120]{2,1,0:T(8,128)(2,1)S(1)} %copy-done, ...), custom_call_target="tpu_custom_call" | custom-call | tf_op jit(solution)/shard_map/project/pallas_call | solution.py:170
  91.4 7.8 %all-to-all-start.1 = ((f32[32,8,128]{2,1,0:T(8,128)}), f32[32,8,128]{2,1,0:T(8,128)S(1)}, u32[]{:S(2)}, u32[]{:S(2)}) async-start(f32[32,8,128]{2,1,0:T(8,128)} %get-tuple-element.47), calls=%async_computation.1 | async-start | bytes 262144 | tf_op jit(solution)/shard_map/all_to_all | solution.py:467
  99.2 1.9 %collective-permute-start.9 = (f32[160,384]{1,0:T(8,128)}, f32[160,384]{1,0:T(8,128)S(1)}, u32[]{:S(2)}, u32[]{:S(2)}) collective-permute-start(f32[160,384]{1,0:T(8,128)} %copy-done.11), channel_id=1, source_target_pairs={{0,1},{1,0},{2,3},{3,2},{4,5},{5,4},{6,7},{7,6},{8,9},{9,8},{10,11... | collective-permute-start | bytes 737288 | tf_op jit(solution)/shard_map/ppermute | solution.py:411
  101.1 2.7 %collective-permute-start.10 = (f32[160,384]{1,0:T(8,128)S(1)}, f32[160,384]{1,0:T(8,128)S(1)}, u32[]{:S(2)}, u32[]{:S(2)}) collective-permute-start(f32[160,384]{1,0:T(8,128)S(1)} %get-tuple-element.45), channel_id=1, source_target_pairs={{0,2},{1,3},{2,0},{3,1},{4,6},{5,7},{6,4},{7,5},{8,10},{9,11},{10,... | collective-permute-start | bytes 737288 | tf_op jit(solution)/shard_map/ppermute | solution.py:411
  105.9 3.4 %collective-permute-done.9.m1_hbm = f32[160,384]{1,0:T(8,128)S(1)} collective-permute-done((f32[160,384]{1,0:T(8,128)}, f32[160,384]{1,0:T(8,128)S(1)}, u32[]{:S(2)}, u32[]{:S(2)}) %collective-permute-start.9) | collective-permute-done | bytes 245792 | tf_op jit(solution)/shard_map/ppermute | solution.py:411
  109.3 6.5 %collective-permute-done.10.m2_hbm = f32[160,384]{1,0:T(8,128)S(1)} collective-permute-done((f32[160,384]{1,0:T(8,128)S(1)}, f32[160,384]{1,0:T(8,128)S(1)}, u32[]{:S(2)}, u32[]{:S(2)}) %collective-permute-start.10) | collective-permute-done | bytes 245792 | tf_op jit(solution)/shard_map/ppermute | solution.py:411
  115.8 2.1 %collective-permute-done.11.m3_hbm = f32[160,384]{1,0:T(8,128)S(1)} collective-permute-done((f32[160,384]{1,0:T(8,128)S(1)}, f32[160,384]{1,0:T(8,128)S(1)}, u32[]{:S(2)}, u32[]{:S(2)}) %collective-permute-start.11) | collective-permute-done | bytes 245792 | tf_op jit(solution)/shard_map/ppermute | solution.py:411
  121.3 2.4 %collective-permute-start.13 = (bf16[640,128]{1,0:T(8,128)(2,1)S(1)}, bf16[640,128]{1,0:T(8,128)(2,1)S(1)}, u32[]{:S(2)}, u32[]{:S(2)}) collective-permute-start(bf16[640,128]{1,0:T(8,128)(2,1)S(1)} %own_rows.1.own), channel_id=1, source_target_pairs={{0,4},{4,0},{1,5},{5,1},{2,6},{6,2},{3,7},{7,3},{8,12},{12,8},{9,1... | collective-permute-start | bytes 491528 | tf_op jit(solution)/shard_map/ppermute | solution.py:39
  123.8 1.3 collective-permute-start.14
  125.1 1.3 collective-permute-start.15
  126.4 10.0 %collective-permute-done.13.near = bf16[640,128]{1,0:T(8,128)(2,1)S(1)} collective-permute-done((bf16[640,128]{1,0:T(8,128)(2,1)S(1)}, bf16[640,128]{1,0:T(8,128)(2,1)S(1)}, u32[]{:S(2)}, u32[]{:S(2)}) %collective-permute-start.13) | collective-permute-done | bytes 163872 | tf_op jit(solution)/shard_map/ppermute | solution.py:39
  136.4 1.1 collective-permute-done.14
  137.7 3.1 %collective-permute-start.19 = (bf16[2,640,128]{2,1,0:T(8,128)(2,1)S(1)}, bf16[2,640,128]{2,1,0:T(8,128)(2,1)}, u32[]{:S(2)}, u32[]{:S(2)}) collective-permute-start(bf16[2,640,128]{2,1,0:T(8,128)(2,1)S(1)} %maximum_select_fusion.spread), channel_id=1, source_target_pairs={{0,64},{128,192},{1,65},{129,193},{2,66},{130,194},{3,67},{131,195... | collective-permute-start | bytes 983048 | tf_op jit(solution)/shard_map/ppermute | solution.py:479
  142.1 6.5 %attend.1 = (bf16[640,256]{1,0:T(8,128)(2,1)S(1)}, f32[5,8,256]{2,1,0:T(8,128)S(1)}, f32[640,256]{1,0:T(8,128)S(1)}) custom-call(s32[6]{0:T(128)S(1)} %stack.54.place_ref, f32[160,256]{1,0:T(8,128)S(1)} %copy-done.8, f32[160,384]{1,0:T(8,128)S(1)} %collective-permute-done.9.m1_hbm, f32[160,384]{1,0:T(8,128)S(1)} %collective-permute-done.10.m2_hbm, ...), custom_call_target="tpu_custom_call" | custom-call | flops 700000000 | bytes 5000000 | tf_op jit(solution)/shard_map/attend/pallas_call | solution.py:301
  148.6 2.0 %close.1 = bf16[256,768]{1,0:T(8,128)(2,1)S(1)} custom-call(s32[6]{0:T(128)S(1)} %stack.54.place_ref, bf16[640,256]{1,0:T(8,128)(2,1)S(1)} %get-tuple-element.61.query, f32[5,8,256]{2,1,0:T(8,128)S(1)} %get-tuple-element.62.stats_ref, f32[640,256]{1,0:T(8,128)S(1)} %get-tuple-element.63.num_ref, bf16[640,128]{1,0:T(8,128)(2,1)S(1)} %collective-permute-done.13.near, ...), custom_call_target="tpu_custom_call" | custom-call | tf_op jit(solution)/shard_map/close/pallas_call | solution.py:357
  150.6 23.5 %all_to_all.15.in_ref = bf16[32,8,768]{2,1,0:T(8,128)(2,1)S(1)} all-to-all(bf16[32,8,768]{2,1,0:T(8,128)(2,1)S(1)} %bitcast.18), channel_id=1, replica_groups=mesh['zl'=2,'core'=2,'y'=4,'zh1'=2,'zh0'=2,'x'=4] {'y','x','zh1'}, dimensions={0} | all-to-all | bytes 786432 | tf_op jit(solution)/shard_map/all_to_all | solution.py:483
  174.1 2.2 %finish.1 = bf16[8,5120]{1,0:T(8,128)(2,1)} custom-call(s32[2]{0:T(128)S(1)} %collective-permute-done.numbers_ref.step_ref, bf16[32,8,768]{2,1,0:T(8,128)(2,1)S(1)} %all_to_all.15.in_ref, bf16[8,5120]{1,0:T(8,128)(2,1)S(1)} %copy-done.6, f32[4,3,5120]{2,1,0:T(4,128)S(1)} %copy.13.mod_ref), custom_call_target="tpu_custom_call" | custom-call | tf_op jit(solution)/shard_map/finish/pallas_call | solution.py:391
  (74 shorter events, 15.4 us)
Async XLA Ops:
  0.0 11.6 %collective-permute-start.1 = (bf16[8,5120]{1,0:T(8,128)(2,1)}, bf16[8,5120]{1,0:T(8,128)(2,1)S(1)}, u32[]{:S(2)}, u32[]{:S(2)}) collective-permute-start(bf16[8,5120]{1,0:T(8,128)(2,1)} %bitcast.25), channel_id=1, source_target_pairs={{0,64},{64,128},{128,192},{192,0},{1,65},{65,129},{129,193},{193,1... | collective-permute-start | bytes 245768 | tf_op jit(solution)/shard_map/ppermute | solution.py:425
  0.0 11.6 %collective-permute-start.2 = (bf16[8,5120]{1,0:T(8,128)(2,1)}, bf16[8,5120]{1,0:T(8,128)(2,1)S(1)}, u32[]{:S(2)}, u32[]{:S(2)}) collective-permute-start(bf16[8,5120]{1,0:T(8,128)(2,1)} %bitcast.26), channel_id=1, source_target_pairs={{0,72},{8,64},{64,136},{72,128},{128,200},{136,192},{192,8},{200,0... | collective-permute-start | bytes 245768 | tf_op jit(solution)/shard_map/ppermute | solution.py:426
  8.4 3.2 %collective-permute-start = (s32[2]{0:T(128)S(1)}, s32[2]{0:T(128)S(1)}, u32[]{:S(2)}, u32[]{:S(2)}) collective-permute-start(s32[2]{0:T(128)S(1)} %pad_add_fusion), channel_id=1, source_target_pairs={{0,64},{64,128},{128,192},{192,0},{1,65},{65,129},{129,193},{193,1... | collective-permute-start | bytes 32 | tf_op jit(solution)/shard_map/ppermute | solution.py:429
  11.6 2.5 %copy-start.5 = (bf16[8,5120]{1,0:T(8,128)(2,1)}, bf16[8,5120]{1,0:T(8,128)(2,1)S(1)}, u32[]{:S(2)}) copy-start(bf16[8,5120]{1,0:T(8,128)(2,1)S(1)} %collective-permute-done.1.mine_ref.hidden_ref) | copy-start | bytes 245764
  14.1 41.4 %copy-start.12 = (bf16[7,8,5120]{2,1,0:T(8,128)(2,1)S(1)}, bf16[7,8,5120]{2,1,0:T(8,128)(2,1)}, u32[]{:S(2)}) copy-start(bf16[7,8,5120]{2,1,0:T(8,128)(2,1)} %param.16) | copy-start | bytes 1720324
  14.1 48.1 %copy-start.15 = (s32[7]{0:T(128)S(1)}, s32[7]{0:T(128)}, u32[]{:S(2)}) copy-start(s32[7]{0:T(128)} %param.18) | copy-start | bytes 88
  14.1 63.8 %all-to-all-start = ((bf16[16,16,5120]{2,1,0:T(8,128)(2,1)}), bf16[16,16,5120]{2,1,0:T(8,128)(2,1)S(1)}, u32[]{:S(2)}, u32[]{:S(2)}) async-start(bf16[16,16,5120]{2,1,0:T(8,128)(2,1)} %modulate.1), calls=%async_computation | async-start | bytes 5242880 | tf_op jit(solution)/shard_map/all_to_all | solution.py:435
  21.3 29.1 %collective-permute-start.3 = (bf16[3,80,1280]{2,1,0:T(8,128)(2,1)}, bf16[3,80,1280]{2,1,0:T(8,128)(2,1)}, u32[]{:S(2)}, u32[]{:S(2)}) collective-permute-start(bf16[3,80,1280]{2,1,0:T(8,128)(2,1)} %constant_dynamic-slice_fusion), channel_id=1, source_target_pairs={{0,4},{4,0},{1,5},{5,1},{2,6},{6,2},{3,7},{7,3},{8,12},{12,8},{9,1... | collective-permute-start | bytes 1843208 | tf_op jit(solution)/shard_map/ppermute | solution.py:39
  50.4 24.4 %collective-permute-start.4 = (bf16[3,80,1280]{2,1,0:T(8,128)(2,1)}, bf16[3,80,1280]{2,1,0:T(8,128)(2,1)}, u32[]{:S(2)}, u32[]{:S(2)}) collective-permute-start(bf16[3,80,1280]{2,1,0:T(8,128)(2,1)} %collective-permute-done.3.t0_ref), channel_id=1, source_target_pairs={{0,128},{128,0},{1,129},{129,1},{2,130},{130,2},{3,131},{131,3},{4... | collective-permute-start | bytes 1843208 | tf_op jit(solution)/shard_map/ppermute | solution.py:39
  57.1 9.7 %collective-permute-start.5 = (bf16[2,56,640]{2,1,0:T(8,128)(2,1)}, bf16[2,56,640]{2,1,0:T(8,128)(2,1)S(1)}, u32[]{:S(2)}, u32[]{:S(2)}) collective-permute-start(bf16[2,56,640]{2,1,0:T(8,128)(2,1)} %get-tuple-element.68), channel_id=1, source_target_pairs={{0,0},{8,8},{16,16},{24,24},{32,32},{40,40},{48,48},{56,56},{64,80... | collective-permute-start | bytes 430088 | tf_op jit(solution)/shard_map/ppermute | solution.py:447
  62.1 12.7 %collective-permute-start.6 = (bf16[2,56,640]{2,1,0:T(8,128)(2,1)}, bf16[2,56,640]{2,1,0:T(8,128)(2,1)S(1)}, u32[]{:S(2)}, u32[]{:S(2)}) collective-permute-start(bf16[2,56,640]{2,1,0:T(8,128)(2,1)} %get-tuple-element.67), channel_id=1, source_target_pairs={{128,8},{136,0},{144,24},{152,16},{160,40},{168,32},{176,56},{184,... | collective-permute-start | bytes 430088 | tf_op jit(solution)/shard_map/ppermute | solution.py:448
  63.1 12.5 %collective-permute-start.7 = (bf16[3,80,1280]{2,1,0:T(8,128)(2,1)}, bf16[3,80,1280]{2,1,0:T(8,128)(2,1)S(1)}, u32[]{:S(2)}, u32[]{:S(2)}) collective-permute-start(bf16[3,80,1280]{2,1,0:T(8,128)(2,1)} %collective-permute-done.3.t0_ref), channel_id=1, source_target_pairs={{0,64},{64,0},{1,65},{65,1},{2,66},{66,2},{3,67},{67,3},{4,68},{68... | collective-permute-start | bytes 1843208 | tf_op jit(solution)/shard_map/ppermute | solution.py:39
  66.8 11.1 %copy-start.13 = (bf16[2,56,640]{2,1,0:T(8,128)(2,1)}, bf16[2,56,640]{2,1,0:T(8,128)(2,1)S(1)}, u32[]{:S(2)}) copy-start(bf16[2,56,640]{2,1,0:T(8,128)(2,1)S(1)} %collective-permute-done.5) | copy-start | bytes 430084
  74.8 3.1 %copy-start.14 = (bf16[2,56,640]{2,1,0:T(8,128)(2,1)}, bf16[2,56,640]{2,1,0:T(8,128)(2,1)S(1)}, u32[]{:S(2)}) copy-start(bf16[2,56,640]{2,1,0:T(8,128)(2,1)S(1)} %collective-permute-done.6) | copy-start | bytes 430084
  74.8 2.3 %collective-permute-start.8 = (bf16[3,80,1280]{2,1,0:T(8,128)(2,1)}, bf16[3,80,1280]{2,1,0:T(8,128)(2,1)S(1)}, u32[]{:S(2)}, u32[]{:S(2)}) collective-permute-start(bf16[3,80,1280]{2,1,0:T(8,128)(2,1)} %collective-permute-done.4.t1_ref), channel_id=1, source_target_pairs={{0,64},{64,0},{1,65},{65,1},{2,66},{66,2},{3,67},{67,3},{4,68},{68... | collective-permute-start | bytes 1843208 | tf_op jit(solution)/shard_map/ppermute | solution.py:39
  75.6 30.3 %collective-permute-start.12 = (bf16[2,112,640]{2,1,0:T(8,128)(2,1)}, bf16[2,112,640]{2,1,0:T(8,128)(2,1)}, u32[]{:S(2)}, u32[]{:S(2)}) collective-permute-start(bf16[2,112,640]{2,1,0:T(8,128)(2,1)} %pad_maximum_fusion), channel_id=1, source_target_pairs={{0,4},{4,0},{1,5},{5,1},{2,6},{6,2},{3,7},{7,3},{8,12},{12,8},{9,1... | collective-permute-start | bytes 860168 | tf_op jit(solution)/shard_map/ppermute | solution.py:39
  77.9 1.7 copy-start
  79.6 1.1 copy-start.2
  80.7 1.1 copy-start.4
  91.4 26.4 %all-to-all-start.1 = ((f32[32,8,128]{2,1,0:T(8,128)}), f32[32,8,128]{2,1,0:T(8,128)S(1)}, u32[]{:S(2)}, u32[]{:S(2)}) async-start(f32[32,8,128]{2,1,0:T(8,128)} %get-tuple-element.47), calls=%async_computation.1 | async-start | bytes 262144 | tf_op jit(solution)/shard_map/all_to_all | solution.py:467
  99.2 10.1 %collective-permute-start.9 = (f32[160,384]{1,0:T(8,128)}, f32[160,384]{1,0:T(8,128)S(1)}, u32[]{:S(2)}, u32[]{:S(2)}) collective-permute-start(f32[160,384]{1,0:T(8,128)} %copy-done.11), channel_id=1, source_target_pairs={{0,1},{1,0},{2,3},{3,2},{4,5},{5,4},{6,7},{7,6},{8,9},{9,8},{10,11... | collective-permute-start | bytes 737288 | tf_op jit(solution)/shard_map/ppermute | solution.py:411
  101.1 14.7 %collective-permute-start.10 = (f32[160,384]{1,0:T(8,128)S(1)}, f32[160,384]{1,0:T(8,128)S(1)}, u32[]{:S(2)}, u32[]{:S(2)}) collective-permute-start(f32[160,384]{1,0:T(8,128)S(1)} %get-tuple-element.45), channel_id=1, source_target_pairs={{0,2},{1,3},{2,0},{3,1},{4,6},{5,7},{6,4},{7,5},{8,10},{9,11},{10,... | collective-permute-start | bytes 737288 | tf_op jit(solution)/shard_map/ppermute | solution.py:411
  103.8 14.1 %collective-permute-start.11 = (f32[160,384]{1,0:T(8,128)S(1)}, f32[160,384]{1,0:T(8,128)S(1)}, u32[]{:S(2)}, u32[]{:S(2)}) collective-permute-start(f32[160,384]{1,0:T(8,128)S(1)} %get-tuple-element.46), channel_id=1, source_target_pairs={{0,3},{1,2},{2,1},{3,0},{4,7},{5,6},{6,5},{7,4},{8,11},{9,10},{10,... | collective-permute-start | bytes 737288 | tf_op jit(solution)/shard_map/ppermute | solution.py:411
  118.8 18.7 %collective-permute-start.16 = (bf16[2,224,640]{2,1,0:T(8,128)(2,1)S(1)}, bf16[2,224,640]{2,1,0:T(8,128)(2,1)S(1)}, u32[]{:S(2)}, u32[]{:S(2)}) collective-permute-start(bf16[2,224,640]{2,1,0:T(8,128)(2,1)S(1)} %constant_dynamic-update-slice_fusion.c0), channel_id=1, source_target_pairs={{0,128},{128,0},{1,129},{129,1},{2,130},{130,2},{3,131},{131,3},{4... | collective-permute-start | bytes 1720328 | tf_op jit(solution)/shard_map/ppermute | solution.py:39
  119.0 18.5 %collective-permute-start.17 = (bf16[2,224,640]{2,1,0:T(8,128)(2,1)S(1)}, bf16[2,224,640]{2,1,0:T(8,128)(2,1)}, u32[]{:S(2)}, u32[]{:S(2)}) collective-permute-start(bf16[2,224,640]{2,1,0:T(8,128)(2,1)S(1)} %constant_dynamic-update-slice_fusion.c0), channel_id=1, source_target_pairs={{0,64},{64,0},{1,65},{65,1},{2,66},{66,2},{3,67},{67,3},{4,68},{68... | collective-permute-start | bytes 1720328 | tf_op jit(solution)/shard_map/ppermute | solution.py:39
  121.3 15.0 %collective-permute-start.13 = (bf16[640,128]{1,0:T(8,128)(2,1)S(1)}, bf16[640,128]{1,0:T(8,128)(2,1)S(1)}, u32[]{:S(2)}, u32[]{:S(2)}) collective-permute-start(bf16[640,128]{1,0:T(8,128)(2,1)S(1)} %own_rows.1.own), channel_id=1, source_target_pairs={{0,4},{4,0},{1,5},{5,1},{2,6},{6,2},{3,7},{7,3},{8,12},{12,8},{9,1... | collective-permute-start | bytes 491528 | tf_op jit(solution)/shard_map/ppermute | solution.py:39
  123.8 13.7 %collective-permute-start.14 = (bf16[640,128]{1,0:T(8,128)(2,1)S(1)}, bf16[640,128]{1,0:T(8,128)(2,1)S(1)}, u32[]{:S(2)}, u32[]{:S(2)}) collective-permute-start(bf16[640,128]{1,0:T(8,128)(2,1)S(1)} %own_rows.1.own), channel_id=1, source_target_pairs={{0,128},{1,129},{2,130},{3,131},{4,132},{5,133},{6,134},{7,135},{8... | collective-permute-start | bytes 491528 | tf_op jit(solution)/shard_map/ppermute | solution.py:474
  125.1 12.5 %collective-permute-start.15 = (bf16[640,128]{1,0:T(8,128)(2,1)S(1)}, bf16[640,128]{1,0:T(8,128)(2,1)S(1)}, u32[]{:S(2)}, u32[]{:S(2)}) collective-permute-start(bf16[640,128]{1,0:T(8,128)(2,1)S(1)} %own_rows.1.own), channel_id=1, source_target_pairs={{0,132},{4,128},{1,133},{5,129},{2,134},{6,130},{3,135},{7,131},{8... | collective-permute-start | bytes 491528 | tf_op jit(solution)/shard_map/ppermute | solution.py:475
  137.5 3.6 %collective-permute-start.18 = (bf16[2,224,640]{2,1,0:T(8,128)(2,1)S(1)}, bf16[2,224,640]{2,1,0:T(8,128)(2,1)}, u32[]{:S(2)}, u32[]{:S(2)}) collective-permute-start(bf16[2,224,640]{2,1,0:T(8,128)(2,1)S(1)} %collective-permute-done.16.c1), channel_id=1, source_target_pairs={{0,64},{64,0},{1,65},{65,1},{2,66},{66,2},{3,67},{67,3},{4,68},{68... | collective-permute-start | bytes 1720328 | tf_op jit(solution)/shard_map/ppermute | solution.py:39
  137.7 10.8 %collective-permute-start.19 = (bf16[2,640,128]{2,1,0:T(8,128)(2,1)S(1)}, bf16[2,640,128]{2,1,0:T(8,128)(2,1)}, u32[]{:S(2)}, u32[]{:S(2)}) collective-permute-start(bf16[2,640,128]{2,1,0:T(8,128)(2,1)S(1)} %maximum_select_fusion.spread), channel_id=1, source_target_pairs={{0,64},{128,192},{1,65},{129,193},{2,66},{130,194},{3,67},{131,195... | collective-permute-start | bytes 983048 | tf_op jit(solution)/shard_map/ppermute | solution.py:479
  141.1 0.9 copy-start.8
  148.5 25.6 %copy-start.6 = (bf16[8,5120]{1,0:T(8,128)(2,1)S(1)}, bf16[8,5120]{1,0:T(8,128)(2,1)}, u32[]{:S(2)}) copy-start(bf16[8,5120]{1,0:T(8,128)(2,1)} %copy-done.5) | copy-start | bytes 245764
  (6 other events, 4.6 us)

commit v3 on v2

--- a/solution.py
+++ b/solution.py
@@ -66,8 +66,7 @@
     rows = jnp.concatenate(
         [jnp.where(first, mine, other), jnp.where(first, other, mine)], axis=0
     ).astype(BF16)
-    for i in range(16):
-        out_ref[i] = rows
+    out_ref[...] = rows
 
 
 def modulate(numbers, place, mine, other, modulation):
@@ -81,128 +80,134 @@
                 pl.BlockSpec((TOK, WIDTH), lambda i, n, p: (0, 0)),
                 pl.BlockSpec((1, 3, WIDTH), lambda i, n, p: (n[0], 0, 0)),
             ],
-            out_specs=pl.BlockSpec((16, 2 * TOK, WIDTH), lambda i, n, p: (0, 0, 0)),
+            out_specs=pl.BlockSpec((2 * TOK, WIDTH), lambda i, n, p: (0, 0)),
         ),
-        out_shape=jax.ShapeDtypeStruct((16, 2 * TOK, WIDTH), BF16),
+        out_shape=jax.ShapeDtypeStruct((2 * TOK, WIDTH), BF16),
         compiler_params=params(16),
         name="modulate",
     )(numbers, place, mine, other, modulation)
 
 
 def project_kernel(
-    place_ref, x_ref, own_ref, t0_ref, t1_ref, t2_ref, t3_ref,
-    q_ref, kv_ref, sums_ref, m1_hbm, m2_hbm, m3_hbm, acc, m_ref, sem,
+    place_ref, x0_hbm, x1_hbm, x2_hbm, x3_hbm, own_hbm, t0_hbm, t1_hbm, t2_hbm, t3_hbm,
+    sums_hbm, m0_hbm, m1_hbm, m2_hbm, m3_hbm,
+    x_ref, own_ref, t_ref, acc, m_ref, sums_ref, x_sem, own_sem, t_sem, out_sem,
 ):
-    step = pl.program_id(0)
     half = place_ref[1]
     mine = pl.multiple_of(half * 3 * COLS, 16)
     theirs = pl.multiple_of((1 - half) * 3 * COLS, 16)
-    x = x_ref[...]
-
-    @pl.when(step == 0)
-    def _():
-        acc[...] = jnp.zeros_like(acc)
-
-    def add(weight, at):
-        acc[pl.ds(at, 3 * COLS), :] += lax.dot_general(
-            weight.reshape(3 * COLS, TILE), x, (((1,), (1,)), ((), ())), preferred_element_type=F32
+
+    x_copies = []
+    for j, x_hbm in enumerate((x0_hbm, x1_hbm, x2_hbm, x3_hbm)):
+        for i in range(4):
+            at = pl.multiple_of(64 * (place_ref[4] ^ j) + 16 * (place_ref[2] ^ i), 16)
+            x_copies.append(
+                pltpu.make_async_copy(
+                    x_hbm.at[pl.ds(16 * i, 16), :], x_ref.at[pl.ds(at, 16), :], x_sem.at[4 * j + i]
+                )
+            )
+    own_copies = [
+        pltpu.make_async_copy(own_hbm.at[i], own_ref.at[pl.ds(COLS * i, COLS), :], own_sem.at[i])
+        for i in range(3)
+    ]
+    t_copies = [
+        pltpu.make_async_copy(t_hbm, t_ref.at[j], t_sem.at[j])
+        for j, t_hbm in enumerate((t0_hbm, t1_hbm, t2_hbm, t3_hbm))
+    ]
+    for copy in x_copies + own_copies + t_copies:
+        copy.start()
+
+    def times(weight, x):
+        return lax.dot_general(weight, x, (((1,), (1,)), ((), ())), preferred_element_type=F32)
+
+    for copy in x_copies + own_copies:
+        copy.wait()
+    acc[pl.ds(mine, 3 * COLS), :] = times(own_ref[...], x_ref[...])
+    for copy in t_copies:
+        copy.wait()
+    for tile in range(4):
+        j = 2 * (place_ref[0] ^ (tile % 2)) + (place_ref[3] ^ (tile // 2))
+        part = times(t_ref[j].reshape(3 * COLS, TILE), x_ref[:, TILE * tile : TILE * tile + TILE])
+        if tile:
+            acc[pl.ds(theirs, 3 * COLS), :] += part
+        else:
+            acc[pl.ds(theirs, 3 * COLS), :] = part
+
+    q, k, v = [
+        jnp.concatenate(
+            [acc[(3 * e + i) * COLS : (3 * e + i + 1) * COLS, :] for e in range(2)], axis=0
         )
-
-    add(own_ref[...], mine)
-    for i, theirs_ref in enumerate((t0_ref, t1_ref, t2_ref, t3_ref)):
-
-        @pl.when(step == i)
-        def _(theirs_ref=theirs_ref):
-            add(theirs_ref[...], theirs)
-
-    @pl.when(step == 3)
-    def _():
-        q, k, v = [
-            jnp.concatenate(
-                [acc[(3 * e + i) * COLS : (3 * e + i + 1) * COLS, :] for e in range(2)], axis=0
-            )
-            for i in range(3)
-        ]
-        q_ref[...] = q
-        for i in range(3):
-            m_ref[i, :, 0:HALF_TOK] = q
-        lane = lax.broadcasted_iota(jnp.int32, (2 * COLS, 128), 1)
-        quarters = []
+        for i in range(3)
+    ]
+    for i in range(4):
+        m_ref[i, :, 0:HALF_TOK] = q
+    lane = lax.broadcasted_iota(jnp.int32, (2 * COLS, 128), 1)
+    quarters = []
+    for t in range(2):
+        kt = k[:, 128 * t : 128 * t + 128]
+        vt = v[:, 128 * t : 128 * t + 128]
+        quarters.append(jnp.where(lane < 64, kt, pltpu.roll(vt, 64, 1)))
+        quarters.append(jnp.where(lane < 64, pltpu.roll(kt, 64, 1), vt))
+    for here in range(4):
+
+        @pl.when(place_ref[2] == here)
+        def _(here=here):
+            for i in range(4):
+                m_ref[i, :, HALF_TOK : HALF_TOK + 128] = quarters[here ^ i]
+
+    sub = lax.broadcasted_iota(jnp.int32, (TOK, 128), 0)
+    tile = jnp.zeros((TOK, 128), F32)
+    for i, part in enumerate((q, k)):
+        total = jnp.sum(part * part, axis=0, keepdims=True)
         for t in range(2):
-            kt = k[:, 128 * t : 128 * t + 128]
-            vt = v[:, 128 * t : 128 * t + 128]
-            quarters.append(jnp.where(lane < 64, kt, pltpu.roll(vt, 64, 1)))
-            quarters.append(jnp.where(lane < 64, pltpu.roll(kt, 64, 1), vt))
-        for here in range(4):
-
-            @pl.when(place_ref[2] == here)
-            def _(here=here):
-                kv_ref[...] = quarters[here]
-                for i in range(3):
-                    m_ref[i, :, HALF_TOK : HALF_TOK + 128] = quarters[here ^ (i + 1)]
-
-        copies = [
-            pltpu.make_async_copy(m_ref.at[i], to, sem.at[i])
-            for i, to in enumerate((m1_hbm, m2_hbm, m3_hbm))
-        ]
-        for copy in copies:
-            copy.start()
-        sub = lax.broadcasted_iota(jnp.int32, (TOK, 128), 0)
-        tile = jnp.zeros((TOK, 128), F32)
-        for i, part in enumerate((q, k)):
-            total = jnp.sum(part * part, axis=0, keepdims=True)
-            for t in range(2):
-                tile = jnp.where(sub == 2 * i + t, total[:, 128 * t : 128 * t + 128], tile)
-        for i in range(32):
-            sums_ref[i] = tile
-        for copy in copies:
-            copy.wait()
+            tile = jnp.where(sub == 2 * i + t, total[:, 128 * t : 128 * t + 128], tile)
+    for i in range(32):
+        sums_ref[i] = tile
+    copies = [
+        pltpu.make_async_copy(m_ref.at[i], to, out_sem.at[i])
+        for i, to in enumerate((m0_hbm, m1_hbm, m2_hbm, m3_hbm))
+    ] + [pltpu.make_async_copy(sums_ref, sums_hbm, out_sem.at[4])]
+    for copy in copies:
+        copy.start()
+    for copy in copies:
+        copy.wait()
 
 
 def project(place, x, own, theirs):
-    def tile(j, place):
-        return 2 * ((j % 2 + place[3]) % 2) + (j // 2 + place[0]) % 2
-
-    piece = pl.BlockSpec((3, COLS, TILE), lambda j, p: (0, 0, 0))
-    whole = lambda *shape: pl.BlockSpec(shape, lambda j, p: (0,) * len(shape))
     both = (2 * COLS, HALF_TOK + 128)
-    outs = [(2 * COLS, HALF_TOK), (2 * COLS, 128), (32, TOK, 128)]
+    outs = [(32, TOK, 128), both, both, both, both]
+    hbm = pl.BlockSpec(memory_space=pltpu.HBM)
     return pl.pallas_call(
         project_kernel,
-        grid_spec=pltpu.PrefetchScalarGridSpec(
-            num_scalar_prefetch=1,
-            grid=(4,),
-            in_specs=[
-                pl.BlockSpec((HALF_TOK, TILE), lambda j, p: (0, tile(j, p))),
-                pl.BlockSpec((3, COLS, TILE), lambda j, p: (0, 0, tile(j, p))),
-                piece, piece, piece, piece,
-            ],
-            out_specs=[whole(*shape) for shape in outs] + [pl.BlockSpec(memory_space=pltpu.HBM)] * 3,
-            scratch_shapes=[
-                pltpu.VMEM((6 * COLS, HALF_TOK), F32),
-                pltpu.VMEM((3,) + both, F32),
-                pltpu.SemaphoreType.DMA((3,)),
-            ],
-        ),
-        out_shape=[jax.ShapeDtypeStruct(shape, F32) for shape in outs + [both] * 3],
-        compiler_params=params(24),
+        in_specs=[pl.BlockSpec(memory_space=pltpu.SMEM)] + [hbm] * 9,
+        out_specs=[hbm] * 5,
+        scratch_shapes=[
+            pltpu.VMEM((HALF_TOK, WIDTH), BF16),
+            pltpu.VMEM((3 * COLS, WIDTH), BF16),
+            pltpu.VMEM((4, 3, COLS, TILE), BF16),
+            pltpu.VMEM((6 * COLS, HALF_TOK), F32),
+            pltpu.VMEM((4,) + both, F32),
+            pltpu.VMEM((32, TOK, 128), F32),
+            pltpu.SemaphoreType.DMA((16,)),
+            pltpu.SemaphoreType.DMA((3,)),
+            pltpu.SemaphoreType.DMA((4,)),
+            pltpu.SemaphoreType.DMA((5,)),
+        ],
+        out_shape=[jax.ShapeDtypeStruct(shape, F32) for shape in outs],
+        compiler_params=params(60),
         name="project",
-    )(place, x, own, *theirs)
-
-
-def gather_rows(place_ref, mine, messages, columns, held, sem, rate, gain_ref, out_ref, lanes=None):
-    copies = [
-        pltpu.make_async_copy(m.at[:, columns], held.at[i], sem.at[i]) for i, m in enumerate(messages)
-    ]
+    )(place, *x, own, *theirs)
+
+
+def gather_rows(place_ref, pieces, held, sem, rate, gain_ref, out_ref, lanes=None):
+    copies = [pltpu.make_async_copy(p, held.at[i], sem.at[i]) for i, p in enumerate(pieces)]
     for copy in copies:
         copy.start()
-    for i in range(4):
-        if i:
-            copies[i - 1].wait()
+    for i, copy in enumerate(copies):
+        copy.wait()
         for e in range(2):
             at = pl.multiple_of((place_ref[2] ^ i) * COLS + e * (PART // 2), 16)
-            part = slice(COLS * e, COLS * e + COLS)
-            raw = held[i - 1, part, :] if i else mine[part, :]
+            raw = held[i, COLS * e : COLS * e + COLS, :]
             rows = raw * rate * gain_ref[pl.ds(at, COLS), :]
             if lanes is not None:
                 rows = jnp.where(lanes, rows, raw)
@@ -216,31 +221,29 @@
     return lax.rsqrt(picked[0] / WIDTH + EPS)
 
 
-def own_kernel(place_ref, kv0_ref, m1_hbm, m2_hbm, m3_hbm, sums_ref, gain_ref, out_ref, held, sem):
+def own_kernel(place_ref, m0_hbm, m1_hbm, m2_hbm, m3_hbm, sums_ref, gain_ref, out_ref, held, sem):
     rates = all_rates(sums_ref)
     rate = jnp.where(place_ref[2] < 2, rates[2:3, :], rates[3:4, :])
     rate = jnp.broadcast_to(rate, (TOK, 128))
     rate = jnp.where(place_ref[2] % 2 == 0, rate, pltpu.roll(rate, 64, 1))[0:1, :]
     lanes = lax.broadcasted_iota(jnp.int32, (COLS, 128), 1) < 64
-    gather_rows(
-        place_ref, kv0_ref, (m1_hbm, m2_hbm, m3_hbm), pl.ds(HALF_TOK, 128), held, sem,
-        rate, gain_ref, out_ref, lanes,
-    )
-
-
-def own_rows(place, kv, messages, sums, gain):
+    pieces = [m.at[:, pl.ds(HALF_TOK, 128)] for m in (m0_hbm, m1_hbm, m2_hbm, m3_hbm)]
+    gather_rows(place_ref, pieces, held, sem, rate, gain_ref, out_ref, lanes)
+
+
+def own_rows(place, messages, sums, gain):
     vmem = pl.BlockSpec(memory_space=pltpu.VMEM)
     return pl.pallas_call(
         own_kernel,
-        in_specs=[pl.BlockSpec(memory_space=pltpu.SMEM), vmem]
-        + [pl.BlockSpec(memory_space=pltpu.HBM)] * 3
+        in_specs=[pl.BlockSpec(memory_space=pltpu.SMEM)]
+        + [pl.BlockSpec(memory_space=pltpu.HBM)] * 4
         + [vmem, vmem],
         out_specs=vmem,
-        scratch_shapes=[pltpu.VMEM((3, 2 * COLS, 128), F32), pltpu.SemaphoreType.DMA((3,))],
+        scratch_shapes=[pltpu.VMEM((4, 2 * COLS, 128), F32), pltpu.SemaphoreType.DMA((4,))],
         out_shape=jax.ShapeDtypeStruct((PART, 128), BF16),
         compiler_params=params(8),
         name="own_rows",
-    )(place, kv, *messages, sums, gain)
+    )(place, *messages, sums, gain)
 
 
 def absorb(q, parts, top, den, num):
@@ -273,7 +276,7 @@
 
 
 def attend_kernel(
-    place_ref, q0, m1_hbm, m2_hbm, m3_hbm, sums_ref, gain_ref, c0, c1, c2, c3, own, bias_ref,
+    place_ref, m0_hbm, m1_hbm, m2_hbm, m3_hbm, sums_ref, gain_ref, c0, c1, c2, c3, own, bias_ref,
     query, stats, num_ref, held, sem,
 ):
     head = pl.program_id(0)
@@ -282,10 +285,8 @@
     def _():
         rates = all_rates(sums_ref)
         rate = jnp.concatenate([rates[0:1, :], rates[1:2, :]], axis=1)
-        gather_rows(
-            place_ref, q0, (m1_hbm, m2_hbm, m3_hbm), pl.ds(0, HALF_TOK), held, sem,
-            rate, gain_ref, query,
-        )
+        pieces = [m.at[:, pl.ds(0, HALF_TOK)] for m in (m0_hbm, m1_hbm, m2_hbm, m3_hbm)]
+        gather_rows(place_ref, pieces, held, sem, rate, gain_ref, query)
 
     q = query[pl.ds(pl.multiple_of(head * HEAD, HEAD), HEAD), :]
     parts = [(c[0], c[1], bias_ref[...]) for c in (c0, c1, c2, c3)] + [own[...]]
@@ -295,7 +296,7 @@
     stats[0, 1:2, :] = den
 
 
-def attend(place, query, messages, sums, gain, cached, own, bias):
+def attend(place, messages, sums, gain, cached, own, bias):
     cached_spec = pl.BlockSpec((2, CACHED // 4, HEAD), lambda h, p: (0, 0, h))
     whole = lambda *shape: pl.BlockSpec(shape, lambda h, p: (0,) * len(shape))
     return pl.pallas_call(
@@ -303,8 +304,7 @@
         grid_spec=pltpu.PrefetchScalarGridSpec(
             num_scalar_prefetch=1,
             grid=(PART_HEADS,),
-            in_specs=[whole(2 * COLS, HALF_TOK)]
-            + [pl.BlockSpec(memory_space=pltpu.HBM)] * 3
+            in_specs=[pl.BlockSpec(memory_space=pltpu.HBM)] * 4
             + [whole(32, TOK, 128), whole(PART, 1)]
             + [cached_spec] * 4
             + [pl.BlockSpec((HEAD, 128), lambda h, p: (h, 0)), whole(CACHED // 4, 1)],
@@ -313,7 +313,7 @@
                 pl.BlockSpec((1, 8, HALF_TOK), lambda h, p: (h, 0, 0)),
                 pl.BlockSpec((HEAD, HALF_TOK), lambda h, p: (h, 0)),
             ],
-            scratch_shapes=[pltpu.VMEM((3, 2 * COLS, HALF_TOK), F32), pltpu.SemaphoreType.DMA((3,))],
+            scratch_shapes=[pltpu.VMEM((4, 2 * COLS, HALF_TOK), F32), pltpu.SemaphoreType.DMA((4,))],
         ),
         out_shape=[
             jax.ShapeDtypeStruct((PART, HALF_TOK), BF16),
@@ -323,7 +323,7 @@
         compiler_params=params(14),
         cost_estimate=pl.CostEstimate(flops=700_000_000, bytes_accessed=5_000_000, transcendentals=1_300_000),
         name="attend",
-    )(place, query, *messages, sums, gain, *cached, own, bias)
+    )(place, *messages, sums, gain, *cached, own, bias)
 
 
 def close_kernel(place_ref, query, stats_ref, num_ref, near, spread, beside, out_ref, stats):
@@ -432,8 +432,9 @@
     w_sent, mine, other = lax.optimization_barrier((w_sent, mine, other))
     w0 = swapped(w_sent, "zh0")
     pair = modulate(numbers, place, mine, other, modulation)
-    tokens = lax.all_to_all(pair, ("y", "x"), 0, 0, tiled=True).reshape(HALF_TOK, WIDTH)
-    w0, cache_k, cache_v = lax.optimization_barrier((w0, cache_k, cache_v))
+    row = jnp.concatenate([pair] + [flipped(pair, "x", (4,), i) for i in (1, 2, 3)], axis=0)
+    tokens = [flipped(row, "y", (4,), i) for i in (1, 2, 3)]
+    w0, cache_k, cache_v, row = lax.optimization_barrier((w0, cache_k, cache_v, row))
     w1 = swapped(w0, "zl")
     w2 = swapped(w0, "core")
 
@@ -456,28 +457,31 @@
     q_cols = lax.dynamic_slice_in_dim(q_gain, group * PART, PART)[:, None]
     k_cols = lax.dynamic_slice_in_dim(k_gain, group * PART, PART)[:, None]
 
-    w1, c_same, c_flip, bias, q_cols, k_cols = lax.optimization_barrier(
-        (w1, c_same, c_flip, bias, q_cols, k_cols)
+    w1, tokens, c_same, c_flip, bias, q_cols, k_cols = lax.optimization_barrier(
+        (w1, tokens, c_same, c_flip, bias, q_cols, k_cols)
     )
     w3 = swapped(w1, "core")
     cached = jnp.concatenate([c_same, c_flip], axis=1)
     across = swapped(cached, "zh0")
-    query, kv, sums, m1, m2, m3 = project(place, tokens, w_qkv, (w0, w1, w2, w3))
-    messages = [flipped(m, "x", (4,), i) for i, m in ((1, m1), (2, m2), (3, m3))]
+    tokens = [row] + tokens
+
+    sums, m0, m1, m2, m3 = project(place, tokens, w_qkv, (w0, w1, w2, w3))
+    messages = [m0] + [flipped(m, "x", (4,), i) for i, m in ((1, m1), (2, m2), (3, m3))]
+    sums, across = lax.optimization_barrier((sums, across))
+    cached = jnp.concatenate([cached, across], axis=1)
     sums = lax.all_to_all(sums, ("y", "zh1", "x"), 0, 0, tiled=True)
-    messages, sums, across = lax.optimization_barrier((messages, sums, across))
-    cached = jnp.concatenate([cached, across], axis=1)
     beyond = swapped(cached, "zl")
     beside = swapped(cached, "core")
-    own = own_rows(place, kv, messages, sums, k_cols)
+    messages, sums, beyond, beside = lax.optimization_barrier((messages, sums, beyond, beside))
+    own = own_rows(place, messages, sums, k_cols)
     near = swapped(own, "zh0")
     low = lax.ppermute(own, SECTION, [(0, 2)])
     high = lax.ppermute(own, SECTION + ("zh0",), [(h, 2 * 2 + 1 - h) for h in range(2)])
-    near, low, high, beyond, beside = lax.optimization_barrier((near, low, high, beyond, beside))
     cached = [cached, beyond, beside, swapped(beyond, "core")]
+    query, stats, num = attend(place, messages, sums, q_cols, cached, own, bias)
+    near, low, high, num = lax.optimization_barrier((near, low, high, num))
     fresh = jnp.where(zl == 0, jnp.stack([own, near]), jnp.stack([low, high]))
     passed = lax.ppermute(fresh, SECTION, [(0, 1), (2, 3)])
-    query, stats, num = attend(place, query, messages, sums, q_cols, cached, own, bias)
     shares = close(place, query, stats, num, [near, fresh, passed])
     shares = shares.reshape(32, TOK, PART + 128)
     shares = lax.all_to_all(shares, ("y", "x", "zh1"), 0, 0, tiled=True)

time: 178 us -> 166 us (0.933)
  local copies, waits for them, and re-layouts: 18.1 us -> 6.99 us
  waiting for transfers between devices: 63 us -> 53.5 us
  blocking collectives: 23.5 us -> 28.5 us
  starting transfers between devices: 44.9 us -> 49.9 us
    ppermute x9, waiting for transfers between devices: 38.3 us -> 15.2 us  [swapped(): return lax.ppermute(value, axis, [(0, 1), (1, 0)])]
    unnamed x35 -> x23, local copies, waits for them, and re-layouts: 12.3 us -> 1.99 us
    ppermute x3 -> x9, starting transfers between devices: 4.79 us -> 13.8 us  [flipped(): return lax.ppermute(value, axes, [(i, i ^ by) for i in range(count)])]
    ppermute x3 -> x9, waiting for transfers between devices: 12 us -> 20.6 us  [flipped(): return lax.ppermute(value, axes, [(i, i ^ by) for i in range(count)])]
    all_to_all x1 -> x0, starting transfers between devices: 7.17 us -> none  [shards(): lax.all_to_all(pair, ('y', 'x'), 0, 0, tiled=True).reshape(HALF_TOK, WIDTH)]
    ppermute x9, starting transfers between devices: 7.39 us -> 13.4 us  [swapped(): return lax.ppermute(value, axis, [(0, 1), (1, 0)])]
    all_to_all x1, blocking collectives: 23.5 us -> 28.5 us  [shards(): shares = lax.all_to_all(shares, ('y', 'x', 'zh1'), 0, 0, tiled=True)]
    ppermute x1, waiting for transfers between devices: 7.98 us -> 12.4 us  [shards(): lax.ppermute(c_flip, four, [(spot(f ^ 2, y, z), spot(f, y ^ f, 1 - z)) fo...]
  transfers between devices with their start and end apart: 22 -> 27, of which waited for: 9 -> 12; matrix products, arithmetic and copies ran while one was open for 6% -> 6% of each run, Pallas kernels for 9% -> 10%
where the time goes in v3:
time: 166 us
  waiting for transfers between devices  53.5 us (32%)
  starting transfers between devices  49.9 us (30%)
  blocking collectives  28.5 us (17%)
  Pallas kernels  20.5 us (12%)
  local copies, waits for them, and re-layouts  6.99 us (4%)
  other arithmetic  4.62 us (3%)
    all_to_all x1, blocking collectives, shards(): shares = lax.all_to_all(shares, ('y', 'x', 'zh1'), 0, 0, tiled=True)  28.5 us
    ppermute x9, waiting for transfers between devices, flipped(): return lax.ppermute(value, axes, [(i, i ^ by) for i in range(count)])  20.6 us
    ppermute x9, waiting for transfers between devices, swapped(): return lax.ppermute(value, axis, [(0, 1), (1, 0)])  15.2 us
    ppermute x9, starting transfers between devices, flipped(): return lax.ppermute(value, axes, [(i, i ^ by) for i in range(count)])  13.8 us
    ppermute x9, starting transfers between devices, swapped(): return lax.ppermute(value, axis, [(0, 1), (1, 0)])  13.4 us
    ppermute x1, waiting for transfers between devices, shards(): lax.ppermute(c_flip, four, [(spot(f ^ 2, y, z), spot(f, y ^ f, 1 - z)) fo...  12.4 us
    pallas_call x1, Pallas kernels, project(): pl.pallas_call(project_kernel, in_specs=[pl.BlockSpec(memory_space=pltpu....  8.31 us
    ppermute x1, starting transfers between devices, shards(): lax.ppermute(hidden[0], SECTION + ('zh1',), [(2 * s + z, 2 * t + 1 - z) f...  7.01 us
  transfers between devices with their start and end apart: 27, of which 12 were waited for; matrix products, arithmetic and copies ran while one was open for 6% of the time, Pallas kernels for 10%

profile of v3, /device:TPU:32, one launch (start us, length us, event | category | flops | bytes accessed | tf_op | source)
XLA Modules:
  0.0 165.8 jit_solution(17916618674299320869)
XLA Ops:
  0.0 7.0 %collective-permute-start.2 = (bf16[8,5120]{1,0:T(8,128)(2,1)}, bf16[8,5120]{1,0:T(8,128)(2,1)S(1)}, u32[]{:S(2)}, u32[]{:S(2)}) collective-permute-start(bf16[8,5120]{1,0:T(8,128)(2,1)} %bitcast.22), channel_id=1, source_target_pairs={{0,72},{8,64},{64,136},{72,128},{128,200},{136,192},{192,8},{200,0... | collective-permute-start | bytes 245768 | tf_op jit(solution)/shard_map/ppermute | solution.py:426
  8.4 2.0 %constant_dynamic-slice_fusion = bf16[3,80,1280]{2,1,0:T(8,128)(2,1)} fusion(bf16[3,80,5120]{2,1,0:T(8,128)(2,1)} %own_hbm.1, s32[]{:T(128)S(6)} %select_n.32), kind=kLoop, calls=%fused_computation.14 | loop fusion | bytes 1228804 | tf_op jit(solution)/shard_map/dynamic_slice | solution.py:431
  12.3 3.0 %collective-permute-start.6 = (bf16[16,5120]{1,0:T(8,128)(2,1)S(1)}, bf16[16,5120]{1,0:T(8,128)(2,1)S(1)}, u32[]{:S(2)}, u32[]{:S(2)}) collective-permute-start(bf16[16,5120]{1,0:T(8,128)(2,1)S(1)} %modulate.1), channel_id=1, source_target_pairs={{0,3},{1,2},{2,1},{3,0},{4,7},{5,6},{6,5},{7,4},{8,11},{9,10},{10,... | collective-permute-start | bytes 491528 | tf_op jit(solution)/shard_map/ppermute | solution.py:411
  16.5 1.6 collective-permute-start.3
  18.1 5.2 %collective-permute-done.6 = bf16[16,5120]{1,0:T(8,128)(2,1)S(1)} collective-permute-done((bf16[16,5120]{1,0:T(8,128)(2,1)S(1)}, bf16[16,5120]{1,0:T(8,128)(2,1)S(1)}, u32[]{:S(2)}, u32[]{:S(2)}) %collective-permute-start.6) | collective-permute-done | bytes 163872 | tf_op jit(solution)/shard_map/ppermute | solution.py:411
  24.3 1.6 collective-permute-start.8
  25.9 2.9 %collective-permute-start.9 = (bf16[64,5120]{1,0:T(8,128)(2,1)S(1)}, bf16[64,5120]{1,0:T(8,128)(2,1)S(1)}, u32[]{:S(2)}, u32[]{:S(2)}) collective-permute-start(bf16[64,5120]{1,0:T(8,128)(2,1)S(1)} %pad_maximum_fusion.x0_hbm), channel_id=1, source_target_pairs={{0,32},{16,48},{32,0},{48,16},{1,33},{17,49},{33,1},{49,17},{2,34}... | collective-permute-start | bytes 1966088 | tf_op jit(solution)/shard_map/ppermute | solution.py:411
  29.1 15.2 %collective-permute-done.3.t0_hbm = bf16[3,80,1280]{2,1,0:T(8,128)(2,1)} collective-permute-done((bf16[3,80,1280]{2,1,0:T(8,128)(2,1)}, bf16[3,80,1280]{2,1,0:T(8,128)(2,1)}, u32[]{:S(2)}, u32[]{:S(2)}) %collective-permute-start.3) | collective-permute-done | bytes 614432 | tf_op jit(solution)/shard_map/ppermute | solution.py:39
  44.2 2.9 %collective-permute-start.7 = (bf16[3,80,1280]{2,1,0:T(8,128)(2,1)}, bf16[3,80,1280]{2,1,0:T(8,128)(2,1)}, u32[]{:S(2)}, u32[]{:S(2)}) collective-permute-start(bf16[3,80,1280]{2,1,0:T(8,128)(2,1)} %collective-permute-done.3.t0_hbm), channel_id=1, source_target_pairs={{0,128},{128,0},{1,129},{129,1},{2,130},{130,2},{3,131},{131,3},{4... | collective-permute-start | bytes 1843208 | tf_op jit(solution)/shard_map/ppermute | solution.py:39
  47.2 1.7 %fusion = (bf16[2,56,640]{2,1,0:T(8,128)(2,1)S(1)}, bf16[2,56,640]{2,1,0:T(8,128)(2,1)}) fusion(s32[]{:T(128)S(6)} %select_n.34, bf16[1,56,5120]{2,1,0:T(8,128)(2,1)} %bitcast.19, bf16[1,56,5120]{2,1,0:T(8,128)(2,1)} %bitcast.20, s32[]{:T(128)S(6)} %select_n.33), kind=kLoop, calls=%fused_computation.7 | loop fusion | flops 573440 | bytes 1433608 | tf_op jit(solution)/shard_map/stack | solution.py:441
  48.8 5.1 %collective-permute-start.11 = (bf16[2,56,640]{2,1,0:T(8,128)(2,1)}, bf16[2,56,640]{2,1,0:T(8,128)(2,1)S(1)}, u32[]{:S(2)}, u32[]{:S(2)}) collective-permute-start(bf16[2,56,640]{2,1,0:T(8,128)(2,1)} %get-tuple-element.80), channel_id=1, source_target_pairs={{0,0},{8,8},{16,16},{24,24},{32,32},{40,40},{48,48},{56,56},{64,80... | collective-permute-start | bytes 430088 | tf_op jit(solution)/shard_map/ppermute | solution.py:448
  56.2 2.2 %collective-permute-done.11 = bf16[2,56,640]{2,1,0:T(8,128)(2,1)S(1)} collective-permute-done((bf16[2,56,640]{2,1,0:T(8,128)(2,1)}, bf16[2,56,640]{2,1,0:T(8,128)(2,1)S(1)}, u32[]{:S(2)}, u32[]{:S(2)}) %collective-permute-start.11) | collective-permute-done | bytes 143392 | tf_op jit(solution)/shard_map/ppermute | solution.py:448
  59.2 12.4 %collective-permute-done.12 = bf16[2,56,640]{2,1,0:T(8,128)(2,1)} collective-permute-done((bf16[2,56,640]{2,1,0:T(8,128)(2,1)S(1)}, bf16[2,56,640]{2,1,0:T(8,128)(2,1)}, u32[]{:S(2)}, u32[]{:S(2)}) %collective-permute-start.12) | collective-permute-done | bytes 143392 | tf_op jit(solution)/shard_map/ppermute | solution.py:449
  71.6 1.8 %collective-permute-start.13 = (bf16[3,80,1280]{2,1,0:T(8,128)(2,1)}, bf16[3,80,1280]{2,1,0:T(8,128)(2,1)S(1)}, u32[]{:S(2)}, u32[]{:S(2)}) collective-permute-start(bf16[3,80,1280]{2,1,0:T(8,128)(2,1)} %collective-permute-done.3.t0_hbm), channel_id=1, source_target_pairs={{0,64},{64,0},{1,65},{65,1},{2,66},{66,2},{3,67},{67,3},{4,68},{68... | collective-permute-start | bytes 1843208 | tf_op jit(solution)/shard_map/ppermute | solution.py:39
  77.7 8.3 %project.1 = (f32[32,8,128]{2,1,0:T(8,128)}, f32[160,384]{1,0:T(8,128)}, f32[160,384]{1,0:T(8,128)}, f32[160,384]{1,0:T(8,128)}, f32[160,384]{1,0:T(8,128)}) custom-call(s32[6]{0:T(128)} %copy-done.1, bf16[64,5120]{1,0:T(8,128)(2,1)} %copy-done.3, bf16[64,5120]{1,0:T(8,128)(2,1)} %copy-done.4, bf16[64,5120]{1,0:T(8,128)(2,1)} %copy-done.5, ...), custom_call_target="tpu_custom_call" | custom-call | tf_op jit(solution)/shard_map/project/pallas_call | solution.py:180
  86.1 3.7 %collective-permute-start.19 = (bf16[2,224,640]{2,1,0:T(8,128)(2,1)S(1)}, bf16[2,224,640]{2,1,0:T(8,128)(2,1)S(1)}, u32[]{:S(2)}, u32[]{:S(2)}) collective-permute-start(bf16[2,224,640]{2,1,0:T(8,128)(2,1)S(1)} %constant_dynamic-update-slice_fusion.c0), channel_id=1, source_target_pairs={{0,128},{128,0},{1,129},{129,1},{2,130},{130,2},{3,131},{131,3},{4... | collective-permute-start | bytes 1720328 | tf_op jit(solution)/shard_map/ppermute | solution.py:39
  89.8 6.7 %all-to-all-start = ((f32[32,8,128]{2,1,0:T(8,128)}), f32[32,8,128]{2,1,0:T(8,128)S(1)}, u32[]{:S(2)}, u32[]{:S(2)}) async-start(f32[32,8,128]{2,1,0:T(8,128)} %get-tuple-element.60), calls=%async_computation | async-start | bytes 262144 | tf_op jit(solution)/shard_map/all_to_all | solution.py:472
  96.5 1.9 %collective-permute-start.15 = (f32[160,384]{1,0:T(8,128)}, f32[160,384]{1,0:T(8,128)S(1)}, u32[]{:S(2)}, u32[]{:S(2)}) collective-permute-start(f32[160,384]{1,0:T(8,128)} %get-tuple-element.54), channel_id=1, source_target_pairs={{0,1},{1,0},{2,3},{3,2},{4,5},{5,4},{6,7},{7,6},{8,9},{9,8},{10,11... | collective-permute-start | bytes 737288 | tf_op jit(solution)/shard_map/ppermute | solution.py:411
  98.4 2.7 %collective-permute-start.16 = (f32[160,384]{1,0:T(8,128)}, f32[160,384]{1,0:T(8,128)S(1)}, u32[]{:S(2)}, u32[]{:S(2)}) collective-permute-start(f32[160,384]{1,0:T(8,128)} %get-tuple-element.55), channel_id=1, source_target_pairs={{0,2},{1,3},{2,0},{3,1},{4,6},{5,7},{6,4},{7,5},{8,10},{9,11},{10,... | collective-permute-start | bytes 737288 | tf_op jit(solution)/shard_map/ppermute | solution.py:411
  101.3 5.0 %collective-permute-done.15.m1_hbm = f32[160,384]{1,0:T(8,128)S(1)} collective-permute-done((f32[160,384]{1,0:T(8,128)}, f32[160,384]{1,0:T(8,128)S(1)}, u32[]{:S(2)}, u32[]{:S(2)}) %collective-permute-start.15) | collective-permute-done | bytes 245792 | tf_op jit(solution)/shard_map/ppermute | solution.py:411
  106.3 6.8 %collective-permute-done.16.m2_hbm = f32[160,384]{1,0:T(8,128)S(1)} collective-permute-done((f32[160,384]{1,0:T(8,128)}, f32[160,384]{1,0:T(8,128)S(1)}, u32[]{:S(2)}, u32[]{:S(2)}) %collective-permute-start.16) | collective-permute-done | bytes 245792 | tf_op jit(solution)/shard_map/ppermute | solution.py:411
  113.1 2.6 %collective-permute-done.17.m3_hbm = f32[160,384]{1,0:T(8,128)S(1)} collective-permute-done((f32[160,384]{1,0:T(8,128)}, f32[160,384]{1,0:T(8,128)S(1)}, u32[]{:S(2)}, u32[]{:S(2)}) %collective-permute-start.17) | collective-permute-done | bytes 245792 | tf_op jit(solution)/shard_map/ppermute | solution.py:411
  117.1 2.1 %collective-permute-start.22 = (bf16[640,128]{1,0:T(8,128)(2,1)S(1)}, bf16[640,128]{1,0:T(8,128)(2,1)S(1)}, u32[]{:S(2)}, u32[]{:S(2)}) collective-permute-start(bf16[640,128]{1,0:T(8,128)(2,1)S(1)} %own_rows.1.own), channel_id=1, source_target_pairs={{0,4},{4,0},{1,5},{5,1},{2,6},{6,2},{3,7},{7,3},{8,12},{12,8},{9,1... | collective-permute-start | bytes 491528 | tf_op jit(solution)/shard_map/ppermute | solution.py:39
  119.2 1.3 collective-permute-start.23
  120.5 1.3 collective-permute-start.24
  122.1 6.5 %attend.1 = (bf16[640,256]{1,0:T(8,128)(2,1)S(1)}, f32[5,8,256]{2,1,0:T(8,128)S(1)}, f32[640,256]{1,0:T(8,128)S(1)}) custom-call(s32[6]{0:T(128)S(1)} %copy-done.2, f32[160,384]{1,0:T(8,128)S(1)} %copy-done, f32[160,384]{1,0:T(8,128)S(1)} %collective-permute-done.15.m1_hbm, f32[160,384]{1,0:T(8,128)S(1)} %collective-permute-done.16.m2_hbm, ...), custom_call_target="tpu_custom_call" | custom-call | flops 700000000 | bytes 5000000 | tf_op jit(solution)/shard_map/attend/pallas_call | solution.py:302
  128.6 1.3 collective-permute-done.24
  130.9 1.3 collective-permute-start.25
  132.2 1.2 collective-permute-done.25.beside
  133.5 1.5 close.1
  135.0 28.5 %all_to_all.10.in_ref = bf16[32,8,768]{2,1,0:T(8,128)(2,1)S(1)} all-to-all(bf16[32,8,768]{2,1,0:T(8,128)(2,1)S(1)} %bitcast.16), channel_id=1, replica_groups=mesh['zl'=2,'core'=2,'y'=4,'zh1'=2,'zh0'=2,'x'=4] {'y','x','zh1'}, dimensions={0} | all-to-all | bytes 786432 | tf_op jit(solution)/shard_map/all_to_all | solution.py:487
  163.5 2.2 %finish.1 = bf16[8,5120]{1,0:T(8,128)(2,1)} custom-call(s32[2]{0:T(128)S(1)} %collective-permute-done.numbers_ref.step_ref, bf16[32,8,768]{2,1,0:T(8,128)(2,1)S(1)} %all_to_all.10.in_ref, bf16[8,5120]{1,0:T(8,128)(2,1)S(1)} %collective-permute-done.1.mine_ref.hidden_ref, f32[4,3,5120]{2,1,0:T(4,128)S(1)} %copy.13.mod_ref), custom_call_target="tpu_custom_call" | custom-call | tf_op jit(solution)/shard_map/finish/pallas_call | solution.py:391
  (73 shorter events, 14.7 us)
Async XLA Ops:
  0.0 10.7 %collective-permute-start.1 = (bf16[8,5120]{1,0:T(8,128)(2,1)}, bf16[8,5120]{1,0:T(8,128)(2,1)S(1)}, u32[]{:S(2)}, u32[]{:S(2)}) collective-permute-start(bf16[8,5120]{1,0:T(8,128)(2,1)} %bitcast.21), channel_id=1, source_target_pairs={{0,64},{64,128},{128,192},{192,0},{1,65},{65,129},{129,193},{193,1... | collective-permute-start | bytes 245768 | tf_op jit(solution)/shard_map/ppermute | solution.py:425
  0.0 10.7 %collective-permute-start.2 = (bf16[8,5120]{1,0:T(8,128)(2,1)}, bf16[8,5120]{1,0:T(8,128)(2,1)S(1)}, u32[]{:S(2)}, u32[]{:S(2)}) collective-permute-start(bf16[8,5120]{1,0:T(8,128)(2,1)} %bitcast.22), channel_id=1, source_target_pairs={{0,72},{8,64},{64,136},{72,128},{128,200},{136,192},{192,8},{200,0... | collective-permute-start | bytes 245768 | tf_op jit(solution)/shard_map/ppermute | solution.py:426
  8.4 3.0 %collective-permute-start = (s32[2]{0:T(128)S(1)}, s32[2]{0:T(128)S(1)}, u32[]{:S(2)}, u32[]{:S(2)}) collective-permute-start(s32[2]{0:T(128)S(1)} %pad_add_fusion), channel_id=1, source_target_pairs={{0,64},{64,128},{128,192},{192,0},{1,65},{65,129},{129,193},{193,1... | collective-permute-start | bytes 32 | tf_op jit(solution)/shard_map/ppermute | solution.py:429
  10.7 38.2 %copy-start.1 = (s32[6]{0:T(128)}, s32[6]{0:T(128)S(1)}, u32[]{:S(2)}) copy-start(s32[6]{0:T(128)S(1)} %stack.54.place_ref) | copy-start | bytes 76
  12.3 46.0 %copy-start.9 = (s32[7]{0:T(128)S(1)}, s32[7]{0:T(128)}, u32[]{:S(2)}) copy-start(s32[7]{0:T(128)} %param.18) | copy-start | bytes 88
  12.3 11.0 %collective-permute-start.6 = (bf16[16,5120]{1,0:T(8,128)(2,1)S(1)}, bf16[16,5120]{1,0:T(8,128)(2,1)S(1)}, u32[]{:S(2)}, u32[]{:S(2)}) collective-permute-start(bf16[16,5120]{1,0:T(8,128)(2,1)S(1)} %modulate.1), channel_id=1, source_target_pairs={{0,3},{1,2},{2,1},{3,0},{4,7},{5,6},{6,5},{7,4},{8,11},{9,10},{10,... | collective-permute-start | bytes 491528 | tf_op jit(solution)/shard_map/ppermute | solution.py:411
  15.3 8.6 %collective-permute-start.5 = (bf16[16,5120]{1,0:T(8,128)(2,1)S(1)}, bf16[16,5120]{1,0:T(8,128)(2,1)S(1)}, u32[]{:S(2)}, u32[]{:S(2)}) collective-permute-start(bf16[16,5120]{1,0:T(8,128)(2,1)S(1)} %modulate.1), channel_id=1, source_target_pairs={{0,2},{1,3},{2,0},{3,1},{4,6},{5,7},{6,4},{7,5},{8,10},{9,11},{10,... | collective-permute-start | bytes 491528 | tf_op jit(solution)/shard_map/ppermute | solution.py:411
  16.1 8.1 %collective-permute-start.4 = (bf16[16,5120]{1,0:T(8,128)(2,1)S(1)}, bf16[16,5120]{1,0:T(8,128)(2,1)S(1)}, u32[]{:S(2)}, u32[]{:S(2)}) collective-permute-start(bf16[16,5120]{1,0:T(8,128)(2,1)S(1)} %modulate.1), channel_id=1, source_target_pairs={{0,1},{1,0},{2,3},{3,2},{4,5},{5,4},{6,7},{7,6},{8,9},{9,8},{10,11... | collective-permute-start | bytes 491528 | tf_op jit(solution)/shard_map/ppermute | solution.py:411
  16.5 27.7 %collective-permute-start.3 = (bf16[3,80,1280]{2,1,0:T(8,128)(2,1)}, bf16[3,80,1280]{2,1,0:T(8,128)(2,1)}, u32[]{:S(2)}, u32[]{:S(2)}) collective-permute-start(bf16[3,80,1280]{2,1,0:T(8,128)(2,1)} %constant_dynamic-slice_fusion), channel_id=1, source_target_pairs={{0,4},{4,0},{1,5},{5,1},{2,6},{6,2},{3,7},{7,3},{8,12},{12,8},{9,1... | collective-permute-start | bytes 1843208 | tf_op jit(solution)/shard_map/ppermute | solution.py:39
  24.3 52.6 %copy-start.3 = (bf16[64,5120]{1,0:T(8,128)(2,1)}, bf16[64,5120]{1,0:T(8,128)(2,1)S(1)}, u32[]{:S(2)}) copy-start(bf16[64,5120]{1,0:T(8,128)(2,1)S(1)} %pad_maximum_fusion.x0_hbm) | copy-start | bytes 1966084
  24.3 49.1 %collective-permute-start.8 = (bf16[64,5120]{1,0:T(8,128)(2,1)S(1)}, bf16[64,5120]{1,0:T(8,128)(2,1)S(1)}, u32[]{:S(2)}, u32[]{:S(2)}) collective-permute-start(bf16[64,5120]{1,0:T(8,128)(2,1)S(1)} %pad_maximum_fusion.x0_hbm), channel_id=1, source_target_pairs={{0,16},{16,0},{32,48},{48,32},{1,17},{17,1},{33,49},{49,33},{2,18}... | collective-permute-start | bytes 1966088 | tf_op jit(solution)/shard_map/ppermute | solution.py:411
  25.9 47.5 %collective-permute-start.9 = (bf16[64,5120]{1,0:T(8,128)(2,1)S(1)}, bf16[64,5120]{1,0:T(8,128)(2,1)S(1)}, u32[]{:S(2)}, u32[]{:S(2)}) collective-permute-start(bf16[64,5120]{1,0:T(8,128)(2,1)S(1)} %pad_maximum_fusion.x0_hbm), channel_id=1, source_target_pairs={{0,32},{16,48},{32,0},{48,16},{1,33},{17,49},{33,1},{49,17},{2,34}... | collective-permute-start | bytes 1966088 | tf_op jit(solution)/shard_map/ppermute | solution.py:411
  28.8 44.6 %collective-permute-start.10 = (bf16[64,5120]{1,0:T(8,128)(2,1)S(1)}, bf16[64,5120]{1,0:T(8,128)(2,1)S(1)}, u32[]{:S(2)}, u32[]{:S(2)}) collective-permute-start(bf16[64,5120]{1,0:T(8,128)(2,1)S(1)} %pad_maximum_fusion.x0_hbm), channel_id=1, source_target_pairs={{0,48},{16,32},{32,16},{48,0},{1,49},{17,33},{33,17},{49,1},{2,50}... | collective-permute-start | bytes 1966088 | tf_op jit(solution)/shard_map/ppermute | solution.py:411
  44.2 29.2 %collective-permute-start.7 = (bf16[3,80,1280]{2,1,0:T(8,128)(2,1)}, bf16[3,80,1280]{2,1,0:T(8,128)(2,1)}, u32[]{:S(2)}, u32[]{:S(2)}) collective-permute-start(bf16[3,80,1280]{2,1,0:T(8,128)(2,1)} %collective-permute-done.3.t0_hbm), channel_id=1, source_target_pairs={{0,128},{128,0},{1,129},{129,1},{2,130},{130,2},{3,131},{131,3},{4... | collective-permute-start | bytes 1843208 | tf_op jit(solution)/shard_map/ppermute | solution.py:39
  48.8 9.5 %collective-permute-start.11 = (bf16[2,56,640]{2,1,0:T(8,128)(2,1)}, bf16[2,56,640]{2,1,0:T(8,128)(2,1)S(1)}, u32[]{:S(2)}, u32[]{:S(2)}) collective-permute-start(bf16[2,56,640]{2,1,0:T(8,128)(2,1)} %get-tuple-element.80), channel_id=1, source_target_pairs={{0,0},{8,8},{16,16},{24,24},{32,32},{40,40},{48,48},{56,56},{64,80... | collective-permute-start | bytes 430088 | tf_op jit(solution)/shard_map/ppermute | solution.py:448
  58.3 13.3 %collective-permute-start.12 = (bf16[2,56,640]{2,1,0:T(8,128)(2,1)S(1)}, bf16[2,56,640]{2,1,0:T(8,128)(2,1)}, u32[]{:S(2)}, u32[]{:S(2)}) collective-permute-start(bf16[2,56,640]{2,1,0:T(8,128)(2,1)S(1)} %get-tuple-element.79), channel_id=1, source_target_pairs={{128,8},{136,0},{144,24},{152,16},{160,40},{168,32},{176,56},{184,... | collective-permute-start | bytes 430088 | tf_op jit(solution)/shard_map/ppermute | solution.py:449
  71.6 5.3 %collective-permute-start.13 = (bf16[3,80,1280]{2,1,0:T(8,128)(2,1)}, bf16[3,80,1280]{2,1,0:T(8,128)(2,1)S(1)}, u32[]{:S(2)}, u32[]{:S(2)}) collective-permute-start(bf16[3,80,1280]{2,1,0:T(8,128)(2,1)} %collective-permute-done.3.t0_hbm), channel_id=1, source_target_pairs={{0,64},{64,0},{1,65},{65,1},{2,66},{66,2},{3,67},{67,3},{4,68},{68... | collective-permute-start | bytes 1843208 | tf_op jit(solution)/shard_map/ppermute | solution.py:39
  73.5 4.2 %collective-permute-start.14 = (bf16[3,80,1280]{2,1,0:T(8,128)(2,1)}, bf16[3,80,1280]{2,1,0:T(8,128)(2,1)}, u32[]{:S(2)}, u32[]{:S(2)}) collective-permute-start(bf16[3,80,1280]{2,1,0:T(8,128)(2,1)} %collective-permute-done.7.t1_hbm), channel_id=1, source_target_pairs={{0,64},{64,0},{1,65},{65,1},{2,66},{66,2},{3,67},{67,3},{4,68},{68... | collective-permute-start | bytes 1843208 | tf_op jit(solution)/shard_map/ppermute | solution.py:39
  74.7 11.3 %collective-permute-start.18 = (bf16[2,112,640]{2,1,0:T(8,128)(2,1)S(1)}, bf16[2,112,640]{2,1,0:T(8,128)(2,1)S(1)}, u32[]{:S(2)}, u32[]{:S(2)}) collective-permute-start(bf16[2,112,640]{2,1,0:T(8,128)(2,1)S(1)} %pad_maximum_fusion.1), channel_id=1, source_target_pairs={{0,4},{4,0},{1,5},{5,1},{2,6},{6,2},{3,7},{7,3},{8,12},{12,8},{9,1... | collective-permute-start | bytes 860168 | tf_op jit(solution)/shard_map/ppermute | solution.py:39
  76.8 39.2 %copy-start.2 = (s32[6]{0:T(128)S(1)}, s32[6]{0:T(128)}, u32[]{:S(2)}) copy-start(s32[6]{0:T(128)} %copy-done.1) | copy-start | bytes 76
  86.0 30.0 %copy-start = (f32[160,384]{1,0:T(8,128)S(1)}, f32[160,384]{1,0:T(8,128)}, u32[]{:S(2)}) copy-start(f32[160,384]{1,0:T(8,128)} %get-tuple-element.62.m0_hbm) | copy-start | bytes 737284
  86.1 29.6 %collective-permute-start.19 = (bf16[2,224,640]{2,1,0:T(8,128)(2,1)S(1)}, bf16[2,224,640]{2,1,0:T(8,128)(2,1)S(1)}, u32[]{:S(2)}, u32[]{:S(2)}) collective-permute-start(bf16[2,224,640]{2,1,0:T(8,128)(2,1)S(1)} %constant_dynamic-update-slice_fusion.c0), channel_id=1, source_target_pairs={{0,128},{128,0},{1,129},{129,1},{2,130},{130,2},{3,131},{131,3},{4... | collective-permute-start | bytes 1720328 | tf_op jit(solution)/shard_map/ppermute | solution.py:39
  89.8 25.9 %collective-permute-start.20 = (bf16[2,224,640]{2,1,0:T(8,128)(2,1)S(1)}, bf16[2,224,640]{2,1,0:T(8,128)(2,1)}, u32[]{:S(2)}, u32[]{:S(2)}) collective-permute-start(bf16[2,224,640]{2,1,0:T(8,128)(2,1)S(1)} %constant_dynamic-update-slice_fusion.c0), channel_id=1, source_target_pairs={{0,64},{64,0},{1,65},{65,1},{2,66},{66,2},{3,67},{67,3},{4,68},{68... | collective-permute-start | bytes 1720328 | tf_op jit(solution)/shard_map/ppermute | solution.py:39
  89.8 25.9 %all-to-all-start = ((f32[32,8,128]{2,1,0:T(8,128)}), f32[32,8,128]{2,1,0:T(8,128)S(1)}, u32[]{:S(2)}, u32[]{:S(2)}) async-start(f32[32,8,128]{2,1,0:T(8,128)} %get-tuple-element.60), calls=%async_computation | async-start | bytes 262144 | tf_op jit(solution)/shard_map/all_to_all | solution.py:472
  96.5 9.8 %collective-permute-start.15 = (f32[160,384]{1,0:T(8,128)}, f32[160,384]{1,0:T(8,128)S(1)}, u32[]{:S(2)}, u32[]{:S(2)}) collective-permute-start(f32[160,384]{1,0:T(8,128)} %get-tuple-element.54), channel_id=1, source_target_pairs={{0,1},{1,0},{2,3},{3,2},{4,5},{5,4},{6,7},{7,6},{8,9},{9,8},{10,11... | collective-permute-start | bytes 737288 | tf_op jit(solution)/shard_map/ppermute | solution.py:411
  98.4 14.7 %collective-permute-start.16 = (f32[160,384]{1,0:T(8,128)}, f32[160,384]{1,0:T(8,128)S(1)}, u32[]{:S(2)}, u32[]{:S(2)}) collective-permute-start(f32[160,384]{1,0:T(8,128)} %get-tuple-element.55), channel_id=1, source_target_pairs={{0,2},{1,3},{2,0},{3,1},{4,6},{5,7},{6,4},{7,5},{8,10},{9,11},{10,... | collective-permute-start | bytes 737288 | tf_op jit(solution)/shard_map/ppermute | solution.py:411
  101.1 14.6 %collective-permute-start.17 = (f32[160,384]{1,0:T(8,128)}, f32[160,384]{1,0:T(8,128)S(1)}, u32[]{:S(2)}, u32[]{:S(2)}) collective-permute-start(f32[160,384]{1,0:T(8,128)} %get-tuple-element.56), channel_id=1, source_target_pairs={{0,3},{1,2},{2,1},{3,0},{4,7},{5,6},{6,5},{7,4},{8,11},{9,10},{10,... | collective-permute-start | bytes 737288 | tf_op jit(solution)/shard_map/ppermute | solution.py:411
  115.7 6.3 %collective-permute-start.21 = (bf16[2,224,640]{2,1,0:T(8,128)(2,1)S(1)}, bf16[2,224,640]{2,1,0:T(8,128)(2,1)}, u32[]{:S(2)}, u32[]{:S(2)}) collective-permute-start(bf16[2,224,640]{2,1,0:T(8,128)(2,1)S(1)} %collective-permute-done.19.c1), channel_id=1, source_target_pairs={{0,64},{64,0},{1,65},{65,1},{2,66},{66,2},{3,67},{67,3},{4,68},{68... | collective-permute-start | bytes 1720328 | tf_op jit(solution)/shard_map/ppermute | solution.py:39
  117.1 11.5 %collective-permute-start.22 = (bf16[640,128]{1,0:T(8,128)(2,1)S(1)}, bf16[640,128]{1,0:T(8,128)(2,1)S(1)}, u32[]{:S(2)}, u32[]{:S(2)}) collective-permute-start(bf16[640,128]{1,0:T(8,128)(2,1)S(1)} %own_rows.1.own), channel_id=1, source_target_pairs={{0,4},{4,0},{1,5},{5,1},{2,6},{6,2},{3,7},{7,3},{8,12},{12,8},{9,1... | collective-permute-start | bytes 491528 | tf_op jit(solution)/shard_map/ppermute | solution.py:39
  119.2 9.4 %collective-permute-start.23 = (bf16[640,128]{1,0:T(8,128)(2,1)S(1)}, bf16[640,128]{1,0:T(8,128)(2,1)}, u32[]{:S(2)}, u32[]{:S(2)}) collective-permute-start(bf16[640,128]{1,0:T(8,128)(2,1)S(1)} %own_rows.1.own), channel_id=1, source_target_pairs={{0,128},{1,129},{2,130},{3,131},{4,132},{5,133},{6,134},{7,135},{8... | collective-permute-start | bytes 491528 | tf_op jit(solution)/shard_map/ppermute | solution.py:478
  120.5 9.4 %collective-permute-start.24 = (bf16[640,128]{1,0:T(8,128)(2,1)S(1)}, bf16[640,128]{1,0:T(8,128)(2,1)}, u32[]{:S(2)}, u32[]{:S(2)}) collective-permute-start(bf16[640,128]{1,0:T(8,128)(2,1)S(1)} %own_rows.1.own), channel_id=1, source_target_pairs={{0,132},{4,128},{1,133},{5,129},{2,134},{6,130},{3,135},{7,131},{8... | collective-permute-start | bytes 491528 | tf_op jit(solution)/shard_map/ppermute | solution.py:479
  130.9 2.5 %collective-permute-start.25 = (bf16[2,640,128]{2,1,0:T(8,128)(2,1)S(1)}, bf16[2,640,128]{2,1,0:T(8,128)(2,1)S(1)}, u32[]{:S(2)}, u32[]{:S(2)}) collective-permute-start(bf16[2,640,128]{2,1,0:T(8,128)(2,1)S(1)} %maximum_select_fusion.spread), channel_id=1, source_target_pairs={{0,64},{128,192},{1,65},{129,193},{2,66},{130,194},{3,67},{131,195... | collective-permute-start | bytes 983048 | tf_op jit(solution)/shard_map/ppermute | solution.py:484
  (5 other events, 21.1 us)

commit v4 on v3

--- a/solution.py
+++ b/solution.py
@@ -279,48 +279,35 @@
     place_ref, m0_hbm, m1_hbm, m2_hbm, m3_hbm, sums_ref, gain_ref, c0, c1, c2, c3, own, bias_ref,
     query, stats, num_ref, held, sem,
 ):
-    head = pl.program_id(0)
-
-    @pl.when(head == 0)
-    def _():
-        rates = all_rates(sums_ref)
-        rate = jnp.concatenate([rates[0:1, :], rates[1:2, :]], axis=1)
-        pieces = [m.at[:, pl.ds(0, HALF_TOK)] for m in (m0_hbm, m1_hbm, m2_hbm, m3_hbm)]
-        gather_rows(place_ref, pieces, held, sem, rate, gain_ref, query)
-
-    q = query[pl.ds(pl.multiple_of(head * HEAD, HEAD), HEAD), :]
-    parts = [(c[0], c[1], bias_ref[...]) for c in (c0, c1, c2, c3)] + [own[...]]
-    top, den, num = absorb(q, parts, None, None, None)
-    num_ref[...] = num
-    stats[0, 0:1, :] = top
-    stats[0, 1:2, :] = den
+    rates = all_rates(sums_ref)
+    rate = jnp.concatenate([rates[0:1, :], rates[1:2, :]], axis=1)
+    pieces = [m.at[:, pl.ds(0, HALF_TOK)] for m in (m0_hbm, m1_hbm, m2_hbm, m3_hbm)]
+    gather_rows(place_ref, pieces, held, sem, rate, gain_ref, query)
+    bias = bias_ref[...]
+    for head in range(PART_HEADS):
+        cols = slice(HEAD * head, HEAD * head + HEAD)
+        parts = [(c[0, :, cols], c[1, :, cols], bias) for c in (c0, c1, c2, c3)] + [own[cols, :]]
+        top, den, num = absorb(query[cols, :], parts, None, None, None)
+        num_ref[cols, :] = num
+        stats[head, 0:1, :] = top
+        stats[head, 1:2, :] = den
 
 
 def attend(place, messages, sums, gain, cached, own, bias):
-    cached_spec = pl.BlockSpec((2, CACHED // 4, HEAD), lambda h, p: (0, 0, h))
-    whole = lambda *shape: pl.BlockSpec(shape, lambda h, p: (0,) * len(shape))
+    vmem = pl.BlockSpec(memory_space=pltpu.VMEM)
     return pl.pallas_call(
         attend_kernel,
-        grid_spec=pltpu.PrefetchScalarGridSpec(
-            num_scalar_prefetch=1,
-            grid=(PART_HEADS,),
-            in_specs=[pl.BlockSpec(memory_space=pltpu.HBM)] * 4
-            + [whole(32, TOK, 128), whole(PART, 1)]
-            + [cached_spec] * 4
-            + [pl.BlockSpec((HEAD, 128), lambda h, p: (h, 0)), whole(CACHED // 4, 1)],
-            out_specs=[
-                whole(PART, HALF_TOK),
-                pl.BlockSpec((1, 8, HALF_TOK), lambda h, p: (h, 0, 0)),
-                pl.BlockSpec((HEAD, HALF_TOK), lambda h, p: (h, 0)),
-            ],
-            scratch_shapes=[pltpu.VMEM((4, 2 * COLS, HALF_TOK), F32), pltpu.SemaphoreType.DMA((4,))],
-        ),
+        in_specs=[pl.BlockSpec(memory_space=pltpu.SMEM)]
+        + [pl.BlockSpec(memory_space=pltpu.HBM)] * 4
+        + [vmem] * 8,
+        out_specs=[vmem] * 3,
+        scratch_shapes=[pltpu.VMEM((4, 2 * COLS, HALF_TOK), F32), pltpu.SemaphoreType.DMA((4,))],
         out_shape=[
             jax.ShapeDtypeStruct((PART, HALF_TOK), BF16),
             jax.ShapeDtypeStruct((PART_HEADS, 8, HALF_TOK), F32),
             jax.ShapeDtypeStruct((PART, HALF_TOK), F32),
         ],
-        compiler_params=params(14),
+        compiler_params=params(20),
         cost_estimate=pl.CostEstimate(flops=700_000_000, bytes_accessed=5_000_000, transcendentals=1_300_000),
         name="attend",
     )(place, *messages, sums, gain, *cached, own, bias)
@@ -374,14 +361,14 @@
             dens.append(full[:, 8:16])
         top = jnp.maximum(jnp.maximum(tops[0], tops[1]), jnp.maximum(tops[2], tops[3]))
         shares = [jnp.exp((t - top) * (1.0 / math.sqrt(HEAD))) * d for t, d in zip(tops, dens)]
-        total = shares[0] + shares[1] + shares[2] + shares[3]
+        rest = 1.0 / (shares[0] + shares[1] + shares[2] + shares[3])
+        shares = [share * rest for share in shares]
         for n in range(PART_HEADS):
             cols = slice(HEAD * n, HEAD * n + HEAD)
             to = slice(PART * g + HEAD * n, PART * g + HEAD * n + HEAD)
             joined = jnp.zeros((TOK, HEAD), F32)
             for j in range(4):
                 joined = joined + in_ref[8 * (g // 2) + 2 * j + g % 2, :, cols].astype(F32) * shares[j][:, n : n + 1]
-            joined = joined / total[:, n : n + 1]
             out_ref[:, to] = (
                 hidden_ref[:, to].astype(F32) + mod_ref[0, 2:3, to] * joined
             ).astype(BF16)

time: 166 us -> 166 us (level)
  Pallas kernels: 20.5 us -> 18.4 us
  waiting for transfers between devices: 53.5 us -> 55.4 us
    pallas_call x1, Pallas kernels: 6.49 us -> 4.63 us  [attend(): pl.pallas_call(attend_kernel, in_specs=[pl.BlockSpec(memory_space=pltpu.S...]
    ppermute x9, waiting for transfers between devices: 15.2 us -> 17 us  [swapped(): return lax.ppermute(value, axis, [(0, 1), (1, 0)])]
  transfers between devices with their start and end apart: 27 -> 27, of which waited for: 12 -> 13; matrix products, arithmetic and copies ran while one was open for 6% -> 6% of each run, Pallas kernels for 10% -> 8%
where the time goes in v4:
time: 166 us; the launch traced here: 165 us
  waiting for transfers between devices  55.4 us (33%)
  starting transfers between devices  49.9 us (30%)
  blocking collectives  28.5 us (17%)
  Pallas kernels  18.4 us (11%)
  local copies, waits for them, and re-layouts  6.99 us (4%)
  other arithmetic  4.62 us (3%)
    all_to_all x1, blocking collectives, shards(): shares = lax.all_to_all(shares, ('y', 'x', 'zh1'), 0, 0, tiled=True)  28.5 us
    ppermute x9, waiting for transfers between devices, flipped(): return lax.ppermute(value, axes, [(i, i ^ by) for i in range(count)])  20.6 us
    ppermute x9, waiting for transfers between devices, swapped(): return lax.ppermute(value, axis, [(0, 1), (1, 0)])  17 us
    ppermute x9, starting transfers between devices, flipped(): return lax.ppermute(value, axes, [(i, i ^ by) for i in range(count)])  13.8 us
    ppermute x9, starting transfers between devices, swapped(): return lax.ppermute(value, axis, [(0, 1), (1, 0)])  13.4 us
    ppermute x1, waiting for transfers between devices, shards(): lax.ppermute(c_flip, four, [(spot(f ^ 2, y, z), spot(f, y ^ f, 1 - z)) fo...  12.4 us
    pallas_call x1, Pallas kernels, project(): pl.pallas_call(project_kernel, in_specs=[pl.BlockSpec(memory_space=pltpu....  8.31 us
    ppermute x1, starting transfers between devices, shards(): lax.ppermute(hidden[0], SECTION + ('zh1',), [(2 * s + z, 2 * t + 1 - z) f...  7.01 us
  transfers between devices with their start and end apart: 27, of which 13 were waited for; matrix products, arithmetic and copies ran while one was open for 6% of the time, Pallas kernels for 8%

profile of v4, /device:TPU:32, one launch (start us, length us, event | category | flops | bytes accessed | tf_op | source)
XLA Modules:
  0.0 165.5 jit_solution(2757561066476057130)
XLA Ops:
  0.0 7.0 %collective-permute-start.2 = (bf16[8,5120]{1,0:T(8,128)(2,1)}, bf16[8,5120]{1,0:T(8,128)(2,1)S(1)}, u32[]{:S(2)}, u32[]{:S(2)}) collective-permute-start(bf16[8,5120]{1,0:T(8,128)(2,1)} %bitcast.22), channel_id=1, source_target_pairs={{0,72},{8,64},{64,136},{72,128},{128,200},{136,192},{192,8},{200,0... | collective-permute-start | bytes 245768 | tf_op jit(solution)/shard_map/ppermute | solution.py:413
  8.4 2.0 %constant_dynamic-slice_fusion = bf16[3,80,1280]{2,1,0:T(8,128)(2,1)} fusion(bf16[3,80,5120]{2,1,0:T(8,128)(2,1)} %own_hbm.1, s32[]{:T(128)S(6)} %select_n.32), kind=kLoop, calls=%fused_computation.14 | loop fusion | bytes 1228804 | tf_op jit(solution)/shard_map/dynamic_slice | solution.py:418
  12.3 3.0 %collective-permute-start.6 = (bf16[16,5120]{1,0:T(8,128)(2,1)S(1)}, bf16[16,5120]{1,0:T(8,128)(2,1)S(1)}, u32[]{:S(2)}, u32[]{:S(2)}) collective-permute-start(bf16[16,5120]{1,0:T(8,128)(2,1)S(1)} %modulate.1), channel_id=1, source_target_pairs={{0,3},{1,2},{2,1},{3,0},{4,7},{5,6},{6,5},{7,4},{8,11},{9,10},{10,... | collective-permute-start | bytes 491528 | tf_op jit(solution)/shard_map/ppermute | solution.py:398
  16.5 1.6 collective-permute-start.3
  18.1 5.2 %collective-permute-done.6 = bf16[16,5120]{1,0:T(8,128)(2,1)S(1)} collective-permute-done((bf16[16,5120]{1,0:T(8,128)(2,1)S(1)}, bf16[16,5120]{1,0:T(8,128)(2,1)S(1)}, u32[]{:S(2)}, u32[]{:S(2)}) %collective-permute-start.6) | collective-permute-done | bytes 163872 | tf_op jit(solution)/shard_map/ppermute | solution.py:398
  24.3 1.6 collective-permute-start.8
  25.9 2.9 %collective-permute-start.9 = (bf16[64,5120]{1,0:T(8,128)(2,1)S(1)}, bf16[64,5120]{1,0:T(8,128)(2,1)S(1)}, u32[]{:S(2)}, u32[]{:S(2)}) collective-permute-start(bf16[64,5120]{1,0:T(8,128)(2,1)S(1)} %pad_maximum_fusion.x0_hbm), channel_id=1, source_target_pairs={{0,32},{16,48},{32,0},{48,16},{1,33},{17,49},{33,1},{49,17},{2,34}... | collective-permute-start | bytes 1966088 | tf_op jit(solution)/shard_map/ppermute | solution.py:398
  29.1 15.2 %collective-permute-done.3.t0_hbm = bf16[3,80,1280]{2,1,0:T(8,128)(2,1)} collective-permute-done((bf16[3,80,1280]{2,1,0:T(8,128)(2,1)}, bf16[3,80,1280]{2,1,0:T(8,128)(2,1)}, u32[]{:S(2)}, u32[]{:S(2)}) %collective-permute-start.3) | collective-permute-done | bytes 614432 | tf_op jit(solution)/shard_map/ppermute | solution.py:39
  44.2 2.9 %collective-permute-start.7 = (bf16[3,80,1280]{2,1,0:T(8,128)(2,1)}, bf16[3,80,1280]{2,1,0:T(8,128)(2,1)}, u32[]{:S(2)}, u32[]{:S(2)}) collective-permute-start(bf16[3,80,1280]{2,1,0:T(8,128)(2,1)} %collective-permute-done.3.t0_hbm), channel_id=1, source_target_pairs={{0,128},{128,0},{1,129},{129,1},{2,130},{130,2},{3,131},{131,3},{4... | collective-permute-start | bytes 1843208 | tf_op jit(solution)/shard_map/ppermute | solution.py:39
  47.2 1.7 %fusion = (bf16[2,56,640]{2,1,0:T(8,128)(2,1)S(1)}, bf16[2,56,640]{2,1,0:T(8,128)(2,1)}) fusion(s32[]{:T(128)S(6)} %select_n.34, bf16[1,56,5120]{2,1,0:T(8,128)(2,1)} %bitcast.19, bf16[1,56,5120]{2,1,0:T(8,128)(2,1)} %bitcast.20, s32[]{:T(128)S(6)} %select_n.33), kind=kLoop, calls=%fused_computation.7 | loop fusion | flops 573440 | bytes 1433608 | tf_op jit(solution)/shard_map/stack | solution.py:428
  48.8 5.1 %collective-permute-start.11 = (bf16[2,56,640]{2,1,0:T(8,128)(2,1)}, bf16[2,56,640]{2,1,0:T(8,128)(2,1)S(1)}, u32[]{:S(2)}, u32[]{:S(2)}) collective-permute-start(bf16[2,56,640]{2,1,0:T(8,128)(2,1)} %get-tuple-element.80), channel_id=1, source_target_pairs={{0,0},{8,8},{16,16},{24,24},{32,32},{40,40},{48,48},{56,56},{64,80... | collective-permute-start | bytes 430088 | tf_op jit(solution)/shard_map/ppermute | solution.py:435
  56.2 2.2 %collective-permute-done.11 = bf16[2,56,640]{2,1,0:T(8,128)(2,1)S(1)} collective-permute-done((bf16[2,56,640]{2,1,0:T(8,128)(2,1)}, bf16[2,56,640]{2,1,0:T(8,128)(2,1)S(1)}, u32[]{:S(2)}, u32[]{:S(2)}) %collective-permute-start.11) | collective-permute-done | bytes 143392 | tf_op jit(solution)/shard_map/ppermute | solution.py:435
  59.2 12.4 %collective-permute-done.12 = bf16[2,56,640]{2,1,0:T(8,128)(2,1)} collective-permute-done((bf16[2,56,640]{2,1,0:T(8,128)(2,1)S(1)}, bf16[2,56,640]{2,1,0:T(8,128)(2,1)}, u32[]{:S(2)}, u32[]{:S(2)}) %collective-permute-start.12) | collective-permute-done | bytes 143392 | tf_op jit(solution)/shard_map/ppermute | solution.py:436
  71.6 1.8 %collective-permute-start.13 = (bf16[3,80,1280]{2,1,0:T(8,128)(2,1)}, bf16[3,80,1280]{2,1,0:T(8,128)(2,1)S(1)}, u32[]{:S(2)}, u32[]{:S(2)}) collective-permute-start(bf16[3,80,1280]{2,1,0:T(8,128)(2,1)} %collective-permute-done.3.t0_hbm), channel_id=1, source_target_pairs={{0,64},{64,0},{1,65},{65,1},{2,66},{66,2},{3,67},{67,3},{4,68},{68... | collective-permute-start | bytes 1843208 | tf_op jit(solution)/shard_map/ppermute | solution.py:39
  77.7 8.3 %project.1 = (f32[32,8,128]{2,1,0:T(8,128)}, f32[160,384]{1,0:T(8,128)}, f32[160,384]{1,0:T(8,128)}, f32[160,384]{1,0:T(8,128)}, f32[160,384]{1,0:T(8,128)}) custom-call(s32[6]{0:T(128)} %copy-done.1, bf16[64,5120]{1,0:T(8,128)(2,1)} %copy-done.3, bf16[64,5120]{1,0:T(8,128)(2,1)} %copy-done.4, bf16[64,5120]{1,0:T(8,128)(2,1)} %copy-done.5, ...), custom_call_target="tpu_custom_call" | custom-call | tf_op jit(solution)/shard_map/project/pallas_call | solution.py:180
  86.1 3.7 %collective-permute-start.19 = (bf16[2,224,640]{2,1,0:T(8,128)(2,1)S(1)}, bf16[2,224,640]{2,1,0:T(8,128)(2,1)S(1)}, u32[]{:S(2)}, u32[]{:S(2)}) collective-permute-start(bf16[2,224,640]{2,1,0:T(8,128)(2,1)S(1)} %constant_dynamic-update-slice_fusion.c0), channel_id=1, source_target_pairs={{0,128},{128,0},{1,129},{129,1},{2,130},{130,2},{3,131},{131,3},{4... | collective-permute-start | bytes 1720328 | tf_op jit(solution)/shard_map/ppermute | solution.py:39
  89.8 6.7 %all-to-all-start = ((f32[32,8,128]{2,1,0:T(8,128)}), f32[32,8,128]{2,1,0:T(8,128)S(1)}, u32[]{:S(2)}, u32[]{:S(2)}) async-start(f32[32,8,128]{2,1,0:T(8,128)} %get-tuple-element.60), calls=%async_computation | async-start | bytes 262144 | tf_op jit(solution)/shard_map/all_to_all | solution.py:459
  96.5 1.9 %collective-permute-start.15 = (f32[160,384]{1,0:T(8,128)}, f32[160,384]{1,0:T(8,128)S(1)}, u32[]{:S(2)}, u32[]{:S(2)}) collective-permute-start(f32[160,384]{1,0:T(8,128)} %get-tuple-element.54), channel_id=1, source_target_pairs={{0,1},{1,0},{2,3},{3,2},{4,5},{5,4},{6,7},{7,6},{8,9},{9,8},{10,11... | collective-permute-start | bytes 737288 | tf_op jit(solution)/shard_map/ppermute | solution.py:398
  98.4 2.7 %collective-permute-start.16 = (f32[160,384]{1,0:T(8,128)}, f32[160,384]{1,0:T(8,128)S(1)}, u32[]{:S(2)}, u32[]{:S(2)}) collective-permute-start(f32[160,384]{1,0:T(8,128)} %get-tuple-element.55), channel_id=1, source_target_pairs={{0,2},{1,3},{2,0},{3,1},{4,6},{5,7},{6,4},{7,5},{8,10},{9,11},{10,... | collective-permute-start | bytes 737288 | tf_op jit(solution)/shard_map/ppermute | solution.py:398
  101.3 5.0 %collective-permute-done.15.m1_hbm = f32[160,384]{1,0:T(8,128)S(1)} collective-permute-done((f32[160,384]{1,0:T(8,128)}, f32[160,384]{1,0:T(8,128)S(1)}, u32[]{:S(2)}, u32[]{:S(2)}) %collective-permute-start.15) | collective-permute-done | bytes 245792 | tf_op jit(solution)/shard_map/ppermute | solution.py:398
  106.3 6.8 %collective-permute-done.16.m2_hbm = f32[160,384]{1,0:T(8,128)S(1)} collective-permute-done((f32[160,384]{1,0:T(8,128)}, f32[160,384]{1,0:T(8,128)S(1)}, u32[]{:S(2)}, u32[]{:S(2)}) %collective-permute-start.16) | collective-permute-done | bytes 245792 | tf_op jit(solution)/shard_map/ppermute | solution.py:398
  113.1 2.6 %collective-permute-done.17.m3_hbm = f32[160,384]{1,0:T(8,128)S(1)} collective-permute-done((f32[160,384]{1,0:T(8,128)}, f32[160,384]{1,0:T(8,128)S(1)}, u32[]{:S(2)}, u32[]{:S(2)}) %collective-permute-start.17) | collective-permute-done | bytes 245792 | tf_op jit(solution)/shard_map/ppermute | solution.py:398
  117.1 2.1 %collective-permute-start.22 = (bf16[640,128]{1,0:T(8,128)(2,1)S(1)}, bf16[640,128]{1,0:T(8,128)(2,1)S(1)}, u32[]{:S(2)}, u32[]{:S(2)}) collective-permute-start(bf16[640,128]{1,0:T(8,128)(2,1)S(1)} %own_rows.1.own), channel_id=1, source_target_pairs={{0,4},{4,0},{1,5},{5,1},{2,6},{6,2},{3,7},{7,3},{8,12},{12,8},{9,1... | collective-permute-start | bytes 491528 | tf_op jit(solution)/shard_map/ppermute | solution.py:39
  119.2 1.3 collective-permute-start.23
  120.5 1.3 collective-permute-start.24
  122.1 4.6 %attend.1 = (bf16[640,256]{1,0:T(8,128)(2,1)S(1)}, f32[5,8,256]{2,1,0:T(8,128)S(1)}, f32[640,256]{1,0:T(8,128)S(1)}) custom-call(s32[6]{0:T(128)S(1)} %copy-done.2, f32[160,384]{1,0:T(8,128)S(1)} %copy-done, f32[160,384]{1,0:T(8,128)S(1)} %collective-permute-done.15.m1_hbm, f32[160,384]{1,0:T(8,128)S(1)} %collective-permute-done.16.m2_hbm, ...), custom_call_target="tpu_custom_call" | custom-call | flops 700000000 | bytes 5000000 | tf_op jit(solution)/shard_map/attend/pallas_call | solution.py:298
  126.7 1.9 %collective-permute-done.22.near = bf16[640,128]{1,0:T(8,128)(2,1)S(1)} collective-permute-done((bf16[640,128]{1,0:T(8,128)(2,1)S(1)}, bf16[640,128]{1,0:T(8,128)(2,1)S(1)}, u32[]{:S(2)}, u32[]{:S(2)}) %collective-permute-start.22) | collective-permute-done | bytes 163872 | tf_op jit(solution)/shard_map/ppermute | solution.py:39
  128.6 1.3 collective-permute-done.24
  130.9 1.3 collective-permute-start.25
  133.5 1.5 close.1
  135.0 28.5 %all_to_all.10.in_ref = bf16[32,8,768]{2,1,0:T(8,128)(2,1)S(1)} all-to-all(bf16[32,8,768]{2,1,0:T(8,128)(2,1)S(1)} %bitcast.16), channel_id=1, replica_groups=mesh['zl'=2,'core'=2,'y'=4,'zh1'=2,'zh0'=2,'x'=4] {'y','x','zh1'}, dimensions={0} | all-to-all | bytes 786432 | tf_op jit(solution)/shard_map/all_to_all | solution.py:474
  163.5 2.0 %finish.1 = bf16[8,5120]{1,0:T(8,128)(2,1)} custom-call(s32[2]{0:T(128)S(1)} %collective-permute-done.numbers_ref.step_ref, bf16[32,8,768]{2,1,0:T(8,128)(2,1)S(1)} %all_to_all.10.in_ref, bf16[8,5120]{1,0:T(8,128)(2,1)S(1)} %collective-permute-done.1.mine_ref.hidden_ref, f32[4,3,5120]{2,1,0:T(4,128)S(1)} %copy.13.mod_ref), custom_call_target="tpu_custom_call" | custom-call | tf_op jit(solution)/shard_map/finish/pallas_call | solution.py:378
  (73 shorter events, 15.9 us)
Async XLA Ops:
  0.0 10.7 %collective-permute-start.1 = (bf16[8,5120]{1,0:T(8,128)(2,1)}, bf16[8,5120]{1,0:T(8,128)(2,1)S(1)}, u32[]{:S(2)}, u32[]{:S(2)}) collective-permute-start(bf16[8,5120]{1,0:T(8,128)(2,1)} %bitcast.21), channel_id=1, source_target_pairs={{0,64},{64,128},{128,192},{192,0},{1,65},{65,129},{129,193},{193,1... | collective-permute-start | bytes 245768 | tf_op jit(solution)/shard_map/ppermute | solution.py:412
  0.0 10.7 %collective-permute-start.2 = (bf16[8,5120]{1,0:T(8,128)(2,1)}, bf16[8,5120]{1,0:T(8,128)(2,1)S(1)}, u32[]{:S(2)}, u32[]{:S(2)}) collective-permute-start(bf16[8,5120]{1,0:T(8,128)(2,1)} %bitcast.22), channel_id=1, source_target_pairs={{0,72},{8,64},{64,136},{72,128},{128,200},{136,192},{192,8},{200,0... | collective-permute-start | bytes 245768 | tf_op jit(solution)/shard_map/ppermute | solution.py:413
  8.4 3.0 %collective-permute-start = (s32[2]{0:T(128)S(1)}, s32[2]{0:T(128)S(1)}, u32[]{:S(2)}, u32[]{:S(2)}) collective-permute-start(s32[2]{0:T(128)S(1)} %pad_add_fusion), channel_id=1, source_target_pairs={{0,64},{64,128},{128,192},{192,0},{1,65},{65,129},{129,193},{193,1... | collective-permute-start | bytes 32 | tf_op jit(solution)/shard_map/ppermute | solution.py:416
  10.7 38.2 %copy-start.1 = (s32[6]{0:T(128)}, s32[6]{0:T(128)S(1)}, u32[]{:S(2)}) copy-start(s32[6]{0:T(128)S(1)} %stack.54.place_ref) | copy-start | bytes 76
  12.3 46.0 %copy-start.9 = (s32[7]{0:T(128)S(1)}, s32[7]{0:T(128)}, u32[]{:S(2)}) copy-start(s32[7]{0:T(128)} %param.18) | copy-start | bytes 88
  12.3 11.0 %collective-permute-start.6 = (bf16[16,5120]{1,0:T(8,128)(2,1)S(1)}, bf16[16,5120]{1,0:T(8,128)(2,1)S(1)}, u32[]{:S(2)}, u32[]{:S(2)}) collective-permute-start(bf16[16,5120]{1,0:T(8,128)(2,1)S(1)} %modulate.1), channel_id=1, source_target_pairs={{0,3},{1,2},{2,1},{3,0},{4,7},{5,6},{6,5},{7,4},{8,11},{9,10},{10,... | collective-permute-start | bytes 491528 | tf_op jit(solution)/shard_map/ppermute | solution.py:398
  15.3 8.6 %collective-permute-start.5 = (bf16[16,5120]{1,0:T(8,128)(2,1)S(1)}, bf16[16,5120]{1,0:T(8,128)(2,1)S(1)}, u32[]{:S(2)}, u32[]{:S(2)}) collective-permute-start(bf16[16,5120]{1,0:T(8,128)(2,1)S(1)} %modulate.1), channel_id=1, source_target_pairs={{0,2},{1,3},{2,0},{3,1},{4,6},{5,7},{6,4},{7,5},{8,10},{9,11},{10,... | collective-permute-start | bytes 491528 | tf_op jit(solution)/shard_map/ppermute | solution.py:398
  16.1 8.1 %collective-permute-start.4 = (bf16[16,5120]{1,0:T(8,128)(2,1)S(1)}, bf16[16,5120]{1,0:T(8,128)(2,1)S(1)}, u32[]{:S(2)}, u32[]{:S(2)}) collective-permute-start(bf16[16,5120]{1,0:T(8,128)(2,1)S(1)} %modulate.1), channel_id=1, source_target_pairs={{0,1},{1,0},{2,3},{3,2},{4,5},{5,4},{6,7},{7,6},{8,9},{9,8},{10,11... | collective-permute-start | bytes 491528 | tf_op jit(solution)/shard_map/ppermute | solution.py:398
  16.5 27.7 %collective-permute-start.3 = (bf16[3,80,1280]{2,1,0:T(8,128)(2,1)}, bf16[3,80,1280]{2,1,0:T(8,128)(2,1)}, u32[]{:S(2)}, u32[]{:S(2)}) collective-permute-start(bf16[3,80,1280]{2,1,0:T(8,128)(2,1)} %constant_dynamic-slice_fusion), channel_id=1, source_target_pairs={{0,4},{4,0},{1,5},{5,1},{2,6},{6,2},{3,7},{7,3},{8,12},{12,8},{9,1... | collective-permute-start | bytes 1843208 | tf_op jit(solution)/shard_map/ppermute | solution.py:39
  24.3 52.6 %copy-start.3 = (bf16[64,5120]{1,0:T(8,128)(2,1)}, bf16[64,5120]{1,0:T(8,128)(2,1)S(1)}, u32[]{:S(2)}) copy-start(bf16[64,5120]{1,0:T(8,128)(2,1)S(1)} %pad_maximum_fusion.x0_hbm) | copy-start | bytes 1966084
  24.3 49.1 %collective-permute-start.8 = (bf16[64,5120]{1,0:T(8,128)(2,1)S(1)}, bf16[64,5120]{1,0:T(8,128)(2,1)S(1)}, u32[]{:S(2)}, u32[]{:S(2)}) collective-permute-start(bf16[64,5120]{1,0:T(8,128)(2,1)S(1)} %pad_maximum_fusion.x0_hbm), channel_id=1, source_target_pairs={{0,16},{16,0},{32,48},{48,32},{1,17},{17,1},{33,49},{49,33},{2,18}... | collective-permute-start | bytes 1966088 | tf_op jit(solution)/shard_map/ppermute | solution.py:398
  25.9 47.5 %collective-permute-start.9 = (bf16[64,5120]{1,0:T(8,128)(2,1)S(1)}, bf16[64,5120]{1,0:T(8,128)(2,1)S(1)}, u32[]{:S(2)}, u32[]{:S(2)}) collective-permute-start(bf16[64,5120]{1,0:T(8,128)(2,1)S(1)} %pad_maximum_fusion.x0_hbm), channel_id=1, source_target_pairs={{0,32},{16,48},{32,0},{48,16},{1,33},{17,49},{33,1},{49,17},{2,34}... | collective-permute-start | bytes 1966088 | tf_op jit(solution)/shard_map/ppermute | solution.py:398
  28.8 44.6 %collective-permute-start.10 = (bf16[64,5120]{1,0:T(8,128)(2,1)S(1)}, bf16[64,5120]{1,0:T(8,128)(2,1)S(1)}, u32[]{:S(2)}, u32[]{:S(2)}) collective-permute-start(bf16[64,5120]{1,0:T(8,128)(2,1)S(1)} %pad_maximum_fusion.x0_hbm), channel_id=1, source_target_pairs={{0,48},{16,32},{32,16},{48,0},{1,49},{17,33},{33,17},{49,1},{2,50}... | collective-permute-start | bytes 1966088 | tf_op jit(solution)/shard_map/ppermute | solution.py:398
  44.2 29.2 %collective-permute-start.7 = (bf16[3,80,1280]{2,1,0:T(8,128)(2,1)}, bf16[3,80,1280]{2,1,0:T(8,128)(2,1)}, u32[]{:S(2)}, u32[]{:S(2)}) collective-permute-start(bf16[3,80,1280]{2,1,0:T(8,128)(2,1)} %collective-permute-done.3.t0_hbm), channel_id=1, source_target_pairs={{0,128},{128,0},{1,129},{129,1},{2,130},{130,2},{3,131},{131,3},{4... | collective-permute-start | bytes 1843208 | tf_op jit(solution)/shard_map/ppermute | solution.py:39
  48.8 9.5 %collective-permute-start.11 = (bf16[2,56,640]{2,1,0:T(8,128)(2,1)}, bf16[2,56,640]{2,1,0:T(8,128)(2,1)S(1)}, u32[]{:S(2)}, u32[]{:S(2)}) collective-permute-start(bf16[2,56,640]{2,1,0:T(8,128)(2,1)} %get-tuple-element.80), channel_id=1, source_target_pairs={{0,0},{8,8},{16,16},{24,24},{32,32},{40,40},{48,48},{56,56},{64,80... | collective-permute-start | bytes 430088 | tf_op jit(solution)/shard_map/ppermute | solution.py:435
  58.3 13.3 %collective-permute-start.12 = (bf16[2,56,640]{2,1,0:T(8,128)(2,1)S(1)}, bf16[2,56,640]{2,1,0:T(8,128)(2,1)}, u32[]{:S(2)}, u32[]{:S(2)}) collective-permute-start(bf16[2,56,640]{2,1,0:T(8,128)(2,1)S(1)} %get-tuple-element.79), channel_id=1, source_target_pairs={{128,8},{136,0},{144,24},{152,16},{160,40},{168,32},{176,56},{184,... | collective-permute-start | bytes 430088 | tf_op jit(solution)/shard_map/ppermute | solution.py:436
  71.6 5.3 %collective-permute-start.13 = (bf16[3,80,1280]{2,1,0:T(8,128)(2,1)}, bf16[3,80,1280]{2,1,0:T(8,128)(2,1)S(1)}, u32[]{:S(2)}, u32[]{:S(2)}) collective-permute-start(bf16[3,80,1280]{2,1,0:T(8,128)(2,1)} %collective-permute-done.3.t0_hbm), channel_id=1, source_target_pairs={{0,64},{64,0},{1,65},{65,1},{2,66},{66,2},{3,67},{67,3},{4,68},{68... | collective-permute-start | bytes 1843208 | tf_op jit(solution)/shard_map/ppermute | solution.py:39
  73.5 4.2 %collective-permute-start.14 = (bf16[3,80,1280]{2,1,0:T(8,128)(2,1)}, bf16[3,80,1280]{2,1,0:T(8,128)(2,1)}, u32[]{:S(2)}, u32[]{:S(2)}) collective-permute-start(bf16[3,80,1280]{2,1,0:T(8,128)(2,1)} %collective-permute-done.7.t1_hbm), channel_id=1, source_target_pairs={{0,64},{64,0},{1,65},{65,1},{2,66},{66,2},{3,67},{67,3},{4,68},{68... | collective-permute-start | bytes 1843208 | tf_op jit(solution)/shard_map/ppermute | solution.py:39
  74.7 11.3 %collective-permute-start.18 = (bf16[2,112,640]{2,1,0:T(8,128)(2,1)S(1)}, bf16[2,112,640]{2,1,0:T(8,128)(2,1)S(1)}, u32[]{:S(2)}, u32[]{:S(2)}) collective-permute-start(bf16[2,112,640]{2,1,0:T(8,128)(2,1)S(1)} %pad_maximum_fusion.1), channel_id=1, source_target_pairs={{0,4},{4,0},{1,5},{5,1},{2,6},{6,2},{3,7},{7,3},{8,12},{12,8},{9,1... | collective-permute-start | bytes 860168 | tf_op jit(solution)/shard_map/ppermute | solution.py:39
  76.8 39.2 %copy-start.2 = (s32[6]{0:T(128)S(1)}, s32[6]{0:T(128)}, u32[]{:S(2)}) copy-start(s32[6]{0:T(128)} %copy-done.1) | copy-start | bytes 76
  86.0 30.0 %copy-start = (f32[160,384]{1,0:T(8,128)S(1)}, f32[160,384]{1,0:T(8,128)}, u32[]{:S(2)}) copy-start(f32[160,384]{1,0:T(8,128)} %get-tuple-element.62.m0_hbm) | copy-start | bytes 737284
  86.1 29.6 %collective-permute-start.19 = (bf16[2,224,640]{2,1,0:T(8,128)(2,1)S(1)}, bf16[2,224,640]{2,1,0:T(8,128)(2,1)S(1)}, u32[]{:S(2)}, u32[]{:S(2)}) collective-permute-start(bf16[2,224,640]{2,1,0:T(8,128)(2,1)S(1)} %constant_dynamic-update-slice_fusion.c0), channel_id=1, source_target_pairs={{0,128},{128,0},{1,129},{129,1},{2,130},{130,2},{3,131},{131,3},{4... | collective-permute-start | bytes 1720328 | tf_op jit(solution)/shard_map/ppermute | solution.py:39
  89.8 25.9 %collective-permute-start.20 = (bf16[2,224,640]{2,1,0:T(8,128)(2,1)S(1)}, bf16[2,224,640]{2,1,0:T(8,128)(2,1)}, u32[]{:S(2)}, u32[]{:S(2)}) collective-permute-start(bf16[2,224,640]{2,1,0:T(8,128)(2,1)S(1)} %constant_dynamic-update-slice_fusion.c0), channel_id=1, source_target_pairs={{0,64},{64,0},{1,65},{65,1},{2,66},{66,2},{3,67},{67,3},{4,68},{68... | collective-permute-start | bytes 1720328 | tf_op jit(solution)/shard_map/ppermute | solution.py:39
  89.8 25.9 %all-to-all-start = ((f32[32,8,128]{2,1,0:T(8,128)}), f32[32,8,128]{2,1,0:T(8,128)S(1)}, u32[]{:S(2)}, u32[]{:S(2)}) async-start(f32[32,8,128]{2,1,0:T(8,128)} %get-tuple-element.60), calls=%async_computation | async-start | bytes 262144 | tf_op jit(solution)/shard_map/all_to_all | solution.py:459
  96.5 9.8 %collective-permute-start.15 = (f32[160,384]{1,0:T(8,128)}, f32[160,384]{1,0:T(8,128)S(1)}, u32[]{:S(2)}, u32[]{:S(2)}) collective-permute-start(f32[160,384]{1,0:T(8,128)} %get-tuple-element.54), channel_id=1, source_target_pairs={{0,1},{1,0},{2,3},{3,2},{4,5},{5,4},{6,7},{7,6},{8,9},{9,8},{10,11... | collective-permute-start | bytes 737288 | tf_op jit(solution)/shard_map/ppermute | solution.py:398
  98.4 14.7 %collective-permute-start.16 = (f32[160,384]{1,0:T(8,128)}, f32[160,384]{1,0:T(8,128)S(1)}, u32[]{:S(2)}, u32[]{:S(2)}) collective-permute-start(f32[160,384]{1,0:T(8,128)} %get-tuple-element.55), channel_id=1, source_target_pairs={{0,2},{1,3},{2,0},{3,1},{4,6},{5,7},{6,4},{7,5},{8,10},{9,11},{10,... | collective-permute-start | bytes 737288 | tf_op jit(solution)/shard_map/ppermute | solution.py:398
  101.1 14.6 %collective-permute-start.17 = (f32[160,384]{1,0:T(8,128)}, f32[160,384]{1,0:T(8,128)S(1)}, u32[]{:S(2)}, u32[]{:S(2)}) collective-permute-start(f32[160,384]{1,0:T(8,128)} %get-tuple-element.56), channel_id=1, source_target_pairs={{0,3},{1,2},{2,1},{3,0},{4,7},{5,6},{6,5},{7,4},{8,11},{9,10},{10,... | collective-permute-start | bytes 737288 | tf_op jit(solution)/shard_map/ppermute | solution.py:398
  115.7 6.3 %collective-permute-start.21 = (bf16[2,224,640]{2,1,0:T(8,128)(2,1)S(1)}, bf16[2,224,640]{2,1,0:T(8,128)(2,1)}, u32[]{:S(2)}, u32[]{:S(2)}) collective-permute-start(bf16[2,224,640]{2,1,0:T(8,128)(2,1)S(1)} %collective-permute-done.19.c1), channel_id=1, source_target_pairs={{0,64},{64,0},{1,65},{65,1},{2,66},{66,2},{3,67},{67,3},{4,68},{68... | collective-permute-start | bytes 1720328 | tf_op jit(solution)/shard_map/ppermute | solution.py:39
  117.1 11.5 %collective-permute-start.22 = (bf16[640,128]{1,0:T(8,128)(2,1)S(1)}, bf16[640,128]{1,0:T(8,128)(2,1)S(1)}, u32[]{:S(2)}, u32[]{:S(2)}) collective-permute-start(bf16[640,128]{1,0:T(8,128)(2,1)S(1)} %own_rows.1.own), channel_id=1, source_target_pairs={{0,4},{4,0},{1,5},{5,1},{2,6},{6,2},{3,7},{7,3},{8,12},{12,8},{9,1... | collective-permute-start | bytes 491528 | tf_op jit(solution)/shard_map/ppermute | solution.py:39
  119.2 9.4 %collective-permute-start.23 = (bf16[640,128]{1,0:T(8,128)(2,1)S(1)}, bf16[640,128]{1,0:T(8,128)(2,1)}, u32[]{:S(2)}, u32[]{:S(2)}) collective-permute-start(bf16[640,128]{1,0:T(8,128)(2,1)S(1)} %own_rows.1.own), channel_id=1, source_target_pairs={{0,128},{1,129},{2,130},{3,131},{4,132},{5,133},{6,134},{7,135},{8... | collective-permute-start | bytes 491528 | tf_op jit(solution)/shard_map/ppermute | solution.py:465
  120.5 9.4 %collective-permute-start.24 = (bf16[640,128]{1,0:T(8,128)(2,1)S(1)}, bf16[640,128]{1,0:T(8,128)(2,1)}, u32[]{:S(2)}, u32[]{:S(2)}) collective-permute-start(bf16[640,128]{1,0:T(8,128)(2,1)S(1)} %own_rows.1.own), channel_id=1, source_target_pairs={{0,132},{4,128},{1,133},{5,129},{2,134},{6,130},{3,135},{7,131},{8... | collective-permute-start | bytes 491528 | tf_op jit(solution)/shard_map/ppermute | solution.py:466
  130.9 2.5 %collective-permute-start.25 = (bf16[2,640,128]{2,1,0:T(8,128)(2,1)S(1)}, bf16[2,640,128]{2,1,0:T(8,128)(2,1)S(1)}, u32[]{:S(2)}, u32[]{:S(2)}) collective-permute-start(bf16[2,640,128]{2,1,0:T(8,128)(2,1)S(1)} %maximum_select_fusion.spread), channel_id=1, source_target_pairs={{0,64},{128,192},{1,65},{129,193},{2,66},{130,194},{3,67},{131,195... | collective-permute-start | bytes 983048 | tf_op jit(solution)/shard_map/ppermute | solution.py:471
  (5 other events, 21.1 us)

commit v5 on v4

--- a/solution.py
+++ b/solution.py
@@ -444,10 +444,9 @@
     q_cols = lax.dynamic_slice_in_dim(q_gain, group * PART, PART)[:, None]
     k_cols = lax.dynamic_slice_in_dim(k_gain, group * PART, PART)[:, None]
 
-    w1, tokens, c_same, c_flip, bias, q_cols, k_cols = lax.optimization_barrier(
-        (w1, tokens, c_same, c_flip, bias, q_cols, k_cols)
-    )
+    w1, tokens, c_same = lax.optimization_barrier((w1, tokens, c_same))
     w3 = swapped(w1, "core")
+    w3, c_flip, bias, q_cols, k_cols = lax.optimization_barrier((w3, c_flip, bias, q_cols, k_cols))
     cached = jnp.concatenate([c_same, c_flip], axis=1)
     across = swapped(cached, "zh0")
     tokens = [row] + tokens

time: 166 us -> 173 us (1.042)
  waiting for transfers between devices: 55.4 us -> 61.3 us
  starting transfers between devices: 49.9 us -> 53.7 us
  blocking collectives: 28.5 us -> 26.7 us
    all_to_all x1, starting transfers between devices: 6.74 us -> 12 us  [shards(): sums = lax.all_to_all(sums, ('y', 'zh1', 'x'), 0, 0, tiled=True)]
    ppermute x9, starting transfers between devices: 13.4 us -> 8.76 us  [swapped(): return lax.ppermute(value, axis, [(0, 1), (1, 0)])]
    ppermute x9, waiting for transfers between devices: 20.6 us -> 24.7 us  [flipped(): return lax.ppermute(value, axes, [(i, i ^ by) for i in range(count)])]
    ppermute x1, waiting for transfers between devices: 12.4 us -> 9 us  [shards(): lax.ppermute(c_flip, four, [(spot(f ^ 2, y, z), spot(f, y ^ f, 1 - z)) fo...]
    ppermute x1, starting transfers between devices: 0.01 us -> 3.1 us  [shards(): lax.ppermute(c_flip, four, [(spot(f ^ 2, y, z), spot(f, y ^ f, 1 - z)) fo...]
    ppermute x1, waiting for transfers between devices: 2.17 us -> 4.39 us  [shards(): lax.ppermute(c_same, four, [(spot(f, y, z), spot(f, y ^ f, z)) for f, y,...]
    all_to_all x1, blocking collectives: 28.5 us -> 26.7 us  [shards(): shares = lax.all_to_all(shares, ('y', 'x', 'zh1'), 0, 0, tiled=True)]
  transfers between devices with their start and end apart: 27 -> 27, of which waited for: 13 -> 16; matrix products, arithmetic and copies ran while one was open for 6% -> 4% of each run, Pallas kernels for 8% -> 8%
where the time goes in v5:
time: 173 us; the launch traced here: 171 us
  waiting for transfers between devices  61.3 us (35%)
  starting transfers between devices  53.7 us (31%)
  blocking collectives  26.7 us (15%)
  Pallas kernels  18.5 us (11%)
  local copies, waits for them, and re-layouts  5.83 us (3%)
  other arithmetic  3.53 us (2%)
    all_to_all x1, blocking collectives, shards(): shares = lax.all_to_all(shares, ('y', 'x', 'zh1'), 0, 0, tiled=True)  26.7 us
    ppermute x9, waiting for transfers between devices, flipped(): return lax.ppermute(value, axes, [(i, i ^ by) for i in range(count)])  24.7 us
    ppermute x9, waiting for transfers between devices, swapped(): return lax.ppermute(value, axis, [(0, 1), (1, 0)])  17.7 us
    ppermute x9, starting transfers between devices, flipped(): return lax.ppermute(value, axes, [(i, i ^ by) for i in range(count)])  13.8 us
    all_to_all x1, starting transfers between devices, shards(): sums = lax.all_to_all(sums, ('y', 'zh1', 'x'), 0, 0, tiled=True)  12 us
    ppermute x1, waiting for transfers between devices, shards(): lax.ppermute(c_flip, four, [(spot(f ^ 2, y, z), spot(f, y ^ f, 1 - z)) fo...  9 us
    ppermute x9, starting transfers between devices, swapped(): return lax.ppermute(value, axis, [(0, 1), (1, 0)])  8.76 us
    pallas_call x1, Pallas kernels, project(): pl.pallas_call(project_kernel, in_specs=[pl.BlockSpec(memory_space=pltpu....  8.42 us
  transfers between devices with their start and end apart: 27, of which 16 were waited for; matrix products, arithmetic and copies ran while one was open for 4% of the time, Pallas kernels for 8%

profile of v5, /device:TPU:32, one launch (start us, length us, event | category | flops | bytes accessed | tf_op | source)
XLA Modules:
  0.0 171.2 jit_solution(11799719921447494401)
XLA Ops:
  0.0 7.0 %collective-permute-start.2 = (bf16[8,5120]{1,0:T(8,128)(2,1)}, bf16[8,5120]{1,0:T(8,128)(2,1)S(1)}, u32[]{:S(2)}, u32[]{:S(2)}) collective-permute-start(bf16[8,5120]{1,0:T(8,128)(2,1)} %bitcast.22), channel_id=1, source_target_pairs={{0,72},{8,64},{64,136},{72,128},{128,200},{136,192},{192,8},{200,0... | collective-permute-start | bytes 245768 | tf_op jit(solution)/shard_map/ppermute | solution.py:413
  8.4 2.0 %constant_dynamic-slice_fusion = bf16[3,80,1280]{2,1,0:T(8,128)(2,1)} fusion(bf16[3,80,5120]{2,1,0:T(8,128)(2,1)} %own_hbm.1, s32[]{:T(128)S(6)} %select_n.32), kind=kLoop, calls=%fused_computation.14 | loop fusion | bytes 1228804 | tf_op jit(solution)/shard_map/dynamic_slice | solution.py:418
  12.3 3.0 %collective-permute-start.6 = (bf16[16,5120]{1,0:T(8,128)(2,1)S(1)}, bf16[16,5120]{1,0:T(8,128)(2,1)S(1)}, u32[]{:S(2)}, u32[]{:S(2)}) collective-permute-start(bf16[16,5120]{1,0:T(8,128)(2,1)S(1)} %modulate.1), channel_id=1, source_target_pairs={{0,3},{1,2},{2,1},{3,0},{4,7},{5,6},{6,5},{7,4},{8,11},{9,10},{10,... | collective-permute-start | bytes 491528 | tf_op jit(solution)/shard_map/ppermute | solution.py:398
  16.5 1.6 collective-permute-start.3
  18.1 5.3 %collective-permute-done.6 = bf16[16,5120]{1,0:T(8,128)(2,1)S(1)} collective-permute-done((bf16[16,5120]{1,0:T(8,128)(2,1)S(1)}, bf16[16,5120]{1,0:T(8,128)(2,1)S(1)}, u32[]{:S(2)}, u32[]{:S(2)}) %collective-permute-start.6) | collective-permute-done | bytes 163872 | tf_op jit(solution)/shard_map/ppermute | solution.py:398
  24.3 1.6 collective-permute-start.8
  25.9 2.9 %collective-permute-start.9 = (bf16[64,5120]{1,0:T(8,128)(2,1)S(1)}, bf16[64,5120]{1,0:T(8,128)(2,1)S(1)}, u32[]{:S(2)}, u32[]{:S(2)}) collective-permute-start(bf16[64,5120]{1,0:T(8,128)(2,1)S(1)} %pad_maximum_fusion.x0_hbm), channel_id=1, source_target_pairs={{0,32},{16,48},{32,0},{48,16},{1,33},{17,49},{33,1},{49,17},{2,34}... | collective-permute-start | bytes 1966088 | tf_op jit(solution)/shard_map/ppermute | solution.py:398
  29.1 15.2 %collective-permute-done.3.t0_hbm = bf16[3,80,1280]{2,1,0:T(8,128)(2,1)} collective-permute-done((bf16[3,80,1280]{2,1,0:T(8,128)(2,1)}, bf16[3,80,1280]{2,1,0:T(8,128)(2,1)}, u32[]{:S(2)}, u32[]{:S(2)}) %collective-permute-start.3) | collective-permute-done | bytes 614432 | tf_op jit(solution)/shard_map/ppermute | solution.py:39
  44.3 2.9 %collective-permute-start.7 = (bf16[3,80,1280]{2,1,0:T(8,128)(2,1)}, bf16[3,80,1280]{2,1,0:T(8,128)(2,1)}, u32[]{:S(2)}, u32[]{:S(2)}) collective-permute-start(bf16[3,80,1280]{2,1,0:T(8,128)(2,1)} %collective-permute-done.3.t0_hbm), channel_id=1, source_target_pairs={{0,128},{128,0},{1,129},{129,1},{2,130},{130,2},{3,131},{131,3},{4... | collective-permute-start | bytes 1843208 | tf_op jit(solution)/shard_map/ppermute | solution.py:39
  47.2 1.7 fusion
  48.9 5.1 %collective-permute-start.11 = (bf16[2,56,640]{2,1,0:T(8,128)(2,1)S(1)}, bf16[2,56,640]{2,1,0:T(8,128)(2,1)S(1)}, u32[]{:S(2)}, u32[]{:S(2)}) collective-permute-start(bf16[2,56,640]{2,1,0:T(8,128)(2,1)S(1)} %get-tuple-element.82), channel_id=1, source_target_pairs={{0,0},{8,8},{16,16},{24,24},{32,32},{40,40},{48,48},{56,56},{64,80... | collective-permute-start | bytes 430088 | tf_op jit(solution)/shard_map/ppermute | solution.py:435
  54.0 4.4 %collective-permute-done.11 = bf16[2,56,640]{2,1,0:T(8,128)(2,1)S(1)} collective-permute-done((bf16[2,56,640]{2,1,0:T(8,128)(2,1)S(1)}, bf16[2,56,640]{2,1,0:T(8,128)(2,1)S(1)}, u32[]{:S(2)}, u32[]{:S(2)}) %collective-permute-start.11) | collective-permute-done | bytes 143392 | tf_op jit(solution)/shard_map/ppermute | solution.py:435
  58.4 4.1 %collective-permute-done.10.x3_hbm = bf16[64,5120]{1,0:T(8,128)(2,1)S(1)} collective-permute-done((bf16[64,5120]{1,0:T(8,128)(2,1)S(1)}, bf16[64,5120]{1,0:T(8,128)(2,1)S(1)}, u32[]{:S(2)}, u32[]{:S(2)}) %collective-permute-start.10) | collective-permute-done | bytes 655392 | tf_op jit(solution)/shard_map/ppermute | solution.py:398
  65.1 3.1 %collective-permute-start.14 = (bf16[2,56,640]{2,1,0:T(8,128)(2,1)}, bf16[2,56,640]{2,1,0:T(8,128)(2,1)S(1)}, u32[]{:S(2)}, u32[]{:S(2)}) collective-permute-start(bf16[2,56,640]{2,1,0:T(8,128)(2,1)} %get-tuple-element.81), channel_id=1, source_target_pairs={{128,8},{136,0},{144,24},{152,16},{160,40},{168,32},{176,56},{184,... | collective-permute-start | bytes 430088 | tf_op jit(solution)/shard_map/ppermute | solution.py:436
  69.1 9.0 %collective-permute-done.14 = bf16[2,56,640]{2,1,0:T(8,128)(2,1)S(1)} collective-permute-done((bf16[2,56,640]{2,1,0:T(8,128)(2,1)}, bf16[2,56,640]{2,1,0:T(8,128)(2,1)S(1)}, u32[]{:S(2)}, u32[]{:S(2)}) %collective-permute-start.14) | collective-permute-done | bytes 143392 | tf_op jit(solution)/shard_map/ppermute | solution.py:436
  78.8 1.9 %collective-permute-start.18 = (bf16[2,112,640]{2,1,0:T(8,128)(2,1)S(1)}, bf16[2,112,640]{2,1,0:T(8,128)(2,1)S(1)}, u32[]{:S(2)}, u32[]{:S(2)}) collective-permute-start(bf16[2,112,640]{2,1,0:T(8,128)(2,1)S(1)} %pad_maximum_fusion.1), channel_id=1, source_target_pairs={{0,4},{4,0},{1,5},{5,1},{2,6},{6,2},{3,7},{7,3},{8,12},{12,8},{9,1... | collective-permute-start | bytes 860168 | tf_op jit(solution)/shard_map/ppermute | solution.py:39
  80.7 8.4 %project.1 = (f32[32,8,128]{2,1,0:T(8,128)}, f32[160,384]{1,0:T(8,128)}, f32[160,384]{1,0:T(8,128)}, f32[160,384]{1,0:T(8,128)}, f32[160,384]{1,0:T(8,128)}) custom-call(s32[6]{0:T(128)} %copy-done.1, bf16[64,5120]{1,0:T(8,128)(2,1)} %copy-done.3, bf16[64,5120]{1,0:T(8,128)(2,1)} %copy-done.4, bf16[64,5120]{1,0:T(8,128)(2,1)} %copy-done.5, ...), custom_call_target="tpu_custom_call" | custom-call | tf_op jit(solution)/shard_map/project/pallas_call | solution.py:180
  89.2 2.3 %collective-permute-done.18 = bf16[2,112,640]{2,1,0:T(8,128)(2,1)S(1)} collective-permute-done((bf16[2,112,640]{2,1,0:T(8,128)(2,1)S(1)}, bf16[2,112,640]{2,1,0:T(8,128)(2,1)S(1)}, u32[]{:S(2)}, u32[]{:S(2)}) %collective-permute-start.18) | collective-permute-done | bytes 286752 | tf_op jit(solution)/shard_map/ppermute | solution.py:39
  91.5 1.6 collective-permute-start.19
  93.1 12.0 %all-to-all-start = ((f32[32,8,128]{2,1,0:T(8,128)}), f32[32,8,128]{2,1,0:T(8,128)S(1)}, u32[]{:S(2)}, u32[]{:S(2)}) async-start(f32[32,8,128]{2,1,0:T(8,128)} %get-tuple-element.62), calls=%async_computation | async-start | bytes 262144 | tf_op jit(solution)/shard_map/all_to_all | solution.py:458
  105.1 1.9 %collective-permute-start.15 = (f32[160,384]{1,0:T(8,128)}, f32[160,384]{1,0:T(8,128)S(1)}, u32[]{:S(2)}, u32[]{:S(2)}) collective-permute-start(f32[160,384]{1,0:T(8,128)} %get-tuple-element.56), channel_id=1, source_target_pairs={{0,1},{1,0},{2,3},{3,2},{4,5},{5,4},{6,7},{7,6},{8,9},{9,8},{10,11... | collective-permute-start | bytes 737288 | tf_op jit(solution)/shard_map/ppermute | solution.py:398
  107.0 2.7 %collective-permute-start.16 = (f32[160,384]{1,0:T(8,128)}, f32[160,384]{1,0:T(8,128)S(1)}, u32[]{:S(2)}, u32[]{:S(2)}) collective-permute-start(f32[160,384]{1,0:T(8,128)} %get-tuple-element.57), channel_id=1, source_target_pairs={{0,2},{1,3},{2,0},{3,1},{4,6},{5,7},{6,4},{7,5},{8,10},{9,11},{10,... | collective-permute-start | bytes 737288 | tf_op jit(solution)/shard_map/ppermute | solution.py:398
  109.9 5.3 %collective-permute-done.15.m1_hbm = f32[160,384]{1,0:T(8,128)S(1)} collective-permute-done((f32[160,384]{1,0:T(8,128)}, f32[160,384]{1,0:T(8,128)S(1)}, u32[]{:S(2)}, u32[]{:S(2)}) %collective-permute-start.15) | collective-permute-done | bytes 245792 | tf_op jit(solution)/shard_map/ppermute | solution.py:398
  115.2 6.5 %collective-permute-done.16.m2_hbm = f32[160,384]{1,0:T(8,128)S(1)} collective-permute-done((f32[160,384]{1,0:T(8,128)}, f32[160,384]{1,0:T(8,128)S(1)}, u32[]{:S(2)}, u32[]{:S(2)}) %collective-permute-start.16) | collective-permute-done | bytes 245792 | tf_op jit(solution)/shard_map/ppermute | solution.py:398
  121.7 2.6 %collective-permute-done.17.m3_hbm = f32[160,384]{1,0:T(8,128)S(1)} collective-permute-done((f32[160,384]{1,0:T(8,128)}, f32[160,384]{1,0:T(8,128)S(1)}, u32[]{:S(2)}, u32[]{:S(2)}) %collective-permute-start.17) | collective-permute-done | bytes 245792 | tf_op jit(solution)/shard_map/ppermute | solution.py:398
  127.3 1.3 collective-permute-start.24
  128.9 4.6 %attend.1 = (bf16[640,256]{1,0:T(8,128)(2,1)S(1)}, f32[5,8,256]{2,1,0:T(8,128)S(1)}, f32[640,256]{1,0:T(8,128)S(1)}) custom-call(s32[6]{0:T(128)S(1)} %copy-done.2, f32[160,384]{1,0:T(8,128)S(1)} %copy-done, f32[160,384]{1,0:T(8,128)S(1)} %collective-permute-done.15.m1_hbm, f32[160,384]{1,0:T(8,128)S(1)} %collective-permute-done.16.m2_hbm, ...), custom_call_target="tpu_custom_call" | custom-call | flops 700000000 | bytes 5000000 | tf_op jit(solution)/shard_map/attend/pallas_call | solution.py:298
  134.4 2.9 %collective-permute-done.24 = bf16[640,128]{1,0:T(8,128)(2,1)} collective-permute-done((bf16[640,128]{1,0:T(8,128)(2,1)S(1)}, bf16[640,128]{1,0:T(8,128)(2,1)}, u32[]{:S(2)}, u32[]{:S(2)}) %collective-permute-start.24) | collective-permute-done | bytes 163872 | tf_op jit(solution)/shard_map/ppermute | solution.py:465
  138.4 1.3 collective-permute-start.25
  140.9 1.5 close.1
  142.5 26.7 %all_to_all.10.in_ref = bf16[32,8,768]{2,1,0:T(8,128)(2,1)S(1)} all-to-all(bf16[32,8,768]{2,1,0:T(8,128)(2,1)S(1)} %bitcast.16), channel_id=1, replica_groups=mesh['zl'=2,'core'=2,'y'=4,'zh1'=2,'zh0'=2,'x'=4] {'y','x','zh1'}, dimensions={0} | all-to-all | bytes 786432 | tf_op jit(solution)/shard_map/all_to_all | solution.py:473
  169.2 2.0 %finish.1 = bf16[8,5120]{1,0:T(8,128)(2,1)} custom-call(s32[2]{0:T(128)S(1)} %collective-permute-done.numbers_ref.step_ref, bf16[32,8,768]{2,1,0:T(8,128)(2,1)S(1)} %all_to_all.10.in_ref, bf16[8,5120]{1,0:T(8,128)(2,1)S(1)} %collective-permute-done.1.mine_ref.hidden_ref, f32[4,3,5120]{2,1,0:T(4,128)S(1)} %copy.13.mod_ref), custom_call_target="tpu_custom_call" | custom-call | tf_op jit(solution)/shard_map/finish/pallas_call | solution.py:378
  (75 shorter events, 15.2 us)
Async XLA Ops:
  0.0 10.7 %collective-permute-start.1 = (bf16[8,5120]{1,0:T(8,128)(2,1)}, bf16[8,5120]{1,0:T(8,128)(2,1)S(1)}, u32[]{:S(2)}, u32[]{:S(2)}) collective-permute-start(bf16[8,5120]{1,0:T(8,128)(2,1)} %bitcast.21), channel_id=1, source_target_pairs={{0,64},{64,128},{128,192},{192,0},{1,65},{65,129},{129,193},{193,1... | collective-permute-start | bytes 245768 | tf_op jit(solution)/shard_map/ppermute | solution.py:412
  0.0 10.7 %collective-permute-start.2 = (bf16[8,5120]{1,0:T(8,128)(2,1)}, bf16[8,5120]{1,0:T(8,128)(2,1)S(1)}, u32[]{:S(2)}, u32[]{:S(2)}) collective-permute-start(bf16[8,5120]{1,0:T(8,128)(2,1)} %bitcast.22), channel_id=1, source_target_pairs={{0,72},{8,64},{64,136},{72,128},{128,200},{136,192},{192,8},{200,0... | collective-permute-start | bytes 245768 | tf_op jit(solution)/shard_map/ppermute | solution.py:413
  8.4 3.0 %collective-permute-start = (s32[2]{0:T(128)S(1)}, s32[2]{0:T(128)S(1)}, u32[]{:S(2)}, u32[]{:S(2)}) collective-permute-start(s32[2]{0:T(128)S(1)} %pad_add_fusion), channel_id=1, source_target_pairs={{0,64},{64,128},{128,192},{192,0},{1,65},{65,129},{129,193},{193,1... | collective-permute-start | bytes 32 | tf_op jit(solution)/shard_map/ppermute | solution.py:416
  10.7 38.2 %copy-start.1 = (s32[6]{0:T(128)}, s32[6]{0:T(128)S(1)}, u32[]{:S(2)}) copy-start(s32[6]{0:T(128)S(1)} %stack.54.place_ref) | copy-start | bytes 76
  12.3 55.9 %copy-start.10 = (s32[7]{0:T(128)S(1)}, s32[7]{0:T(128)}, u32[]{:S(2)}) copy-start(s32[7]{0:T(128)} %param.18) | copy-start | bytes 88
  12.3 11.0 %collective-permute-start.6 = (bf16[16,5120]{1,0:T(8,128)(2,1)S(1)}, bf16[16,5120]{1,0:T(8,128)(2,1)S(1)}, u32[]{:S(2)}, u32[]{:S(2)}) collective-permute-start(bf16[16,5120]{1,0:T(8,128)(2,1)S(1)} %modulate.1), channel_id=1, source_target_pairs={{0,3},{1,2},{2,1},{3,0},{4,7},{5,6},{6,5},{7,4},{8,11},{9,10},{10,... | collective-permute-start | bytes 491528 | tf_op jit(solution)/shard_map/ppermute | solution.py:398
  15.3 8.6 %collective-permute-start.5 = (bf16[16,5120]{1,0:T(8,128)(2,1)S(1)}, bf16[16,5120]{1,0:T(8,128)(2,1)S(1)}, u32[]{:S(2)}, u32[]{:S(2)}) collective-permute-start(bf16[16,5120]{1,0:T(8,128)(2,1)S(1)} %modulate.1), channel_id=1, source_target_pairs={{0,2},{1,3},{2,0},{3,1},{4,6},{5,7},{6,4},{7,5},{8,10},{9,11},{10,... | collective-permute-start | bytes 491528 | tf_op jit(solution)/shard_map/ppermute | solution.py:398
  16.1 8.1 %collective-permute-start.4 = (bf16[16,5120]{1,0:T(8,128)(2,1)S(1)}, bf16[16,5120]{1,0:T(8,128)(2,1)S(1)}, u32[]{:S(2)}, u32[]{:S(2)}) collective-permute-start(bf16[16,5120]{1,0:T(8,128)(2,1)S(1)} %modulate.1), channel_id=1, source_target_pairs={{0,1},{1,0},{2,3},{3,2},{4,5},{5,4},{6,7},{7,6},{8,9},{9,8},{10,11... | collective-permute-start | bytes 491528 | tf_op jit(solution)/shard_map/ppermute | solution.py:398
  16.5 27.7 %collective-permute-start.3 = (bf16[3,80,1280]{2,1,0:T(8,128)(2,1)}, bf16[3,80,1280]{2,1,0:T(8,128)(2,1)}, u32[]{:S(2)}, u32[]{:S(2)}) collective-permute-start(bf16[3,80,1280]{2,1,0:T(8,128)(2,1)} %constant_dynamic-slice_fusion), channel_id=1, source_target_pairs={{0,4},{4,0},{1,5},{5,1},{2,6},{6,2},{3,7},{7,3},{8,12},{12,8},{9,1... | collective-permute-start | bytes 1843208 | tf_op jit(solution)/shard_map/ppermute | solution.py:39
  24.3 56.4 %copy-start.3 = (bf16[64,5120]{1,0:T(8,128)(2,1)}, bf16[64,5120]{1,0:T(8,128)(2,1)S(1)}, u32[]{:S(2)}) copy-start(bf16[64,5120]{1,0:T(8,128)(2,1)S(1)} %pad_maximum_fusion.x0_hbm) | copy-start | bytes 1966084
  24.3 34.1 %collective-permute-start.8 = (bf16[64,5120]{1,0:T(8,128)(2,1)S(1)}, bf16[64,5120]{1,0:T(8,128)(2,1)S(1)}, u32[]{:S(2)}, u32[]{:S(2)}) collective-permute-start(bf16[64,5120]{1,0:T(8,128)(2,1)S(1)} %pad_maximum_fusion.x0_hbm), channel_id=1, source_target_pairs={{0,16},{16,0},{32,48},{48,32},{1,17},{17,1},{33,49},{49,33},{2,18}... | collective-permute-start | bytes 1966088 | tf_op jit(solution)/shard_map/ppermute | solution.py:398
  25.9 32.4 %collective-permute-start.9 = (bf16[64,5120]{1,0:T(8,128)(2,1)S(1)}, bf16[64,5120]{1,0:T(8,128)(2,1)S(1)}, u32[]{:S(2)}, u32[]{:S(2)}) collective-permute-start(bf16[64,5120]{1,0:T(8,128)(2,1)S(1)} %pad_maximum_fusion.x0_hbm), channel_id=1, source_target_pairs={{0,32},{16,48},{32,0},{48,16},{1,33},{17,49},{33,1},{49,17},{2,34}... | collective-permute-start | bytes 1966088 | tf_op jit(solution)/shard_map/ppermute | solution.py:398
  28.8 33.6 %collective-permute-start.10 = (bf16[64,5120]{1,0:T(8,128)(2,1)S(1)}, bf16[64,5120]{1,0:T(8,128)(2,1)S(1)}, u32[]{:S(2)}, u32[]{:S(2)}) collective-permute-start(bf16[64,5120]{1,0:T(8,128)(2,1)S(1)} %pad_maximum_fusion.x0_hbm), channel_id=1, source_target_pairs={{0,48},{16,32},{32,16},{48,0},{1,49},{17,33},{33,17},{49,1},{2,50}... | collective-permute-start | bytes 1966088 | tf_op jit(solution)/shard_map/ppermute | solution.py:398
  44.3 18.2 %collective-permute-start.7 = (bf16[3,80,1280]{2,1,0:T(8,128)(2,1)}, bf16[3,80,1280]{2,1,0:T(8,128)(2,1)}, u32[]{:S(2)}, u32[]{:S(2)}) collective-permute-start(bf16[3,80,1280]{2,1,0:T(8,128)(2,1)} %collective-permute-done.3.t0_hbm), channel_id=1, source_target_pairs={{0,128},{128,0},{1,129},{129,1},{2,130},{130,2},{3,131},{131,3},{4... | collective-permute-start | bytes 1843208 | tf_op jit(solution)/shard_map/ppermute | solution.py:39
  48.9 9.5 %collective-permute-start.11 = (bf16[2,56,640]{2,1,0:T(8,128)(2,1)S(1)}, bf16[2,56,640]{2,1,0:T(8,128)(2,1)S(1)}, u32[]{:S(2)}, u32[]{:S(2)}) collective-permute-start(bf16[2,56,640]{2,1,0:T(8,128)(2,1)S(1)} %get-tuple-element.82), channel_id=1, source_target_pairs={{0,0},{8,8},{16,16},{24,24},{32,32},{40,40},{48,48},{56,56},{64,80... | collective-permute-start | bytes 430088 | tf_op jit(solution)/shard_map/ppermute | solution.py:435
  62.5 15.7 %collective-permute-start.13 = (bf16[3,80,1280]{2,1,0:T(8,128)(2,1)}, bf16[3,80,1280]{2,1,0:T(8,128)(2,1)}, u32[]{:S(2)}, u32[]{:S(2)}) collective-permute-start(bf16[3,80,1280]{2,1,0:T(8,128)(2,1)} %collective-permute-done.7.t1_hbm), channel_id=1, source_target_pairs={{0,64},{64,0},{1,65},{65,1},{2,66},{66,2},{3,67},{67,3},{4,68},{68... | collective-permute-start | bytes 1843208 | tf_op jit(solution)/shard_map/ppermute | solution.py:39
  62.5 18.2 %collective-permute-start.12 = (bf16[3,80,1280]{2,1,0:T(8,128)(2,1)}, bf16[3,80,1280]{2,1,0:T(8,128)(2,1)}, u32[]{:S(2)}, u32[]{:S(2)}) collective-permute-start(bf16[3,80,1280]{2,1,0:T(8,128)(2,1)} %collective-permute-done.3.t0_hbm), channel_id=1, source_target_pairs={{0,64},{64,0},{1,65},{65,1},{2,66},{66,2},{3,67},{67,3},{4,68},{68... | collective-permute-start | bytes 1843208 | tf_op jit(solution)/shard_map/ppermute | solution.py:39
  65.1 13.0 %collective-permute-start.14 = (bf16[2,56,640]{2,1,0:T(8,128)(2,1)}, bf16[2,56,640]{2,1,0:T(8,128)(2,1)S(1)}, u32[]{:S(2)}, u32[]{:S(2)}) collective-permute-start(bf16[2,56,640]{2,1,0:T(8,128)(2,1)} %get-tuple-element.81), channel_id=1, source_target_pairs={{128,8},{136,0},{144,24},{152,16},{160,40},{168,32},{176,56},{184,... | collective-permute-start | bytes 430088 | tf_op jit(solution)/shard_map/ppermute | solution.py:436
  78.8 12.7 %collective-permute-start.18 = (bf16[2,112,640]{2,1,0:T(8,128)(2,1)S(1)}, bf16[2,112,640]{2,1,0:T(8,128)(2,1)S(1)}, u32[]{:S(2)}, u32[]{:S(2)}) collective-permute-start(bf16[2,112,640]{2,1,0:T(8,128)(2,1)S(1)} %pad_maximum_fusion.1), channel_id=1, source_target_pairs={{0,4},{4,0},{1,5},{5,1},{2,6},{6,2},{3,7},{7,3},{8,12},{12,8},{9,1... | collective-permute-start | bytes 860168 | tf_op jit(solution)/shard_map/ppermute | solution.py:39
  89.2 35.5 %copy-start = (f32[160,384]{1,0:T(8,128)S(1)}, f32[160,384]{1,0:T(8,128)}, u32[]{:S(2)}) copy-start(f32[160,384]{1,0:T(8,128)} %get-tuple-element.64.m0_hbm) | copy-start | bytes 737284
  89.2 35.5 %copy-start.2 = (s32[6]{0:T(128)S(1)}, s32[6]{0:T(128)}, u32[]{:S(2)}) copy-start(s32[6]{0:T(128)} %copy-done.1) | copy-start | bytes 76
  91.5 32.8 %collective-permute-start.19 = (bf16[2,224,640]{2,1,0:T(8,128)(2,1)S(1)}, bf16[2,224,640]{2,1,0:T(8,128)(2,1)S(1)}, u32[]{:S(2)}, u32[]{:S(2)}) collective-permute-start(bf16[2,224,640]{2,1,0:T(8,128)(2,1)S(1)} %constant_dynamic-update-slice_fusion.c0), channel_id=1, source_target_pairs={{0,128},{128,0},{1,129},{129,1},{2,130},{130,2},{3,131},{131,3},{4... | collective-permute-start | bytes 1720328 | tf_op jit(solution)/shard_map/ppermute | solution.py:39
  93.1 31.2 %collective-permute-start.20 = (bf16[2,224,640]{2,1,0:T(8,128)(2,1)S(1)}, bf16[2,224,640]{2,1,0:T(8,128)(2,1)}, u32[]{:S(2)}, u32[]{:S(2)}) collective-permute-start(bf16[2,224,640]{2,1,0:T(8,128)(2,1)S(1)} %constant_dynamic-update-slice_fusion.c0), channel_id=1, source_target_pairs={{0,64},{64,0},{1,65},{65,1},{2,66},{66,2},{3,67},{67,3},{4,68},{68... | collective-permute-start | bytes 1720328 | tf_op jit(solution)/shard_map/ppermute | solution.py:39
  93.1 31.2 %all-to-all-start = ((f32[32,8,128]{2,1,0:T(8,128)}), f32[32,8,128]{2,1,0:T(8,128)S(1)}, u32[]{:S(2)}, u32[]{:S(2)}) async-start(f32[32,8,128]{2,1,0:T(8,128)} %get-tuple-element.62), calls=%async_computation | async-start | bytes 262144 | tf_op jit(solution)/shard_map/all_to_all | solution.py:458
  105.1 10.1 %collective-permute-start.15 = (f32[160,384]{1,0:T(8,128)}, f32[160,384]{1,0:T(8,128)S(1)}, u32[]{:S(2)}, u32[]{:S(2)}) collective-permute-start(f32[160,384]{1,0:T(8,128)} %get-tuple-element.56), channel_id=1, source_target_pairs={{0,1},{1,0},{2,3},{3,2},{4,5},{5,4},{6,7},{7,6},{8,9},{9,8},{10,11... | collective-permute-start | bytes 737288 | tf_op jit(solution)/shard_map/ppermute | solution.py:398
  107.0 14.7 %collective-permute-start.16 = (f32[160,384]{1,0:T(8,128)}, f32[160,384]{1,0:T(8,128)S(1)}, u32[]{:S(2)}, u32[]{:S(2)}) collective-permute-start(f32[160,384]{1,0:T(8,128)} %get-tuple-element.57), channel_id=1, source_target_pairs={{0,2},{1,3},{2,0},{3,1},{4,6},{5,7},{6,4},{7,5},{8,10},{9,11},{10,... | collective-permute-start | bytes 737288 | tf_op jit(solution)/shard_map/ppermute | solution.py:398
  109.7 14.6 %collective-permute-start.17 = (f32[160,384]{1,0:T(8,128)}, f32[160,384]{1,0:T(8,128)S(1)}, u32[]{:S(2)}, u32[]{:S(2)}) collective-permute-start(f32[160,384]{1,0:T(8,128)} %get-tuple-element.58), channel_id=1, source_target_pairs={{0,3},{1,2},{2,1},{3,0},{4,7},{5,6},{6,5},{7,4},{8,11},{9,10},{10,... | collective-permute-start | bytes 737288 | tf_op jit(solution)/shard_map/ppermute | solution.py:398
  124.3 4.5 %collective-permute-start.21 = (bf16[2,224,640]{2,1,0:T(8,128)(2,1)S(1)}, bf16[2,224,640]{2,1,0:T(8,128)(2,1)}, u32[]{:S(2)}, u32[]{:S(2)}) collective-permute-start(bf16[2,224,640]{2,1,0:T(8,128)(2,1)S(1)} %collective-permute-done.19.c1), channel_id=1, source_target_pairs={{0,64},{64,0},{1,65},{65,1},{2,66},{66,2},{3,67},{67,3},{4,68},{68... | collective-permute-start | bytes 1720328 | tf_op jit(solution)/shard_map/ppermute | solution.py:39
  125.7 8.0 %collective-permute-start.22 = (bf16[640,128]{1,0:T(8,128)(2,1)S(1)}, bf16[640,128]{1,0:T(8,128)(2,1)S(1)}, u32[]{:S(2)}, u32[]{:S(2)}) collective-permute-start(bf16[640,128]{1,0:T(8,128)(2,1)S(1)} %own_rows.1.own), channel_id=1, source_target_pairs={{0,4},{4,0},{1,5},{5,1},{2,6},{6,2},{3,7},{7,3},{8,12},{12,8},{9,1... | collective-permute-start | bytes 491528 | tf_op jit(solution)/shard_map/ppermute | solution.py:39
  126.0 8.4 %collective-permute-start.23 = (bf16[640,128]{1,0:T(8,128)(2,1)S(1)}, bf16[640,128]{1,0:T(8,128)(2,1)}, u32[]{:S(2)}, u32[]{:S(2)}) collective-permute-start(bf16[640,128]{1,0:T(8,128)(2,1)S(1)} %own_rows.1.own), channel_id=1, source_target_pairs={{0,128},{1,129},{2,130},{3,131},{4,132},{5,133},{6,134},{7,135},{8... | collective-permute-start | bytes 491528 | tf_op jit(solution)/shard_map/ppermute | solution.py:464
  127.3 10.1 %collective-permute-start.24 = (bf16[640,128]{1,0:T(8,128)(2,1)S(1)}, bf16[640,128]{1,0:T(8,128)(2,1)}, u32[]{:S(2)}, u32[]{:S(2)}) collective-permute-start(bf16[640,128]{1,0:T(8,128)(2,1)S(1)} %own_rows.1.own), channel_id=1, source_target_pairs={{0,132},{4,128},{1,133},{5,129},{2,134},{6,130},{3,135},{7,131},{8... | collective-permute-start | bytes 491528 | tf_op jit(solution)/shard_map/ppermute | solution.py:465
  138.4 2.5 %collective-permute-start.25 = (bf16[2,640,128]{2,1,0:T(8,128)(2,1)S(1)}, bf16[2,640,128]{2,1,0:T(8,128)(2,1)S(1)}, u32[]{:S(2)}, u32[]{:S(2)}) collective-permute-start(bf16[2,640,128]{2,1,0:T(8,128)(2,1)S(1)} %maximum_select_fusion.spread), channel_id=1, source_target_pairs={{0,64},{128,192},{1,65},{129,193},{2,66},{130,194},{3,67},{131,195... | collective-permute-start | bytes 983048 | tf_op jit(solution)/shard_map/ppermute | solution.py:470
  (6 other events, 79.9 us)
